TPU v7x, 32 devices: a whole 2x2x4 slice. The times are simulated.
32 devices in a mesh: section: 2 (over x), dp: 4 (over z), tensor: 4 (over y, core).
Axes of the slice: x: 2, y: 2, z: 4, core: 2. Of those that a mesh axis runs over, the one named last changes fastest.
Arguments:
- tokens: bfloat16 [2, 4, 1024, 1024], P(None, 'dp', 'tensor'), may hold values from -6 to 6
- cotangent: bfloat16 [2, 4, 1024, 1024], P(None, 'dp', 'tensor'), may hold values from -6 to 6
- ln1_gain: bfloat16 [2, 1024], P('section', 'dp'), may hold values from 0.5 to 1.5
- ln1_bias: bfloat16 [2, 1024], P('section', 'dp'), may hold values from -3 to 3
- w_qkv: bfloat16 [2, 1024, 3072], P('section', 'dp', 'tensor'), may hold values from -0.1875 to 0.1875
- qv_bias: bfloat16 [2, 16, 128], P('section', 'tensor', 'dp'), may hold values from -3 to 3
- w_out: bfloat16 [2, 1024, 1024], P('section', 'tensor', 'dp'), may hold values from -3 to 3
- out_bias: bfloat16 [2, 1024], P('section', 'dp'), may hold values from -3 to 3
- scale_attn: bfloat16 [2, 1024], P('section', 'dp'), may hold values from 0.5 to 1.5
- ln2_gain: bfloat16 [2, 1024], P('section', 'dp'), may hold values from 0.5 to 1.5
- ln2_bias: bfloat16 [2, 1024], P('section', 'dp'), may hold values from -3 to 3
- w_fc1: bfloat16 [2, 1024, 4096], P('section', 'dp', 'tensor'), may hold values from -0.1875 to 0.1875
- fc1_bias: bfloat16 [2, 4, 1024], P('section', 'tensor', 'dp'), may hold values from -3 to 3
- w_fc2: bfloat16 [2, 4096, 1024], P('section', 'tensor', 'dp'), may hold values from -0.09375 to 0.09375
- fc2_bias: bfloat16 [2, 1024], P('section', 'dp'), may hold values from -3 to 3
- scale_mlp: bfloat16 [2, 1024], P('section', 'dp'), may hold values from 0.5 to 1.5
Outputs:
- block_out: bfloat16 [2, 2, 4, 1024, 1024], P('section', None, 'dp', 'tensor')
- input_grads: bfloat16 [2, 2, 4, 1024, 1024], P('section', None, 'dp', 'tensor')
- grad_ln1_gain: float32 [2, 1024], P('section', 'dp')
- grad_ln1_bias: float32 [2, 1024], P('section', 'dp')
- grad_w_qkv: float32 [2, 1024, 3072], P('section', 'dp', 'tensor')
- grad_qv_bias: float32 [2, 16, 128], P('section', 'tensor', 'dp')
- grad_w_out: float32 [2, 1024, 1024], P('section', 'tensor', 'dp')
- grad_out_bias: float32 [2, 1024], P('section', 'dp')
- grad_scale_attn: float32 [2, 1024], P('section', 'dp')
- grad_ln2_gain: float32 [2, 1024], P('section', 'dp')
- grad_ln2_bias: float32 [2, 1024], P('section', 'dp')
- grad_w_fc1: float32 [2, 1024, 4096], P('section', 'dp', 'tensor')
- grad_fc1_bias: float32 [2, 4, 1024], P('section', 'tensor', 'dp')
- grad_w_fc2: float32 [2, 4096, 1024], P('section', 'tensor', 'dp')
- grad_fc2_bias: float32 [2, 1024], P('section', 'dp')
- grad_scale_mlp: float32 [2, 1024], P('section', 'dp')
All inputs are finite; a program needn't handle non-finite values.
Results may differ from a plain program's by a relative error of at most 0.014.
Values may be sent and summed in bfloat16 or wider, within the bound.
No kernel may reach another device: no remote copies, remote signals or barrier semaphores. Data moves between devices by JAX's collectives and lax.ppermute only.
A program may use at most 192 MiB of HBM per device.

v0:
```python
from functools import partial

import jax
import jax.numpy as jnp
from jax import lax
from jax.experimental import pallas as pl
from jax.experimental.pallas import tpu as pltpu
from jax.sharding import PartitionSpec as P

EPSILON = 1e-06
BF = jnp.bfloat16
F32 = jnp.float32
MIB = 1 << 20

LN1_G, LN1_B, OUT_B, SC_ATTN, LN2_G, LN2_B, FC2_B, SC_MLP = range(8)


def dot(a, b):
    return lax.dot_general(a, b, (((1,), (0,)), ((), ())), preferred_element_type=F32)


def dot_bt(a, b):
    return lax.dot_general(a, b, (((1,), (1,)), ((), ())), preferred_element_type=F32)


def dot_at(a, b):
    return lax.dot_general(a, b, (((0,), (0,)), ((), ())), preferred_element_type=F32)


def turn(v):
    return v.astype(F32).T


def params(limit, grid=0):
    return pltpu.CompilerParams(
        vmem_limit_bytes=limit * MIB,
        dimension_semantics=("arbitrary",) * grid if grid else None,
    )


def late(v):
    return pltpu.with_memory_space_constraint(v, pltpu.HBM)


def whole(shape):
    return pl.BlockSpec(shape, lambda i: (0, 0), pipeline_mode=pl.Buffered(1))


def cost(micros):
    return pl.CostEstimate(flops=int(micros * 1.15e9), bytes_accessed=0, transcendentals=0)


def sds(shape, dtype):
    return jax.ShapeDtypeStruct(shape, dtype)


def core_swap(v):
    count = lax.axis_size("tensor")
    return lax.ppermute(v, "tensor", [(i, i ^ 1) for i in range(count)])


def from_chip(v, step):
    count = lax.axis_size("tensor")
    chips = count // 2
    pairs = [(((i // 2 + step) % chips) * 2 + i % 2, i) for i in range(count)]
    return lax.ppermute(v, "tensor", pairs)


def tie(v, *after):
    if not after:
        return v
    return lax.optimization_barrier((v, *after))[0]


def tie_all(vs, *after):
    return lax.optimization_barrier((*vs, *after))[: len(vs)]


def gather_tokens(own, work, beside=()):
    chips = lax.axis_size("tensor") // 2
    came = [from_chip(own, step) for step in range(1, chips)]
    chunks = [(own, core_swap(own))]
    results = [work(chunks[0])]
    for same in came:
        same = tie(same, results[-1], *beside)
        chunks.append((same, core_swap(same)))
        results.append(work(chunks[-1]))
    return chunks, results


def core_sums(sames, others):
    chips, rows = len(sames), sames[0].shape[0]
    if isinstance(others, (list, tuple)):
        came = [core_swap(v) for v in others[1:]]
        local = core_swap(tie(others[0], came[-1]))
    else:
        local = core_swap(others)
        came = [local[c * rows : (c + 1) * rows] for c in range(1, chips)]
    sums = [(a.astype(F32) + b.astype(F32)).astype(BF) for a, b in zip(sames[1:], came)]
    return sums, local


def send_sums(sums):
    chips = len(sums) + 1
    return [from_chip(both, chips - step) for step, both in enumerate(sums, 1)]


def scatter_tokens(sames, others, work=None, beside=None):
    sums, local = core_sums(sames, others)
    terms = send_sums(sums)
    made = work(sums[-1]) if work else local
    more = beside(sums[-1]) if beside else ()
    terms = [tie(t, made, local, *more) for t in terms]
    return [sames[0], *terms, local], made


def swap_section(v):
    return lax.ppermute(v, "section", [(0, 1), (1, 0)])


def assemble(shards, rows):
    count = len(shards)
    cut = len(shards[0])
    size, cols = rows // (count * cut), shards[0][0].shape[1]
    place = jnp.stack([lax.axis_index("dp"), lax.axis_index("section")])

    def body(place_ref, *refs):
        out_ref, sems = refs[count * cut :]
        z, x = place_ref[0], place_ref[1]
        started = []
        for k in range(count):
            base = lax.rem(z + (count - k), count) * (cut * size)
            for i, at in enumerate([base] if cut == 1 else [base + x * size, base + (1 - x) * size]):
                copy = pltpu.make_async_copy(
                    refs[k * cut + i].at[pl.ds(0, size), :],
                    out_ref.at[pl.ds(pl.multiple_of(at, size), size), :],
                    sems.at[k * cut + i],
                )
                copy.start()
                started.append(copy)
        for copy in started:
            copy.wait()

    hbm = pl.BlockSpec(memory_space=pl.ANY)
    return pl.pallas_call(
        body,
        in_specs=[pl.BlockSpec(memory_space=pltpu.SMEM)] + [hbm] * (count * cut),
        out_specs=pl.BlockSpec(memory_space=pltpu.VMEM),
        out_shape=sds((rows, cols), shards[0][0].dtype),
        scratch_shapes=[pltpu.SemaphoreType.DMA((count * cut,))],
        compiler_params=params(6),
        cost_estimate=cost(2),
        name="assemble",
    )(place, *[late(v) for shard in shards for v in shard])


def half_of(v, which):
    half = v.shape[0] // 2
    return lax.dynamic_slice_in_dim(v, which * half, half, 0)


def direct(own):
    count = lax.axis_size("dp")
    return [
        lax.ppermute(own, "dp", [(i, (i + step) % count) for i in range(count)])
        for step in range(1, count)
    ]


def third(values, index):
    cuts = [-(-len(values) * i // 3) for i in range(4)]
    return values[cuts[index] : cuts[index + 1]]


class Ring:
    def __init__(self, own):
        self.last, self.hops, self.backs, self.at, self.back_at = own, [], [], 0, 0

    def hop(self, *gate):
        count = lax.axis_size("dp")
        pairs = [(i, (i + 1) % count) for i in range(count)]
        new = []
        for i in range(len(third(range(count - 1), self.at))):
            self.last = lax.ppermute(tie(self.last, *gate) if i == 0 else self.last, "dp", pairs)
            new.append(self.last)
        self.hops += new
        self.at += 1
        return new

    def back(self, *gate):
        count = lax.axis_size("dp")
        which = third(range(count - 1), self.back_at)
        new = [swap_section(tie(self.hops[i], *gate)) for i in which]
        self.backs += new
        self.back_at += 1
        return new


def in_order(back):
    count = len(back)
    ahead = [back[0], *back[:0:-1]]
    twice = jnp.stack(ahead + ahead)
    return lax.dynamic_slice_in_dim(twice, count - lax.axis_index("dp"), count, 0)


def dp_rows(v, back):
    dp = lax.axis_size("dp")
    part = v.shape[0] // dp
    place = lax.rem(lax.axis_index("dp") + (dp - back), dp)
    return lax.dynamic_slice_in_dim(v, place * part, part, 0)


class RingSum:
    def __init__(self, pair, mine, other=None):
        self.mine, self.other, self.pair = mine, other, pair
        self.terms, self.at, self.done = [], 0, 0

    def total(self, gate=()):
        first = tie(self.terms[0], *gate)
        return sum(t.astype(F32) for t in [first, *self.terms[1:]])

    def one(self, gate):
        dp = lax.axis_size("dp")
        self.done += 1
        new = []
        if self.terms:
            pairs = [(i, (i + 1) % dp) for i in range(dp)]
            self.sent = self.total(gate).astype(BF)
            new.append(lax.ppermute(self.sent, "dp", pairs))
        if self.other is not None:
            new.append(swap_section(tie(dp_rows(self.other, self.done), *gate)))
        self.terms = [*new, dp_rows(self.mine, self.done)]
        return new

    def step(self, *gate):
        self.at += 1
        if self.at == 5:
            self.own = self.total(gate)
            self.came = lax.ppermute(self.own.astype(BF), "section", [self.pair])
            return [self.came]
        count = 1 if self.at == 1 else len(third(range(lax.axis_size("dp") - 1), self.at - 2))
        return [v for i in range(count) for v in self.one(gate if i == 0 else ())]


def standardize(v):
    centred = v - jnp.mean(v, axis=-1, keepdims=True)
    var = jnp.mean(centred * centred, axis=-1, keepdims=True)
    scale = lax.rsqrt(var + EPSILON)
    return centred * scale, scale


def norm_of(v, vec, gain, shift):
    return (standardize(v)[0] * vec[gain : gain + 1, :] + vec[shift : shift + 1, :]).astype(BF)


def norm_back(v, grad, gain):
    xh, scale = standardize(v)
    dxh = grad * gain
    inner = jnp.mean(dxh * xh, axis=-1, keepdims=True)
    out = scale * (dxh - jnp.mean(dxh, axis=-1, keepdims=True) - xh * inner)
    return out, grad * xh


def total(refs):
    out = refs[0][...].astype(F32)
    for ref in refs[1:]:
        out = out + ref[...].astype(F32)
    return out


def fold(v, op):
    return op(v.reshape(-1, 8, v.shape[1]), axis=0)


def add_rows(ref, rows):
    for k, row in enumerate(rows):
        ref[8 * k : 8 * k + 8, :] += fold(row, jnp.sum)


def rowwise(body, row_ins, fulls, row_outs, sums, name):
    rows, width = row_ins[0].shape
    step = min(128, rows)
    some, outs = len(row_ins) + len(fulls), len(row_outs)

    def kernel(*refs):
        if not sums:
            body(*refs)
            return
        sum_ref, acc_ref = refs[some + outs :]

        @pl.when(pl.program_id(0) == 0)
        def _():
            acc_ref[...] = jnp.zeros_like(acc_ref)

        body(*refs[: some + outs], acc_ref)

        @pl.when(pl.program_id(0) == pl.num_programs(0) - 1)
        def _():
            for k in range(sums):
                sum_ref[k : k + 1, :] = jnp.sum(
                    acc_ref[8 * k : 8 * k + 8, :], axis=0, keepdims=True
                )

    out_shape = [sds((rows, width), d) for d in row_outs]
    out_shape += [sds((sums, width), F32)] if sums else []
    block = pl.BlockSpec((step, width), lambda i: (i, 0))
    return pl.pallas_call(
        kernel,
        grid=(rows // step,),
        in_specs=[block] * len(row_ins) + [whole(a.shape) for a in fulls],
        out_specs=[block] * outs + ([whole((sums, width))] if sums else []),
        out_shape=out_shape,
        scratch_shapes=[pltpu.VMEM((8 * sums, width), F32)] if sums else [],
        compiler_params=params(8, 1),
        cost_estimate=cost(2),
        name=name,
    )(*row_ins, *fulls)


def norm_first(x, vec):
    def body(x_ref, vec_ref, out_ref):
        out_ref[...] = norm_of(x_ref[...].astype(F32), vec_ref[...], LN1_G, LN1_B)

    return rowwise(body, [x], [vec], [BF], 0, "norm_first")[0]


def after_attention(x, terms, vec):
    count = len(terms)

    def body(*refs):
        x_ref, term_refs, vec_ref = refs[0], refs[1 : 1 + count], refs[1 + count]
        att_ref, res_ref, norm_ref = refs[2 + count :]
        v = vec_ref[...]
        attended = total(term_refs) + v[OUT_B : OUT_B + 1, :]
        residual = x_ref[...].astype(F32) + v[SC_ATTN : SC_ATTN + 1, :] * attended
        att_ref[...] = attended.astype(BF)
        res_ref[...] = residual
        norm_ref[...] = norm_of(residual, v, LN2_G, LN2_B)

    return rowwise(body, [x, *terms], [vec], [BF, F32, BF], 0, "after_attention")


def after_mlp(residual, terms, vec, vec_next):
    count = len(terms)

    def body(*refs):
        res_ref, term_refs = refs[0], refs[1 : 1 + count]
        vec_ref, next_ref, mlp_ref, y_ref, norm_ref = refs[1 + count :]
        v = vec_ref[...]
        mlp = total(term_refs) + v[FC2_B : FC2_B + 1, :]
        y = (res_ref[...] + v[SC_MLP : SC_MLP + 1, :] * mlp).astype(BF)
        mlp_ref[...] = mlp.astype(BF)
        y_ref[...] = y
        norm_ref[...] = norm_of(y.astype(F32), next_ref[...], LN1_G, LN1_B)

    return rowwise(body, [residual, *terms], [vec, vec_next], [BF, BF, BF], 0, "after_mlp")


def last_output(residual, terms, grad, vec):
    count = len(terms)

    def body(*refs):
        res_ref, term_refs = refs[0], refs[1 : 1 + count]
        grad_ref, vec_ref, y_ref, sum_ref = refs[1 + count :]
        v = vec_ref[...]
        mlp = total(term_refs) + v[FC2_B : FC2_B + 1, :]
        y_ref[...] = (res_ref[...] + v[SC_MLP : SC_MLP + 1, :] * mlp).astype(BF)
        add_rows(sum_ref, [grad_ref[...].astype(F32) * mlp])

    return rowwise(body, [residual, *terms, grad], [vec], [BF], 1, "last_output")


def start_back(grad, vec):
    def body(grad_ref, vec_ref, out_ref, sum_ref):
        low = (vec_ref[...][SC_MLP : SC_MLP + 1, :] * grad_ref[...].astype(F32)).astype(BF)
        out_ref[...] = low
        add_rows(sum_ref, [low.astype(F32)])

    return rowwise(body, [grad], [vec], [BF], 1, "start_back")


def back_second(grad, residual, attended, terms, vec):
    count = len(terms)

    def body(*refs):
        grad_ref, res_ref, att_ref = refs[:3]
        term_refs = refs[3 : 3 + count]
        vec_ref, dres_ref, low_ref, sum_ref = refs[3 + count :]
        v = vec_ref[...]
        dn = total(term_refs)
        back, dgain = norm_back(res_ref[...], dn, v[LN2_G : LN2_G + 1, :])
        dres = grad_ref[...].astype(F32) + back
        low = (v[SC_ATTN : SC_ATTN + 1, :] * dres).astype(BF)
        dres_ref[...] = dres
        low_ref[...] = low
        add_rows(sum_ref, [dgain, dn, dres * att_ref[...].astype(F32), low.astype(F32)])

    return rowwise(
        body, [grad, residual, attended, *terms], [vec], [F32, BF], 4, "back_second"
    )


def back_first(dres, x, terms, vec, mlp_below=None, vec_below=None):
    count = len(terms)
    below = mlp_below is not None

    def body(*refs):
        dres_ref, x_ref = refs[:2]
        term_refs = refs[2 : 2 + count]
        rest = refs[2 + count :]
        if below:
            mlp_ref, vec_ref, under_ref, dx_ref, low_ref, sum_ref = rest
        else:
            vec_ref, dx_ref, sum_ref = rest
        v = vec_ref[...]
        dn = total(term_refs)
        back, dgain = norm_back(x_ref[...].astype(F32), dn, v[LN1_G : LN1_G + 1, :])
        dx = (dres_ref[...] + back).astype(BF)
        dx_ref[...] = dx
        rows = [dgain, dn]
        if below:
            wide = dx.astype(F32)
            low = (under_ref[...][SC_MLP : SC_MLP + 1, :] * wide).astype(BF)
            low_ref[...] = low
            rows += [wide * mlp_ref[...].astype(F32), low.astype(F32)]
        add_rows(sum_ref, rows)

    row_ins = [dres, x, *terms] + ([mlp_below] if below else [])
    fulls = [vec] + ([vec_below] if below else [])
    return rowwise(body, row_ins, fulls, [BF, BF] if below else [BF], 4 if below else 2, "back_first")


def project_qkv(pair, weight, bias):
    rows, width = pair[0].shape
    cols = bias.shape[1]

    def body(a_ref, b_ref, w_ref, bias_ref, out_ref):
        w = w_ref[...]
        shift = bias_ref[...]
        out_ref[:rows, :] = (dot(a_ref[...], w) + shift).astype(BF)
        out_ref[rows:, :] = (dot(b_ref[...], w) + shift).astype(BF)

    return pl.pallas_call(
        body,
        grid=(1,),
        in_specs=[
            whole((rows, width)), whole((rows, width)), whole((width, cols)), whole((1, cols))
        ],
        out_specs=whole((2 * rows, cols)),
        out_shape=sds((2 * rows, cols), BF),
        compiler_params=params(6, 1),
        cost_estimate=cost(0.5),
        name="project_qkv",
    )(*pair, weight, bias)


def head_rows(v, head, size):
    rows = lax.broadcasted_iota(jnp.int32, v.shape, 0)
    return jnp.where(rows // size == head, v, jnp.zeros_like(v))


def head_cols(v, head, size):
    cols = lax.broadcasted_iota(jnp.int32, v.shape, 1)
    return jnp.where(cols // size == head, v, jnp.zeros_like(v))


def attention(packed, weight, size):
    chips = len(packed)
    span = packed[0].shape[0]
    half = span // 2
    width = packed[0].shape[1] // 3
    seq = chips * span
    heads = width // size
    model = weight.shape[0]
    step = min(256, seq)
    chunk = min(128, seq)
    score = size**-0.5

    def body(*refs):
        in_refs, w_ref = refs[:chips], refs[chips]
        head_refs = refs[chips + 1 : 2 * chips + 1]
        lse_ref = refs[2 * chips + 1]
        same_refs, other_ref = refs[2 * chips + 2 : 3 * chips + 2], refs[3 * chips + 2]
        k_ref, qt_ref, vt_ref, ot_ref, s_ref, p_ref = refs[3 * chips + 3 :]
        for c in range(chips):
            at = slice(c * span, (c + 1) * span)
            k_ref[at, :] = in_refs[c][:, width : 2 * width]
            qt_ref[:, at] = (turn(in_refs[c][:, :width]) * score).astype(BF)
            vt_ref[:, at] = turn(in_refs[c][:, 2 * width :]).astype(BF)

        def one(i, carry):
            at = pl.ds(pl.multiple_of(i * step, step), step)
            q = qt_ref[:, at]
            s_ref[0] = dot(k_ref[...], head_rows(q, 0, size))
            for h in range(heads):
                if h + 1 < heads:
                    s_ref[(h + 1) % 2] = dot(k_ref[...], head_rows(q, h + 1, size))
                now = h % 2
                top = fold(s_ref[now, :chunk, :], jnp.max)
                for r in range(chunk, seq, chunk):
                    top = jnp.maximum(top, fold(s_ref[now, r : r + chunk, :], jnp.max))
                top = jnp.max(top, axis=0, keepdims=True)
                norm = jnp.zeros((8, step), F32)
                for r in range(0, seq, chunk):
                    p = jnp.exp(s_ref[now, r : r + chunk, :] - top)
                    norm = norm + fold(p, jnp.sum)
                    p_ref[now, r : r + chunk, :] = p.astype(BF)
                norm = jnp.sum(norm, axis=0, keepdims=True)
                rows = slice(h * size, (h + 1) * size)
                ot_ref[rows, at] = dot(vt_ref[rows, :], p_ref[now]) / norm
                lse_ref[h : h + 1, at] = top + jnp.log(norm)
            return carry

        lax.fori_loop(0, seq // step, one, 0)
        for c in range(chips):
            at = slice(c * span, (c + 1) * span)
            o = ot_ref[:, at].T.astype(BF)
            head_refs[c][...] = o
            same_refs[c][...] = dot_bt(o[:half], w_ref[...]).astype(BF)
            other_ref[c * half : (c + 1) * half, :] = dot_bt(o[half:], w_ref[...]).astype(BF)

    out = pl.pallas_call(
        body,
        grid=(1,),
        in_specs=[whole((span, 3 * width))] * chips
        + [pl.BlockSpec((model, width), lambda i: (0, 3), pipeline_mode=pl.Buffered(1))],
        out_specs=[whole((span, width))] * chips
        + [whole((heads, seq))]
        + [whole((half, model))] * chips
        + [whole((seq // 2, model))],
        out_shape=[pltpu.HBM((span, width), BF)] * chips
        + [sds((heads, seq), F32)]
        + [sds((half, model), BF)] * chips
        + [sds((seq // 2, model), BF)],
        scratch_shapes=[
            pltpu.VMEM((seq, width), BF),
            pltpu.VMEM((width, seq), BF),
            pltpu.VMEM((width, seq), BF),
            pltpu.VMEM((width, seq), F32),
            pltpu.VMEM((2, seq, step), F32),
            pltpu.VMEM((2, seq, step), BF),
        ],
        compiler_params=params(14, 1),
        cost_estimate=cost(9),
        name="attention",
    )(*packed, weight)
    return out[:chips], out[chips], out[chips + 1 : -1], out[-1]


def attention_back(packed, heads_kept, lse, datt, weight, size):
    chips = len(packed)
    span = packed[0].shape[0]
    half = span // 2
    width = packed[0].shape[1] // 3
    seq = chips * span
    heads = width // size
    model = weight.shape[0]
    step = min(256, seq)
    chunk = min(128, seq)
    score = size**-0.5

    def body(*refs):
        at = 0

        def take(count):
            nonlocal at
            at += count
            return refs[at - count : at]

        in_refs, kept_refs = take(chips), take(chips)
        (lse_ref,) = take(1)
        datt_refs = take(2 * chips)
        (w_ref,) = take(1)
        dqkv_refs = take(chips)
        same_refs = take(chips)
        other_ref, sum_ref = take(2)
        k_ref, v_ref, kt_ref, qt_ref, q_ref, do_ref, dot_ref = take(7)
        inner_ref, s_ref, g_ref, p_ref, ds_ref, dk_ref, dv_ref, dqt_ref = take(8)
        for c in range(chips):
            rows = slice(c * span, (c + 1) * span)
            q = in_refs[c][:, :width].astype(F32) * score
            k = in_refs[c][:, width : 2 * width]
            q_ref[rows, :] = q.astype(BF)
            qt_ref[:, rows] = q.T.astype(BF)
            k_ref[rows, :] = k
            kt_ref[:, rows] = turn(k).astype(BF)
            v_ref[rows, :] = in_refs[c][:, 2 * width :]
            for b in range(2):
                d = dot(datt_refs[2 * c + b][...], w_ref[:, 3 * width :]).astype(BF)
                here = slice(c * span + b * half, c * span + (b + 1) * half)
                do_ref[here, :] = d
                dt = turn(d)
                dot_ref[:, here] = dt.astype(BF)
                prod = dt * turn(kept_refs[c][b * half : (b + 1) * half, :])
                for h in range(heads):
                    inner_ref[h : h + 1, here] = jnp.sum(
                        prod[h * size : (h + 1) * size, :], axis=0, keepdims=True
                    )

        def one(i, carry):
            at = pl.ds(pl.multiple_of(i * step, step), step)
            qt = qt_ref[:, at]
            dot_t = dot_ref[:, at]
            q = q_ref[at, :]
            do = do_ref[at, :]

            def scores(h):
                s_ref[h % 2] = dot(k_ref[...], head_rows(qt, h, size))
                g_ref[h % 2] = dot(v_ref[...], head_rows(dot_t, h, size))

            scores(0)
            for h in range(heads):
                if h + 1 < heads:
                    scores(h + 1)
                now = h % 2
                cols = slice(h * step, (h + 1) * step)
                lse = lse_ref[h : h + 1, at]
                inner = inner_ref[h : h + 1, at]
                for r in range(0, seq, chunk):
                    p = jnp.exp(s_ref[now, r : r + chunk, :] - lse)
                    ds = p * (g_ref[now, r : r + chunk, :] - inner)
                    p_ref[r : r + chunk, cols] = p.astype(BF)
                    ds_ref[r : r + chunk, cols] = ds.astype(BF)
                rows = slice(h * size, (h + 1) * size)
                dqt_ref[rows, at] = dot(kt_ref[rows, :], ds_ref[:, cols]) * score
            dv = dot(p_ref[...], jnp.concatenate([head_cols(do, h, size) for h in range(heads)], 0))
            dk = dot(ds_ref[...], jnp.concatenate([head_cols(q, h, size) for h in range(heads)], 0))

            @pl.when(i == 0)
            def _():
                dv_ref[...] = dv
                dk_ref[...] = dk

            @pl.when(i > 0)
            def _():
                dv_ref[...] += dv
                dk_ref[...] += dk

            return carry

        lax.fori_loop(0, seq // step, one, 0)
        for c in range(chips):
            rows = slice(c * span, (c + 1) * span)
            out = dqkv_refs[c]
            out[:, :width] = dqt_ref[:, rows].T.astype(BF)
            out[:, width : 2 * width] = dk_ref[rows, :].astype(BF)
            out[:, 2 * width :] = dv_ref[rows, :].astype(BF)
            sums = jnp.sum(out[...].astype(F32), axis=0, keepdims=True)
            if c == 0:
                sum_ref[...] = sums
            else:
                sum_ref[...] += sums
            w = w_ref[:, : 3 * width]
            same_refs[c][...] = dot_bt(out[:half, :], w).astype(BF)
            other_ref[c * half : (c + 1) * half, :] = dot_bt(out[half:, :], w).astype(BF)

    flat = [g for pair in datt for g in pair]
    out_shape = (
        [pltpu.HBM((span, 3 * width), BF)] * chips
        + [pltpu.HBM((half, model), BF)] * chips
        + [sds((seq // 2, model), BF), sds((1, 3 * width), F32)]
    )
    operands = (*map(late, (*packed, *heads_kept)), lse, *flat, late(weight))
    out = pl.pallas_call(
        body,
        grid=(1,),
        in_specs=[whole(a.shape) for a in operands],
        out_specs=[whole(a.shape) for a in out_shape],
        out_shape=out_shape,
        scratch_shapes=[
            pltpu.VMEM((seq, width), BF),
            pltpu.VMEM((seq, width), BF),
            pltpu.VMEM((width, seq), BF),
            pltpu.VMEM((width, seq), BF),
            pltpu.VMEM((seq, width), BF),
            pltpu.VMEM((seq, width), BF),
            pltpu.VMEM((width, seq), BF),
            pltpu.VMEM((heads, seq), F32),
            pltpu.VMEM((2, seq, step), F32),
            pltpu.VMEM((2, seq, step), F32),
            pltpu.VMEM((seq, heads * step), BF),
            pltpu.VMEM((seq, heads * step), BF),
            pltpu.VMEM((seq, width), F32),
            pltpu.VMEM((seq, width), F32),
            pltpu.VMEM((width, seq), F32),
        ],
        compiler_params=params(26, 1),
        cost_estimate=cost(15),
        name="attention_back",
    )(*operands)
    return out[:chips], out[chips : 2 * chips], out[2 * chips], out[2 * chips + 1]


def gelu_both(x):
    away = jnp.abs(x)
    t = 1.0 / (1.0 + (0.3275911 * 0.5**0.5) * away)
    bell = jnp.exp(-0.5 * (x * x))
    poly = t * (
        0.127414796
        + t * (-0.142248368 + t * (0.7107068705 + t * (-0.7265760135 + t * 0.5307027145)))
    )
    tail = poly * bell
    phi = jnp.where(x >= 0, 1.0 - tail, tail)
    return x * phi, phi + x * (bell * 0.3989422804014327)


def mlp_call(body, pairs, extra, weight, bias, outs, parts, scratch, name):
    rows, model = pairs[0].shape
    units = weight.shape[1] // 2
    step = min(256, units)
    blocks = units // step
    cols = lambda j: (0, j)
    in_specs = [whole((rows, model)) for _ in pairs]
    in_specs += [pl.BlockSpec((2 * rows, step), cols) for _ in extra]
    in_specs += [
        pl.BlockSpec((model, step), cols),
        pl.BlockSpec((model, step), lambda j: (0, blocks + j)),
        pl.BlockSpec((1, step), cols),
    ]
    out_specs = [pl.BlockSpec((2 * rows, step), cols) for _ in outs]
    out_specs += [pl.BlockSpec((1, step), cols)]
    out_specs += [whole((rows, model))] * (2 * parts)
    out_shape = [pltpu.HBM((2 * rows, units), d) for d in outs] + [sds((1, units), F32)]
    out_shape += [sds((rows, model), BF)] * (2 * parts)
    count = len(pairs) // 2
    return pl.pallas_call(
        body,
        grid=(blocks,),
        in_specs=in_specs,
        out_specs=out_specs,
        out_shape=out_shape,
        scratch_shapes=[pltpu.VMEM((2 * rows, model), F32)] * parts
        + [pltpu.VMEM((2 * rows, step), F32)] * scratch,
        compiler_params=params(8 + 5 * parts, 1),
        cost_estimate=cost(0.5),
        name=name,
    )(*pairs, *map(late, extra), weight, weight, bias)


def clear(*refs):
    @pl.when(pl.program_id(0) == 0)
    def _():
        for ref in refs:
            ref[...] = jnp.zeros_like(ref)


def finish(acc, low, high):
    rows = low.shape[0]

    @pl.when(pl.program_id(0) == pl.num_programs(0) - 1)
    def _():
        low[...] = acc[:rows, :].astype(BF)
        high[...] = acc[rows:, :].astype(BF)


CHUNK = 32


def mlp_forward(pair, weight, bias):
    rows = pair[0].shape[0]

    def body(a, b, w1_ref, w2_ref, bias_ref, act_ref, slope_ref, sum_ref, lo, hi, acc, pre):
        clear(acc, sum_ref)
        shift = bias_ref[...]
        for i, x in enumerate((a, b)):
            pre[i * rows : (i + 1) * rows, :] = dot(x[...], w1_ref[...])
        for i in range(2):
            at = slice(i * rows, (i + 1) * rows)
            for r in range(i * rows, (i + 1) * rows, CHUNK):
                act, slope = gelu_both(pre[r : r + CHUNK, :] + shift)
                act_ref[r : r + CHUNK, :] = act.astype(BF)
                slope_ref[r : r + CHUNK, :] = slope.astype(BF)
            acc[at, :] += dot_bt(act_ref[at, :], w2_ref[...])
        finish(acc, lo, hi)

    act, slope, _, lo, hi = mlp_call(body, pair, [], weight, bias, [BF, BF], 1, 1, "mlp_forward")
    return act, slope, lo, hi


def mlp_backward(pair, slope, weight, bias):
    rows = pair[0].shape[0]

    def body(a, b, slope_ref, w1_ref, w2_ref, bias_ref, dpre_ref, sum_ref, lo, hi, acc, pre):
        clear(acc)
        for i, g in enumerate((a, b)):
            pre[i * rows : (i + 1) * rows, :] = dot(g[...], w2_ref[...])
        sums = jnp.zeros((8, bias_ref.shape[1]), F32)
        for i in range(2):
            at = slice(i * rows, (i + 1) * rows)
            for r in range(i * rows, (i + 1) * rows, CHUNK):
                d = pre[r : r + CHUNK, :] * slope_ref[r : r + CHUNK, :].astype(F32)
                d = d.astype(BF)
                dpre_ref[r : r + CHUNK, :] = d
                sums = sums + fold(d.astype(F32), jnp.sum)
            acc[at, :] += dot_bt(dpre_ref[at, :], w1_ref[...])
        sum_ref[...] = jnp.sum(sums, axis=0, keepdims=True)
        finish(acc, lo, hi)

    dpre, sums, lo, hi = mlp_call(
        body, pair, [slope], weight, bias, [BF], 1, 1, "mlp_backward"
    )
    return dpre, sums, lo, hi


def mlp_both(pair, grads, weight, bias):
    rows = pair[0].shape[0]

    def body(
        a, b, c, d, w1_ref, w2_ref, bias_ref, act_ref, dpre_ref, sum_ref,
        lo, hi, blo, bhi, acc, back, pre, grad,
    ):
        clear(acc, back)
        shift = bias_ref[...]
        for i, (x, g) in enumerate(((a, c), (b, d))):
            at = slice(i * rows, (i + 1) * rows)
            pre[at, :] = dot(x[...], w1_ref[...])
            grad[at, :] = dot(g[...], w2_ref[...])
        sums = jnp.zeros((8, bias_ref.shape[1]), F32)
        for i in range(2):
            at = slice(i * rows, (i + 1) * rows)
            for r in range(i * rows, (i + 1) * rows, CHUNK):
                act, slope = gelu_both(pre[r : r + CHUNK, :] + shift)
                act_ref[r : r + CHUNK, :] = act.astype(BF)
                dpre = (grad[r : r + CHUNK, :] * slope).astype(BF)
                dpre_ref[r : r + CHUNK, :] = dpre
                sums = sums + fold(dpre.astype(F32), jnp.sum)
            back[at, :] += dot_bt(dpre_ref[at, :], w1_ref[...])
            acc[at, :] += dot_bt(act_ref[at, :], w2_ref[...])
        sum_ref[...] = jnp.sum(sums, axis=0, keepdims=True)
        finish(acc, lo, hi)
        finish(back, blo, bhi)

    act, dpre, sums, lo, hi, blo, bhi = mlp_call(
        body, [*pair, *grads], [], weight, bias, [BF, BF], 2, 2, "mlp_both"
    )
    return act, dpre, sums, lo, hi, blo, bhi


def weight_grads(products, dp, side, name, halves=True, heads=0):
    model = products[0][0][0].shape[1]
    step = model // dp
    half = step // 2
    cut = 2 if halves else 1
    sizes = [(len(left), len(right), right[0].shape[1]) for left, right in products]
    cols = sum(n for _, _, n in sizes)

    def body(side_ref, *refs):
        acc_ref = refs[-1]
        mine, other = refs[-3:-1] if halves else (refs[-2], None)
        at = base = 0
        for many, few, n in sizes:
            lefts, rights = refs[at : at + many], refs[at + many : at + many + few]
            at += many + few
            ratio = many // few
            acc = None
            for i in range(many):
                size = lefts[i].shape[0]
                here = slice((i % ratio) * size, (i % ratio + 1) * size)
                term = dot_at(lefts[i][...], rights[i // ratio][here, :])
                acc = term if acc is None else acc + term
            if halves:
                acc_ref[:, base : base + n] = acc
            elif heads and not base:
                size = n // (3 * heads)
                for k in range(3 * heads):
                    head, kind = k // 3, k % 3
                    at_k = (kind * heads + head) * size
                    mine[:, k * size : (k + 1) * size] = acc[:, at_k : at_k + size].astype(BF)
            else:
                mine[:, base : base + n] = acc.astype(BF)
            base += n
        if not halves:
            return
        low = pl.multiple_of(side_ref[0] * half, half)
        high = pl.multiple_of((1 - side_ref[0]) * half, half)
        mine[...] = acc_ref[pl.ds(low, half), :].astype(BF)
        other[...] = acc_ref[pl.ds(high, half), :].astype(BF)

    specs, operands = [pl.BlockSpec(memory_space=pltpu.SMEM)], [side.reshape(1)]
    for left, right in products:
        specs += [pl.BlockSpec((a.shape[0], step), lambda i: (0, i)) for a in left]
        specs += [whole(b.shape) for b in right]
        operands += [*left, *right]
    return pl.pallas_call(
        body,
        grid=(dp,),
        in_specs=specs,
        out_specs=[pl.BlockSpec((step // cut, cols), lambda i: (i, 0))] * cut,
        out_shape=[sds((model // cut, cols), BF)] * cut,
        scratch_shapes=[pltpu.VMEM((step, cols), F32)],
        compiler_params=params(14, 1),
        cost_estimate=cost(5),
        name=name,
    )(*operands)


def pieces(chunks):
    return [p for pair in chunks for p in pair]


def shards(
    tokens, cotangent, ln1_gain, ln1_bias, w_qkv, qv_bias, w_out, out_bias, scale_attn,
    ln2_gain, ln2_bias, w_fc1, fc1_bias, w_fc2, fc2_bias, scale_mlp,
):
    side = lax.axis_index("section")
    first = side == 0
    dp = lax.axis_size("dp")
    here = lax.axis_index("dp")
    chips = lax.axis_size("tensor") // 2
    rows, model = tokens.shape[2:]
    heads = qv_bias.shape[1]
    size = qv_bias.shape[2] * dp // 2
    width = heads * size
    units = w_fc1.shape[2]
    part = model // dp

    x0 = lax.dynamic_index_in_dim(tokens, side, 0, keepdims=False).reshape(rows, model)
    grad_top = lax.dynamic_index_in_dim(cotangent, side, 0, keepdims=False).reshape(rows, model)

    vectors = (ln1_gain, ln1_bias, out_bias, scale_attn, ln2_gain, ln2_bias, fc2_bias, scale_mlp)
    packed = jnp.concatenate(
        [v.reshape(-1) for v in vectors] + [fc1_bias.reshape(-1), qv_bias.reshape(-1)]
    )
    own_qkv = w_qkv.reshape(part, heads, 3, size).swapaxes(1, 2).reshape(part, 3 * width)
    own_att = jnp.concatenate([own_qkv, w_out[0].T], axis=1)
    give_att = half_of(own_att, 1 - side)
    came_att = swap_section(give_att)
    came_small = swap_section(tie(packed, give_att))
    both_small = jnp.concatenate(
        [jnp.where(first, packed, came_small), jnp.where(first, came_small, packed)]
    )
    cols = 4 * width
    tail = -(-both_small.size // (16 * cols)) * 16
    both_small = jnp.pad(both_small, (0, tail * cols - both_small.size)).reshape(tail, cols)
    mine_att = half_of(own_att, side)
    ring_att0 = jnp.concatenate([jnp.where(first, mine_att, came_att), both_small])
    ring_att1 = jnp.where(first, came_att, mine_att)
    hops_att0 = direct(ring_att0)
    own_ff = jnp.concatenate([w_fc1[0], w_fc2[0].T], axis=1)
    rest_att = swap_section(tie(mine_att, ring_att0))
    came_ff = swap_section(tie(half_of(own_ff, 1 - side), ring_att0))
    mine_ff = half_of(own_ff, side)
    ring_ff0 = jnp.where(first, mine_ff, came_ff)
    ring_ff1 = jnp.where(first, came_ff, mine_ff)

    def other_half(own, rest):
        left = half_of(own, 1 - side)
        return jnp.where(first, left, rest), jnp.where(first, rest, left)


    backs = [swap_section(v) for v in hops_att0]
    back = [ring_att0, *hops_att0]
    back[2] = tie(back[2], backs[-1])
    flat = in_order([v[-tail:] for v in back])
    flat = flat.reshape(dp, -1)[:, : 2 * packed.size].reshape(dp, 2, -1).astype(F32)
    cut = 8 * part
    vecs = flat[:, :, :cut].reshape(dp, 2, 8, part).transpose(1, 2, 0, 3).reshape(2, 8, model)
    vecs = (vecs[0], vecs[1])
    bias_fc1 = flat[:, :, cut : cut + units // dp].swapaxes(0, 1).reshape(2, 1, units)
    qv = flat[:, :, cut + units // dp :].reshape(dp, 2, heads, -1).transpose(1, 2, 0, 3)
    qv = qv.reshape(2, heads, 2, size)
    bias_qkv = jnp.stack([qv[:, :, 0], jnp.zeros_like(qv[:, :, 0]), qv[:, :, 1]], axis=1)
    bias_qkv = bias_qkv.reshape(2, 1, 3 * width)

    norm1 = norm_first(tie(x0, came_ff), vecs[0])
    rest_ff = swap_section(tie(mine_ff, norm1))
    rest_att0, rest_att1 = other_half(own_att, rest_att)
    rest_ff0, rest_ff1 = other_half(own_ff, rest_ff)
    att1 = Ring(ring_att1)
    att0 = assemble([(tie(ring_att0, norm1), rest_att0), *zip(hops_att0, backs)], model)
    ff0, ff1 = Ring(ring_ff0), Ring(ring_ff1)
    hop_ff0 = ff0.hop(norm1)

    def projection(weight, s):
        return lambda pair: project_qkv(pair, weight, bias_qkv[s])

    chunks0, qkv0 = gather_tokens(norm1, projection(att0, 0), [rest_ff, *hop_ff0])
    beside = [*ff0.hop(), *ff0.back()]
    kept0, lse0, sames, others = attention(qkv0, att0, size)
    terms, _ = scatter_tokens(
        sames,
        tie(others, *beside),
        beside=lambda gate: [*ff0.hop(gate), *ff0.back(gate)],
    )
    attended0, residual0, norm2 = after_attention(x0, terms, vecs[0])
    ff0.back()
    beside = [*att1.hop(norm2), *att1.hop()]
    w_ff0 = assemble([(ring_ff0, rest_ff0), *zip(ff0.hops, ff0.backs)], model)
    second0, mlp0 = gather_tokens(
        norm2, lambda pair: mlp_forward(pair, w_ff0, bias_fc1[0]), beside
    )
    act0, slope0, sames, others = zip(*mlp0)
    beside = [*att1.hop(second0[-1][0]), *att1.back(second0[-1][0])]
    terms, _ = scatter_tokens(
        sames,
        [others[0], *[tie(v, *beside) for v in others[1:]]],
        beside=lambda gate: [*ff1.hop(gate), *att1.back(gate), *att1.back(gate)],
    )
    mlp_out0, y0, norm1 = after_mlp(residual0, terms, vecs[0], vecs[1])

    w_att1 = assemble([(ring_att1, rest_att1), *zip(att1.hops, att1.backs)], model)
    low1, sums_fc2_1 = start_back(grad_top, vecs[1])
    beside = [*ff1.hop(norm1), *ff1.back(norm1)]
    chunks1, qkv1 = gather_tokens(norm1, projection(w_att1, 1), beside)
    gate = chunks1[-1][0]
    came = [from_chip(tie(low1, gate), step) for step in range(1, chips)]
    beside = [*came, *ff1.hop(gate), *ff1.back(gate)]
    kept1, lse1, sames, others = attention(qkv1, w_att1, size)
    others = tie(others, *beside)
    grads1 = [(low1, core_swap(low1))] + [(v, core_swap(tie(v, lse1))) for v in came]
    terms, _ = scatter_tokens(
        sames, others, beside=lambda gate: [*ff1.back(gate), *pieces(grads1)]
    )
    attended1, residual1, norm2 = after_attention(y0, terms, vecs[1])
    w_ff1 = assemble([(ring_ff1, rest_ff1), *zip(ff1.hops, ff1.backs)], model)
    spare = list(grads1)
    second1, mlp1 = gather_tokens(
        norm2, lambda pair: mlp_both(pair, spare.pop(0), w_ff1, bias_fc1[1])
    )
    act1, dpre1, sums_fc1_1, sames_y1, others_y1, sames, others = zip(*mlp1)

    def grad_ff(second, dpre, grads, act):
        return lambda after: weight_grads(
            [
                (pieces(second), [late(tie(dpre[0], after)), *map(late, dpre[1:])]),
                (pieces(grads), [late(a) for a in act]),
            ],
            dp,
            side,
            "grad_ff",
        )

    def grad_att(chunks, dqkv, datt, kept):
        return lambda after: weight_grads(
            [
                (pieces(chunks), [late(tie(dqkv[0], after)), *map(late, dqkv[1:])]),
                (pieces(datt), [late(a) for a in kept]),
            ],
            dp,
            side,
            "grad_att",
            False,
            heads,
        )[0]

    old = [tuple(map(late, pair)) for pair in grads1]
    terms, g = scatter_tokens(sames, others, grad_ff(second1, dpre1, old, act1))
    sum_ff1 = RingSum((0, 1), *g)
    dres1, low, sums1 = back_second(grad_top, residual1, attended1, terms, vecs[1])
    came_y0 = lax.ppermute(tie(y0, low), "section", [(1, 0)])
    datt, _ = gather_tokens(low, lambda pair: pair[0], sum_ff1.step())
    sums_y1, local_y1 = core_sums(sames_y1, [tie(v, low) for v in others_y1])
    terms_y1 = send_sums([tie(v, datt[-1][0]) for v in sums_y1])
    beside = [came_y0, *terms_y1, *sum_ff1.step(low)]
    dqkv, sames, others, qkv_sums1 = attention_back(qkv1, kept1, lse1, datt, w_att1, size)
    old = [tuple(map(late, pair)) for pair in chunks1]
    terms, g = scatter_tokens(
        sames, tie(others, *beside), grad_att(old, dqkv, datt, kept1), sum_ff1.step
    )
    sum_att1 = RingSum((0, 1), g)
    sum_att1.step()
    dx1, low0, edge1 = back_first(dres1, late(y0), terms, vecs[1], late(mlp_out0), vecs[0])

    y1, sums_sc_1 = last_output(
        residual1, [tie(sames_y1[0], low0), *terms_y1, local_y1], grad_top, vecs[1]
    )

    slopes = list(slope0)
    grads0, mlp_back0 = gather_tokens(
        low0,
        lambda pair: mlp_backward(pair, slopes.pop(0), w_ff0, bias_fc1[0]),
        [y1, *sum_ff1.step(low0)],
    )
    dpre0, sums_fc1_0, sames, others = zip(*mlp_back0)
    hop_att1 = sum_att1.step(grads0[-1][0])
    old = [tuple(map(late, pair)) for pair in second0]
    terms, g = scatter_tokens(
        sames,
        others,
        grad_ff(old, dpre0, grads0, act0),
        lambda gate: [*sum_ff1.step(gate), *hop_att1],
    )
    sum_ff0 = RingSum((1, 0), *g)
    dres0, low, sums0 = back_second(
        dx1, late(residual0), late(attended0), terms, vecs[0]
    )
    beside = [*sum_att1.step(low), *sum_ff0.step(low)]
    datt, _ = gather_tokens(low, lambda pair: pair[0], beside)
    beside = [*sum_att1.step(low), *sum_ff0.step(low)]
    dqkv, sames, others, qkv_sums0 = attention_back(qkv0, kept0, lse0, datt, att0, size)
    old = [tuple(map(late, pair)) for pair in chunks0]
    others = tie(others, *beside)
    beside = sum_ff0.step(others)
    terms, g = scatter_tokens(
        sames, others, grad_att(old, dqkv, datt, kept0), lambda gate: beside
    )
    step_ff0 = sum_ff0.step(terms[1])
    sum_att0 = RingSum((1, 0), g)
    sum_att0.step()
    going = sum_att0.step()
    terms = [late(terms[0]), *terms[1:-1], late(terms[-1])]
    dx0, edge0 = back_first(late(dres0), late(x0), terms, vecs[0])
    came_dx0 = lax.ppermute(dx0, "section", [(1, 0)])
    second_hop = sum_att0.step(dx0)
    came_y1 = lax.ppermute(tie(y1, sum_att0.sent), "section", [(0, 1)])
    step_att1 = sum_att1.step(dx0)
    third_hop = sum_att0.step()
    sent = sum_att0.sent
    last_ff0 = sum_ff0.step()
    sum_att0.step()
    came_dx1 = lax.ppermute(tie(dx1, sent), "section", [(0, 1)])

    def both(low, high, came_low, came_high):
        mine = jnp.where(first, low, high)
        came = jnp.where(first, came_low, came_high)
        return jnp.stack([jnp.where(first, mine, came), jnp.where(first, came, mine)])[None, :, None]

    block_out = both(y0, y1, came_y0, came_y1)
    input_grads = both(dx0, dx1, came_dx0, came_dx1)
    sum_att0.came = tie(sum_att0.came, block_out, input_grads)

    def by_unit(qkv_sums, unit_sums):
        q = qkv_sums[:, :width].reshape(heads, 1, size)
        v = qkv_sums[:, 2 * width :].reshape(heads, 1, size)
        bias = jnp.concatenate([q, v], 1).reshape(heads, dp, -1).swapaxes(0, 1).reshape(dp, -1)
        return jnp.concatenate([bias, unit_sums.reshape(dp, -1)], axis=1)

    unit0 = by_unit(tie(qkv_sums0, dx0), sum(sums_fc1_0))
    unit1 = by_unit(tie(qkv_sums1, dx0), sum(sums_fc1_1))
    vec = jnp.concatenate(
        [edge0[:2], sums0[:4], edge1[2:4], edge1[:2], sums1[:4], sums_sc_1[:1], sums_fc2_1[:1]]
    )
    vec = tie(vec, *going, *step_ff0)
    vec = vec + core_swap(vec)
    vec = tie(sum([from_chip(vec, step) for step in range(1, chips)], vec), *second_hop, came_y1)
    vec = tie(vec, sent, *last_ff0)
    vec = vec.reshape(2, 8, dp, part).swapaxes(1, 2).reshape(2, dp, 8 * part)
    vec0 = jnp.concatenate([vec[0], unit0], axis=1)
    vec1 = jnp.concatenate([vec[1], unit1], axis=1)
    own = jnp.where(first, vec0, vec1) + swap_section(jnp.where(first, vec1, vec0))
    own = tie(own, *step_att1, came_dx1, sum_att0.own)
    vec = lax.dynamic_slice_in_dim(own, here, 1, 0)
    for step in range(1, dp):
        pairs = [(i, (i + step) % dp) for i in range(dp)]
        other = lax.dynamic_slice_in_dim(own, lax.rem(here + step, dp), 1, 0)
        vec = vec + lax.ppermute(other, "dp", pairs)
    cut = 8 * part + heads * (2 * size // dp)
    bias_grad = vec[:, 8 * part : cut].reshape(1, heads, -1)
    fc1_grad = vec[:, cut:].reshape(1, 1, -1)
    g_ln1, b_ln1, g_ln2, b_ln2, g_sc_attn, g_out_bias, g_sc_mlp, g_fc2_bias = (
        vec[:, i * part : (i + 1) * part] for i in range(8)
    )

    def owned(low, high):
        top = jnp.where(first, low.own, high.came.astype(F32))
        bottom = jnp.where(first, low.came.astype(F32), high.own)
        return jnp.concatenate([top, bottom], 0)

    g_ff = owned(sum_ff0, sum_ff1)
    g_att = jnp.where(
        first,
        sum_att0.own + sum_att0.came.astype(F32),
        sum_att1.own + sum_att1.came.astype(F32),
    )
    g_qkv = g_att[None, :, : 3 * width]
    g_out = g_att[:, 3 * width :].T[None]
    g_fc1 = g_ff[:, :units][None]
    g_fc2 = g_ff[:, units:].T[None]
    return (
        block_out, input_grads, g_ln1, b_ln1, g_qkv, bias_grad, g_out, g_out_bias, g_sc_attn,
        g_ln2, b_ln2, g_fc1, fc1_grad, g_fc2, g_fc2_bias, g_sc_mlp,
    )


def solution(mesh):
    vec = P("section", "dp")
    by_row = P("section", "dp", "tensor")
    by_unit = P("section", "tensor", "dp")
    data = P(None, "dp", "tensor", None)
    split = P("section", None, "dp", "tensor", None)
    given = (
        vec, vec, by_row, by_unit, by_unit, vec, vec, vec, vec, by_row, by_unit, by_unit, vec, vec,
    )
    return jax.shard_map(
        shards,
        mesh=mesh,
        in_specs=(data, data) + given,
        out_specs=(split, split) + given,
        check_vma=False,
    )
```

profile of v0, /device:TPU:0, one launch (start us, length us, event | category | flops | bytes accessed | tf_op | source)
XLA Modules:
  0.0 525.0 jit_solution(16264226020359285228)
XLA Ops:
  8.2 3.8 collective-permute-done.1
  29.6 9.8 %collective-permute-done.6.refs_2_ = bf16[144,1024]{1,0:T(8,128)(2,1)} collective-permute-done((bf16[144,1024]{1,0:T(8,128)(2,1)}, bf16[144,1024]{1,0:T(8,128)(2,1)}, u32[]{:S(2)}, u32[]{:S(2)}) %collective-permute-start.6) | collective-permute-done | bytes 294944 | tf_op jit(solution)/shard_map/ppermute | solution.py:165
  40.9 3.7 collective-permute-done.4.refs_4_
  60.0 6.2 %collective-permute-done.11.a_ref.refs_2_ = bf16[256,1024]{1,0:T(8,128)(2,1)S(1)} collective-permute-done((bf16[256,1024]{1,0:T(8,128)(2,1)S(1)}, bf16[256,1024]{1,0:T(8,128)(2,1)S(1)}, u32[]{:S(2)}, u32[]{:S(2)}) %collective-permute-start.11) | collective-permute-done | bytes 524320 | tf_op jit(solution)/shard_map/ppermute | solution.py:66
  75.0 9.5 %attention.2 = (bf16[512,256]{1,0:T(8,128)(2,1)}, bf16[512,256]{1,0:T(8,128)(2,1)}, f32[4,1024]{1,0:T(4,128)S(1)}, bf16[256,1024]{1,0:T(8,128)(2,1)S(1)}, bf16[2...) custom-call(bf16[512,768]{1,0:T(8,128)(2,1)S(1)} %project_qkv.4.refs_0_, bf16[512,768]{1,0:T(8,128)(2,1)S(1)} %project_qkv.5.refs_1_, ...), custom_call_target="tpu_custom_call" | custom-call | flops 10350000128 | tf_op jit(solution)/shard_map/attention/pallas_call | solution.py:522
  94.2 9.3 %collective-permute-done.18.refs_2_ = bf16[256,1024]{1,0:T(8,128)(2,1)S(1)} collective-permute-done((bf16[256,1024]{1,0:T(8,128)(2,1)S(1)}, bf16[256,1024]{1,0:T(8,128)(2,1)S(1)}, u32[]{:S(2)}, u32[]{:S(2)}) %collective-permute-start.18) | collective-permute-done | bytes 524320 | tf_op jit(solution)/shard_map/ppermute | solution.py:66
  111.8 8.1 %collective-permute-done.24.refs_2_ = bf16[128,1024]{1,0:T(8,128)(2,1)S(1)} collective-permute-done((bf16[128,1024]{1,0:T(8,128)(2,1)S(1)}, bf16[128,1024]{1,0:T(8,128)(2,1)S(1)}, u32[]{:S(2)}, u32[]{:S(2)}) %collective-permute-start.24) | collective-permute-done | bytes 262176 | tf_op jit(solution)/shard_map/ppermute | solution.py:184
  123.6 6.6 %mlp_forward.2 = (bf16[512,1024]{1,0:T(8,128)(2,1)}, bf16[512,1024]{1,0:T(8,128)(2,1)}, f32[1,1024]{1,0:T(1,128)}, bf16[256,1024]{1,0:T(8,128)(2,1)S(1)}, bf16[256,1024]{1,0:T(8,128)(2,1)S(1)}) custom-call(bf16[256,1024]{1,0:T(8,128)(2,1)S(1)} %get-tuple-element.194.a.refs_0_, bf16[256,1024]{1,0:T(8,128)(2,1)S(1)} %collective-permute-done.21.b.refs_1_, ...), custom_call_target="tpu_custom_call" | custom-call | flops 575000000 | tf_op jit(solution)/shard_map/mlp_forward/pallas_call | solution.py:726
  132.2 6.5 %mlp_forward.3 = (bf16[512,1024]{1,0:T(8,128)(2,1)}, bf16[512,1024]{1,0:T(8,128)(2,1)}, f32[1,1024]{1,0:T(1,128)}, bf16[256,1024]{1,0:T(8,128)(2,1)S(1)}, bf16[256,1024]{1,0:T(8,128)(2,1)S(1)}) custom-call(bf16[256,1024]{1,0:T(8,128)(2,1)S(1)} %collective-permute-done.23.a.refs_2_, bf16[256,1024]{1,0:T(8,128)(2,1)S(1)} %collective-permute-done.26.b.refs_3_, ...), custom_call_target="tpu_custom_call" | custom-call | flops 575000000 | tf_op jit(solution)/shard_map/mlp_forward/pallas_call | solution.py:726
  146.4 7.1 %collective-permute-done.33.refs_5_ = bf16[128,1024]{1,0:T(8,128)(2,1)S(1)} collective-permute-done((bf16[128,1024]{1,0:T(8,128)(2,1)S(1)}, bf16[128,1024]{1,0:T(8,128)(2,1)S(1)}, u32[]{:S(2)}, u32[]{:S(2)}) %collective-permute-start.33) | collective-permute-done | bytes 262176 | tf_op jit(solution)/shard_map/ppermute | solution.py:118
  153.5 5.2 collective-permute-done.34.refs_7_
  167.4 9.2 %collective-permute-done.36.a_ref.refs_2_ = bf16[256,1024]{1,0:T(8,128)(2,1)S(1)} collective-permute-done((bf16[256,1024]{1,0:T(8,128)(2,1)S(1)}, bf16[256,1024]{1,0:T(8,128)(2,1)S(1)}, u32[]{:S(2)}, u32[]{:S(2)}) %collective-permute-start.36) | collective-permute-done | bytes 524320 | tf_op jit(solution)/shard_map/ppermute | solution.py:66
  183.8 9.9 %attention.3 = (bf16[512,256]{1,0:T(8,128)(2,1)}, bf16[512,256]{1,0:T(8,128)(2,1)}, f32[4,1024]{1,0:T(4,128)S(1)}, bf16[256,1024]{1,0:T(8,128)(2,1)S(1)}, bf16[2...) custom-call(bf16[512,768]{1,0:T(8,128)(2,1)S(1)} %project_qkv.6.refs_0_, bf16[512,768]{1,0:T(8,128)(2,1)S(1)} %project_qkv.7.refs_1_, ...), custom_call_target="tpu_custom_call" | custom-call | flops 10350000128 | tf_op jit(solution)/shard_map/attention/pallas_call | solution.py:522
  200.9 12.4 %collective-permute-done.44.refs_2_ = bf16[256,1024]{1,0:T(8,128)(2,1)S(1)} collective-permute-done((bf16[256,1024]{1,0:T(8,128)(2,1)S(1)}, bf16[256,1024]{1,0:T(8,128)(2,1)S(1)}, u32[]{:S(2)}, u32[]{:S(2)}) %collective-permute-start.44) | collective-permute-done | bytes 524320 | tf_op jit(solution)/shard_map/ppermute | solution.py:66
  219.7 9.0 %mlp_both.2 = (bf16[512,1024]{1,0:T(8,128)(2,1)}, bf16[512,1024]{1,0:T(8,128)(2,1)}, f32[1,1024]{1,0:T(1,128)S(1)}, bf16[256,1024]{1,0:T(8,128)(2,1)S(1)}, bf16[...) custom-call(bf16[256,1024]{1,0:T(8,128)(2,1)S(1)} %get-tuple-element.227.a.refs_0_, ...), custom_call_target="tpu_custom_call" | custom-call | flops 575000000 | tf_op jit(solution)/shard_map/mlp_both/pallas_call | solution.py:726
  232.1 8.9 %mlp_both.3 = (bf16[512,1024]{1,0:T(8,128)(2,1)}, bf16[512,1024]{1,0:T(8,128)(2,1)}, f32[1,1024]{1,0:T(1,128)S(1)}, bf16[256,1024]{1,0:T(8,128)(2,1)S(1)}, bf16[...) custom-call(bf16[256,1024]{1,0:T(8,128)(2,1)S(1)} %collective-permute-done.49.a.refs_2_, ...), custom_call_target="tpu_custom_call" | custom-call | flops 575000000 | tf_op jit(solution)/shard_map/mlp_both/pallas_call | solution.py:726
  250.0 8.3 %grad_ff.2 = (bf16[512,2048]{1,0:T(8,128)(2,1)S(1)}, bf16[512,2048]{1,0:T(8,128)(2,1)S(1)}) custom-call(s32[1]{0:T(128)} %bitcast.15.side_ref, bf16[256,1024]{1,0:T(8,128)(2,1)S(1)} %copy-done.33, bf16[256,1024]{1,0:T(8,128)(2,1)S(1)} %copy-done.35, bf16[256,1024]{1,0:T(8,128)(2,1)S(1)} %copy-done.37, bf16[256,1024]{1,0:T(8,128)(2,1)S(1)} %copy-done.41, ...), custom_call_target="tpu_custom_call" | custom-call | flops 5750000128 | tf_op jit(solution)/shard_map/grad_ff/pallas_call | solution.py:884
  264.3 9.0 %collective-permute-done.56 = bf16[128,2048]{1,0:T(8,128)(2,1)S(1)} collective-permute-done((bf16[128,2048]{1,0:T(8,128)(2,1)S(1)}, bf16[128,2048]{1,0:T(8,128)(2,1)S(1)}, u32[]{:S(2)}, u32[]{:S(2)}) %collective-permute-start.56) | collective-permute-done | bytes 524320 | tf_op jit(solution)/shard_map/ppermute | solution.py:118
  278.1 17.2 %attention_back.2 = (bf16[512,768]{1,0:T(8,128)(2,1)}, bf16[512,768]{1,0:T(8,128)(2,1)}, bf16[256,1024]{1,0:T(8,128)(2,1)}, bf16[256,1024]{1,0:T(8,128)(2,1)}, b...) custom-call(bf16[512,768]{1,0:T(8,128)(2,1)} %copy-done.12, bf16[512,768]{1,0:T(8,128)(2,1)} %copy-done.13, ...), custom_call_target="tpu_custom_call" | custom-call | flops 17250000896 | tf_op jit(solution)/shard_map/attention_back/pallas_call | solution.py:664
  303.2 5.3 %grad_att.2 = bf16[1024,1024]{1,0:T(8,128)(2,1)S(1)} custom-call(s32[1]{0:T(128)} %bitcast.15.side_ref, bf16[256,1024]{1,0:T(8,128)(2,1)} %copy-done.22, bf16[256,1024]{1,0:T(8,128)(2,1)} %copy-done.23, bf16[256,1024]{1,0:T(8,128)(2,1)} %copy-done.24, bf16[256,1024]{1,0:T(8,128)(2,1)} %copy-done.25, bf16[512,768]{1,0:T(8,128)(2,1)} %get-tuple-element.263.refs_4_, ...), custom_call_target="tpu_custom_call" | custom-call | flops 5750000128 | tf_op jit(solution)/shard_map/grad_att/pallas_call | solution.py:884
  308.6 4.8 collective-permute-done.64.refs_3_
  325.7 5.7 %mlp_backward.2 = (bf16[512,1024]{1,0:T(8,128)(2,1)}, f32[1,1024]{1,0:T(1,128)S(1)}, bf16[256,1024]{1,0:T(8,128)(2,1)S(1)}, bf16[256,1024]{1,0:T(8,128)(2,1)S(1)}) custom-call(bf16[256,1024]{1,0:T(8,128)(2,1)S(1)} %get-tuple-element.269.a.refs_6_, bf16[256,1024]{1,0:T(8,128)(2,1)S(1)} %collective-permute-done.68.b.refs_7_, ...), custom_call_target="tpu_custom_call" | custom-call | flops 575000000 | tf_op jit(solution)/shard_map/mlp_backward/pallas_call | solution.py:726
  338.8 5.9 %mlp_backward.3 = (bf16[512,1024]{1,0:T(8,128)(2,1)}, f32[1,1024]{1,0:T(1,128)S(1)}, bf16[256,1024]{1,0:T(8,128)(2,1)S(1)}, bf16[256,1024]{1,0:T(8,128)(2,1)}) custom-call(bf16[256,1024]{1,0:T(8,128)(2,1)S(1)} %collective-permute-done.69.a.refs_8_, bf16[256,1024]{1,0:T(8,128)(2,1)S(1)} %collective-permute-done.72.b.refs_9_, ...), custom_call_target="tpu_custom_call" | custom-call | flops 575000000 | tf_op jit(solution)/shard_map/mlp_backward/pallas_call | solution.py:726
  354.0 8.3 %grad_ff.3 = (bf16[512,2048]{1,0:T(8,128)(2,1)S(1)}, bf16[512,2048]{1,0:T(8,128)(2,1)S(1)}) custom-call(s32[1]{0:T(128)} %bitcast.15.side_ref, bf16[256,1024]{1,0:T(8,128)(2,1)} %copy-done.18, bf16[256,1024]{1,0:T(8,128)(2,1)} %copy-done.19, bf16[256,1024]{1,0:T(8,128)(2,1)} %copy-done.20, bf16[256,1024]{1,0:T(8,128)(2,1)} %copy-done.21, ...), custom_call_target="tpu_custom_call" | custom-call | flops 5750000128 | tf_op jit(solution)/shard_map/grad_ff/pallas_call | solution.py:884
  376.2 7.7 %collective-permute-done.79.refs_7_.refs_8_ = bf16[256,1024]{1,0:T(8,128)(2,1)S(1)} collective-permute-done((bf16[256,1024]{1,0:T(8,128)(2,1)}, bf16[256,1024]{1,0:T(8,128)(2,1)S(1)}, u32[]{:S(2)}, u32[]{:S(2)}) %collective-permute-start.79) | collective-permute-done | bytes 524320 | tf_op jit(solution)/shard_map/ppermute | solution.py:66
  383.9 4.7 collective-permute-done.80
  397.2 17.4 %attention_back.3 = (bf16[512,768]{1,0:T(8,128)(2,1)}, bf16[512,768]{1,0:T(8,128)(2,1)}, bf16[256,1024]{1,0:T(8,128)(2,1)}, bf16[256,1024]{1,0:T(8,128)(2,1)}, b...) custom-call(bf16[512,768]{1,0:T(8,128)(2,1)} %copy-done.10, bf16[512,768]{1,0:T(8,128)(2,1)} %copy-done.11, ...), custom_call_target="tpu_custom_call" | custom-call | flops 17250000896 | tf_op jit(solution)/shard_map/attention_back/pallas_call | solution.py:664
  426.5 5.4 %grad_att.3 = bf16[1024,1024]{1,0:T(8,128)(2,1)S(1)} custom-call(s32[1]{0:T(128)} %bitcast.15.side_ref, bf16[256,1024]{1,0:T(8,128)(2,1)} %copy-done.14, bf16[256,1024]{1,0:T(8,128)(2,1)} %copy-done.15, bf16[256,1024]{1,0:T(8,128)(2,1)} %copy-done.16, bf16[256,1024]{1,0:T(8,128)(2,1)} %copy-done.17, bf16[512,768]{1,0:T(8,128)(2,1)} %get-tuple-element.309.refs_4_, ...), custom_call_target="tpu_custom_call" | custom-call | flops 5750000128 | tf_op jit(solution)/shard_map/grad_att/pallas_call | solution.py:884
  452.1 4.4 collective-permute-start.91
  460.9 17.5 %collective-permute-done.95 = bf16[128,2048]{1,0:T(8,128)(2,1)} collective-permute-done((bf16[128,2048]{1,0:T(8,128)(2,1)S(1)}, bf16[128,2048]{1,0:T(8,128)(2,1)}, u32[]{:S(2)}, u32[]{:S(2)}) %collective-permute-start.95) | collective-permute-done | bytes 524320 | tf_op jit(solution)/shard_map/ppermute | solution.py:229
  478.3 3.8 collective-permute-start.101
  491.6 5.6 %collective-permute-start.94 = (bf16[256,1024]{1,0:T(8,128)(2,1)S(1)}, bf16[256,1024]{1,0:T(8,128)(2,1)S(1)}, u32[]{:S(2)}, u32[]{:S(2)}) collective-permute-start(bf16[256,1024]{1,0:T(8,128)(2,1)S(1)} %copy-done.57), channel_id=1, source_target_pairs={{0,16},{1,17},{2,18},{3,19},{4,20},{5,21},{6,22},{7,23},{8,24},{9,... | collective-permute-start | bytes 1572872 | tf_op jit(solution)/shard_map/ppermute | solution.py:1111
  (638 shorter events, 265.6 us)
Async XLA Ops:
  20.2 24.3 %collective-permute-start.4 = (bf16[144,1024]{1,0:T(8,128)(2,1)}, bf16[144,1024]{1,0:T(8,128)(2,1)}, u32[]{:S(2)}, u32[]{:S(2)}) collective-permute-start(bf16[144,1024]{1,0:T(8,128)(2,1)} %pad_maximum_fusion.1.refs_0_), channel_id=1, source_target_pairs={{0,8},{4,12},{8,0},{12,4},{1,9},{5,13},{9,1},{13,5},{2,10},{6,14},... | collective-permute-start | bytes 884744 | tf_op jit(solution)/shard_map/ppermute | solution.py:165
  20.3 19.1 %collective-permute-start.6 = (bf16[144,1024]{1,0:T(8,128)(2,1)}, bf16[144,1024]{1,0:T(8,128)(2,1)}, u32[]{:S(2)}, u32[]{:S(2)}) collective-permute-start(bf16[144,1024]{1,0:T(8,128)(2,1)} %pad_maximum_fusion.1.refs_0_), channel_id=1, source_target_pairs={{0,4},{4,8},{8,12},{12,0},{1,5},{5,9},{9,13},{13,1},{2,6},{6,10},{... | collective-permute-start | bytes 884744 | tf_op jit(solution)/shard_map/ppermute | solution.py:165
  21.3 24.8 %collective-permute-start.2 = (bf16[128,2048]{1,0:T(8,128)(2,1)S(1)}, bf16[128,2048]{1,0:T(8,128)(2,1)S(1)}, u32[]{:S(2)}, u32[]{:S(2)}) collective-permute-start(bf16[128,2048]{1,0:T(8,128)(2,1)S(1)} %fusion.7), channel_id=1, source_target_pairs={{0,16},{16,0},{1,17},{17,1},{2,18},{18,2},{3,19},{19,3},{4,20},{20... | collective-permute-start | bytes 1572872 | tf_op jit(solution)/shard_map/ppermute | solution.py:118
  28.1 19.8 %collective-permute-start.5 = (bf16[144,1024]{1,0:T(8,128)(2,1)S(1)}, bf16[144,1024]{1,0:T(8,128)(2,1)S(1)}, u32[]{:S(2)}, u32[]{:S(2)}) collective-permute-start(bf16[144,1024]{1,0:T(8,128)(2,1)S(1)} %collective-permute-done.3.refs_6_), channel_id=1, source_target_pairs={{0,16},{16,0},{1,17},{17,1},{2,18},{18,2},{3,19},{19,3},{4,20},{20... | collective-permute-start | bytes 884744 | tf_op jit(solution)/shard_map/ppermute | solution.py:118
  70.2 16.3 %collective-permute-start.15 = (bf16[128,2048]{1,0:T(8,128)(2,1)}, bf16[128,2048]{1,0:T(8,128)(2,1)S(1)}, u32[]{:S(2)}, u32[]{:S(2)}) collective-permute-start(bf16[128,2048]{1,0:T(8,128)(2,1)} %collective-permute-done.13.refs_2_), channel_id=1, source_target_pairs={{0,4},{4,8},{8,12},{12,0},{1,5},{5,9},{9,13},{13,1},{2,6},{6,10},{... | collective-permute-start | bytes 1572872 | tf_op jit(solution)/shard_map/ppermute | solution.py:184
  108.5 21.7 %collective-permute-start.23 = (bf16[256,1024]{1,0:T(8,128)(2,1)S(1)}, bf16[256,1024]{1,0:T(8,128)(2,1)S(1)}, u32[]{:S(2)}, u32[]{:S(2)}) collective-permute-start(bf16[256,1024]{1,0:T(8,128)(2,1)S(1)} %get-tuple-element.194.a.refs_0_), channel_id=1, source_target_pairs={{2,0},{3,1},{0,2},{1,3},{6,4},{7,5},{4,6},{5,7},{10,8},{11,9},{8,1... | collective-permute-start | bytes 1572872 | tf_op jit(solution)/shard_map/ppermute | solution.py:66
  144.3 16.2 %collective-permute-start.32 = (bf16[128,2048]{1,0:T(8,128)(2,1)S(1)}, bf16[128,2048]{1,0:T(8,128)(2,1)}, u32[]{:S(2)}, u32[]{:S(2)}) collective-permute-start(bf16[128,2048]{1,0:T(8,128)(2,1)S(1)} %copy-done.101), channel_id=1, source_target_pairs={{0,4},{4,8},{8,12},{12,0},{1,5},{5,9},{9,13},{13,1},{2,6},{6,10},{... | collective-permute-start | bytes 1572872 | tf_op jit(solution)/shard_map/ppermute | solution.py:184
  163.2 16.1 %collective-permute-start.37 = (bf16[128,2048]{1,0:T(8,128)(2,1)}, bf16[128,2048]{1,0:T(8,128)(2,1)S(1)}, u32[]{:S(2)}, u32[]{:S(2)}) collective-permute-start(bf16[128,2048]{1,0:T(8,128)(2,1)} %collective-permute-done.32.refs_2_), channel_id=1, source_target_pairs={{0,4},{4,8},{8,12},{12,0},{1,5},{5,9},{9,13},{13,1},{2,6},{6,10},{... | collective-permute-start | bytes 1572872 | tf_op jit(solution)/shard_map/ppermute | solution.py:184
  180.3 16.0 %collective-permute-start.41 = (bf16[128,2048]{1,0:T(8,128)(2,1)S(1)}, bf16[128,2048]{1,0:T(8,128)(2,1)S(1)}, u32[]{:S(2)}, u32[]{:S(2)}) collective-permute-start(bf16[128,2048]{1,0:T(8,128)(2,1)S(1)} %collective-permute-done.37.refs_4_), channel_id=1, source_target_pairs={{0,4},{4,8},{8,12},{12,0},{1,5},{5,9},{9,13},{13,1},{2,6},{6,10},{... | collective-permute-start | bytes 1572872 | tf_op jit(solution)/shard_map/ppermute | solution.py:184
  180.3 16.0 %collective-permute-start.42 = (bf16[128,2048]{1,0:T(8,128)(2,1)S(1)}, bf16[128,2048]{1,0:T(8,128)(2,1)S(1)}, u32[]{:S(2)}, u32[]{:S(2)}) collective-permute-start(bf16[128,2048]{1,0:T(8,128)(2,1)S(1)} %collective-permute-done.37.refs_4_), channel_id=1, source_target_pairs={{0,16},{16,0},{1,17},{17,1},{2,18},{18,2},{3,19},{19,3},{4,20},{20... | collective-permute-start | bytes 1572872 | tf_op jit(solution)/shard_map/ppermute | solution.py:118
  263.0 32.3 %collective-permute-start.58 = (bf16[256,1024]{1,0:T(8,128)(2,1)S(1)}, bf16[256,1024]{1,0:T(8,128)(2,1)S(1)}, u32[]{:S(2)}, u32[]{:S(2)}) collective-permute-start(bf16[256,1024]{1,0:T(8,128)(2,1)S(1)} %copy-done.53), channel_id=1, source_target_pairs={{16,0},{17,1},{18,2},{19,3},{20,4},{21,5},{22,6},{23,7},{24,8},{25... | collective-permute-start | bytes 1572872 | tf_op jit(solution)/shard_map/ppermute | solution.py:1050
  275.9 19.4 %collective-permute-start.61 = (bf16[128,2048]{1,0:T(8,128)(2,1)S(1)}, bf16[128,2048]{1,0:T(8,128)(2,1)S(1)}, u32[]{:S(2)}, u32[]{:S(2)}) collective-permute-start(bf16[128,2048]{1,0:T(8,128)(2,1)S(1)} %add_convert_fusion.12), channel_id=1, source_target_pairs={{0,4},{4,8},{8,12},{12,0},{1,5},{5,9},{9,13},{13,1},{2,6},{6,10},{... | collective-permute-start | bytes 1572872 | tf_op jit(solution)/shard_map/ppermute | solution.py:229
  276.1 19.2 %collective-permute-start.62 = (bf16[128,2048]{1,0:T(8,128)(2,1)S(1)}, bf16[128,2048]{1,0:T(8,128)(2,1)S(1)}, u32[]{:S(2)}, u32[]{:S(2)}) collective-permute-start(bf16[128,2048]{1,0:T(8,128)(2,1)S(1)} %get-tuple-element.260), channel_id=1, source_target_pairs={{0,16},{16,0},{1,17},{17,1},{2,18},{18,2},{3,19},{19,3},{4,20},{20... | collective-permute-start | bytes 1572872 | tf_op jit(solution)/shard_map/ppermute | solution.py:118
  277.0 18.4 %collective-permute-start.60 = (bf16[256,1024]{1,0:T(8,128)(2,1)S(1)}, bf16[256,1024]{1,0:T(8,128)(2,1)S(1)}, u32[]{:S(2)}, u32[]{:S(2)}) collective-permute-start(bf16[256,1024]{1,0:T(8,128)(2,1)S(1)} %add_convert_fusion.13), channel_id=1, source_target_pairs={{2,0},{3,1},{0,2},{1,3},{6,4},{7,5},{4,6},{5,7},{10,8},{11,9},{8,1... | collective-permute-start | bytes 1572872 | tf_op jit(solution)/shard_map/ppermute | solution.py:66
  295.4 27.9 %collective-permute-start.67 = (bf16[256,1024]{1,0:T(8,128)(2,1)S(1)}, bf16[256,1024]{1,0:T(8,128)(2,1)S(1)}, u32[]{:S(2)}, u32[]{:S(2)}) collective-permute-start(bf16[256,1024]{1,0:T(8,128)(2,1)S(1)} %copy-done.61), channel_id=1, source_target_pairs={{0,1},{1,0},{2,3},{3,2},{4,5},{5,4},{6,7},{7,6},{8,9},{9,8},{10,11... | collective-permute-start | bytes 1572872 | tf_op jit(solution)/shard_map/ppermute | solution.py:59
  346.9 18.1 %collective-permute-start.77 = (bf16[256,1024]{1,0:T(8,128)(2,1)S(1)}, bf16[256,1024]{1,0:T(8,128)(2,1)S(1)}, u32[]{:S(2)}, u32[]{:S(2)}) collective-permute-start(bf16[256,1024]{1,0:T(8,128)(2,1)S(1)} %constant_dynamic-slice_fusion.9), channel_id=1, source_target_pairs={{0,4},{4,8},{8,12},{12,0},{1,5},{5,9},{9,13},{13,1},{2,6},{6,10},{... | collective-permute-start | bytes 1572872 | tf_op jit(solution)/shard_map/ppermute | solution.py:229
  376.1 19.7 %collective-permute-start.78 = (bf16[256,1024]{1,0:T(8,128)(2,1)}, bf16[256,1024]{1,0:T(8,128)(2,1)S(1)}, u32[]{:S(2)}, u32[]{:S(2)}) collective-permute-start(bf16[256,1024]{1,0:T(8,128)(2,1)} %get-tuple-element.298.refs_5_.refs_6_), channel_id=1, source_target_pairs={{0,1},{1,0},{2,3},{3,2},{4,5},{5,4},{6,7},{7,6},{8,9},{9,8},{10,11... | collective-permute-start | bytes 1572872 | tf_op jit(solution)/shard_map/ppermute | solution.py:59
  376.1 38.5 %collective-permute-start.85 = (bf16[128,2048]{1,0:T(8,128)(2,1)}, bf16[128,2048]{1,0:T(8,128)(2,1)}, u32[]{:S(2)}, u32[]{:S(2)}) collective-permute-start(bf16[128,2048]{1,0:T(8,128)(2,1)} %get-tuple-element.307), channel_id=1, source_target_pairs={{0,16},{16,0},{1,17},{17,1},{2,18},{18,2},{3,19},{19,3},{4,20},{20... | collective-permute-start | bytes 1572872 | tf_op jit(solution)/shard_map/ppermute | solution.py:118
  390.6 24.0 %collective-permute-start.83 = (bf16[256,1024]{1,0:T(8,128)(2,1)S(1)}, bf16[256,1024]{1,0:T(8,128)(2,1)S(1)}, u32[]{:S(2)}, u32[]{:S(2)}) collective-permute-start(bf16[256,1024]{1,0:T(8,128)(2,1)S(1)} %add_convert_fusion.6), channel_id=1, source_target_pairs={{0,4},{4,8},{8,12},{12,0},{1,5},{5,9},{9,13},{13,1},{2,6},{6,10},{... | collective-permute-start | bytes 1572872 | tf_op jit(solution)/shard_map/ppermute | solution.py:229
  393.6 24.4 %collective-permute-start.84 = (bf16[128,2048]{1,0:T(8,128)(2,1)S(1)}, bf16[128,2048]{1,0:T(8,128)(2,1)S(1)}, u32[]{:S(2)}, u32[]{:S(2)}) collective-permute-start(bf16[128,2048]{1,0:T(8,128)(2,1)S(1)} %add_convert_fusion.5), channel_id=1, source_target_pairs={{0,4},{4,8},{8,12},{12,0},{1,5},{5,9},{9,13},{13,1},{2,6},{6,10},{... | collective-permute-start | bytes 1572872 | tf_op jit(solution)/shard_map/ppermute | solution.py:229
  421.4 16.4 %collective-permute-start.89 = (bf16[128,2048]{1,0:T(8,128)(2,1)}, bf16[128,2048]{1,0:T(8,128)(2,1)}, u32[]{:S(2)}, u32[]{:S(2)}) collective-permute-start(bf16[128,2048]{1,0:T(8,128)(2,1)} %add_convert_fusion.3), channel_id=1, source_target_pairs={{0,4},{4,8},{8,12},{12,0},{1,5},{5,9},{9,13},{13,1},{2,6},{6,10},{... | collective-permute-start | bytes 1572872 | tf_op jit(solution)/shard_map/ppermute | solution.py:229
  421.4 16.4 %collective-permute-start.90 = (bf16[128,2048]{1,0:T(8,128)(2,1)}, bf16[128,2048]{1,0:T(8,128)(2,1)}, u32[]{:S(2)}, u32[]{:S(2)}) collective-permute-start(bf16[128,2048]{1,0:T(8,128)(2,1)} %get-tuple-element.314), channel_id=1, source_target_pairs={{0,16},{16,0},{1,17},{17,1},{2,18},{18,2},{3,19},{19,3},{4,20},{20... | collective-permute-start | bytes 1572872 | tf_op jit(solution)/shard_map/ppermute | solution.py:118
  444.7 61.2 %collective-permute-start.92 = (bf16[256,1024]{1,0:T(8,128)(2,1)}, bf16[256,1024]{1,0:T(8,128)(2,1)}, u32[]{:S(2)}, u32[]{:S(2)}) collective-permute-start(bf16[256,1024]{1,0:T(8,128)(2,1)} %get-tuple-element.316), channel_id=1, source_target_pairs={{16,0},{17,1},{18,2},{19,3},{20,4},{21,5},{22,6},{23,7},{24,8},{25... | collective-permute-start | bytes 1572872 | tf_op jit(solution)/shard_map/ppermute | solution.py:1103
  452.1 32.1 %collective-permute-start.93 = (bf16[256,1024]{1,0:T(8,128)(2,1)}, bf16[256,1024]{1,0:T(8,128)(2,1)}, u32[]{:S(2)}, u32[]{:S(2)}) collective-permute-start(bf16[256,1024]{1,0:T(8,128)(2,1)} %add_convert_fusion.2), channel_id=1, source_target_pairs={{0,4},{4,8},{8,12},{12,0},{1,5},{5,9},{9,13},{13,1},{2,6},{6,10},{... | collective-permute-start | bytes 1572872 | tf_op jit(solution)/shard_map/ppermute | solution.py:229
  452.1 34.6 %collective-permute-start.91 = (bf16[256,1024]{1,0:T(8,128)(2,1)}, bf16[256,1024]{1,0:T(8,128)(2,1)}, u32[]{:S(2)}, u32[]{:S(2)}) collective-permute-start(bf16[256,1024]{1,0:T(8,128)(2,1)} %get-tuple-element.318), channel_id=1, source_target_pairs={{0,16},{1,17},{2,18},{3,19},{4,20},{5,21},{6,22},{7,23},{8,24},{9,... | collective-permute-start | bytes 1572872 | tf_op jit(solution)/shard_map/ppermute | solution.py:1105
  458.1 20.2 %collective-permute-start.95 = (bf16[128,2048]{1,0:T(8,128)(2,1)S(1)}, bf16[128,2048]{1,0:T(8,128)(2,1)}, u32[]{:S(2)}, u32[]{:S(2)}) collective-permute-start(bf16[128,2048]{1,0:T(8,128)(2,1)S(1)} %add_convert_fusion), channel_id=1, source_target_pairs={{0,4},{4,8},{8,12},{12,0},{1,5},{5,9},{9,13},{13,1},{2,6},{6,10},{... | collective-permute-start | bytes 1572872 | tf_op jit(solution)/shard_map/ppermute | solution.py:229
  458.8 23.4 %collective-permute-start.96 = (bf16[128,2048]{1,0:T(8,128)(2,1)}, bf16[128,2048]{1,0:T(8,128)(2,1)}, u32[]{:S(2)}, u32[]{:S(2)}) collective-permute-start(bf16[128,2048]{1,0:T(8,128)(2,1)} %get-tuple-element.327), channel_id=1, source_target_pairs={{0,16},{16,0},{1,17},{17,1},{2,18},{18,2},{3,19},{19,3},{4,20},{20... | collective-permute-start | bytes 1572872 | tf_op jit(solution)/shard_map/ppermute | solution.py:118
  478.3 32.4 %collective-permute-start.101 = (bf16[256,1024]{1,0:T(8,128)(2,1)S(1)}, bf16[256,1024]{1,0:T(8,128)(2,1)S(1)}, u32[]{:S(2)}, u32[]{:S(2)}) collective-permute-start(bf16[256,1024]{1,0:T(8,128)(2,1)S(1)} %fusion.3), channel_id=1, source_target_pairs={{0,16},{1,17},{2,18},{3,19},{4,20},{5,21},{6,22},{7,23},{8,24},{9,... | collective-permute-start | bytes 1572872 | tf_op jit(solution)/shard_map/ppermute | solution.py:239
  484.2 16.2 %collective-permute-start.99 = (bf16[128,2048]{1,0:T(8,128)(2,1)S(1)}, bf16[128,2048]{1,0:T(8,128)(2,1)S(1)}, u32[]{:S(2)}, u32[]{:S(2)}) collective-permute-start(bf16[128,2048]{1,0:T(8,128)(2,1)S(1)} %get-tuple-element.399), channel_id=1, source_target_pairs={{16,0},{17,1},{18,2},{19,3},{20,4},{21,5},{22,6},{23,7},{24,8},{25... | collective-permute-start | bytes 1572872 | tf_op jit(solution)/shard_map/ppermute | solution.py:239
  486.7 16.2 %collective-permute-start.102 = (bf16[256,1024]{1,0:T(8,128)(2,1)S(1)}, bf16[256,1024]{1,0:T(8,128)(2,1)S(1)}, u32[]{:S(2)}, u32[]{:S(2)}) collective-permute-start(bf16[256,1024]{1,0:T(8,128)(2,1)S(1)} %add_convert_fusion.1), channel_id=1, source_target_pairs={{0,4},{4,8},{8,12},{12,0},{1,5},{5,9},{9,13},{13,1},{2,6},{6,10},{... | collective-permute-start | bytes 1572872 | tf_op jit(solution)/shard_map/ppermute | solution.py:229
  491.6 16.7 %collective-permute-start.94 = (bf16[256,1024]{1,0:T(8,128)(2,1)S(1)}, bf16[256,1024]{1,0:T(8,128)(2,1)S(1)}, u32[]{:S(2)}, u32[]{:S(2)}) collective-permute-start(bf16[256,1024]{1,0:T(8,128)(2,1)S(1)} %copy-done.57), channel_id=1, source_target_pairs={{0,16},{1,17},{2,18},{3,19},{4,20},{5,21},{6,22},{7,23},{8,24},{9,... | collective-permute-start | bytes 1572872 | tf_op jit(solution)/shard_map/ppermute | solution.py:1111
  504.3 16.8 %collective-permute-start.106 = (bf16[256,1024]{1,0:T(8,128)(2,1)}, bf16[256,1024]{1,0:T(8,128)(2,1)}, u32[]{:S(2)}, u32[]{:S(2)}) collective-permute-start(bf16[256,1024]{1,0:T(8,128)(2,1)} %get-tuple-element.392), channel_id=1, source_target_pairs={{16,0},{17,1},{18,2},{19,3},{20,4},{21,5},{22,6},{23,7},{24,8},{25... | collective-permute-start | bytes 1572872 | tf_op jit(solution)/shard_map/ppermute | solution.py:239
  (215 other events, 2132.0 us)
where the time goes:
time: 535 us; the launch traced here: 525 us
  waiting for transfers between devices  192 us (36%)
  Pallas kernels  152 us (28%)
  starting transfers between devices  97.7 us (18%)
  local copies, waits for them, and re-layouts  40.7 us (8%)
  other arithmetic  39.6 us (7%)
    ppermute x17, waiting for transfers between devices, from_chip(): return lax.ppermute(v, 'tensor', pairs)  59.9 us
    pallas_call x6, Pallas kernels, mlp_call(): pl.pallas_call(body, grid=(blocks,), in_specs=in_specs, out_specs=out_spe...  42.6 us
    ppermute x12, waiting for transfers between devices, one(): new.append(lax.ppermute(self.sent, 'dp', pairs))  39 us
    pallas_call x2, Pallas kernels, attention_back(): pl.pallas_call(body, grid=(1,), in_specs=[whole(a.shape) for a in operand...  34.6 us
    unnamed x310, local copies, waits for them, and re-layouts  32.1 us
    ppermute x26, waiting for transfers between devices, swap_section(): return lax.ppermute(v, 'section', [(0, 1), (1, 0)])  30.4 us
    pallas_call x4, Pallas kernels, weight_grads(): pl.pallas_call(body, grid=(dp,), in_specs=specs, out_specs=[pl.BlockSpec(...  27.3 us
    ppermute x26, starting transfers between devices, swap_section(): return lax.ppermute(v, 'section', [(0, 1), (1, 0)])  26.2 us
  transfers between devices with their start and end apart: 107, of which 55 were waited for; matrix products, arithmetic and copies ran while one was open for 9% of the time, Pallas kernels for 25%

commit v1 on v0

--- a/solution.py
+++ b/solution.py
@@ -886,7 +886,7 @@
         grid=(dp,),
         in_specs=specs,
         out_specs=[pl.BlockSpec((step // cut, cols), lambda i: (i, 0))] * cut,
-        out_shape=[sds((model // cut, cols), BF)] * cut,
+        out_shape=[pltpu.HBM((model // cut, cols), BF)] * cut,
         scratch_shapes=[pltpu.VMEM((step, cols), F32)],
         compiler_params=params(14, 1),
         cost_estimate=cost(5),
@@ -1094,21 +1094,25 @@
     terms, g = scatter_tokens(
         sames, others, grad_att(old, dqkv, datt, kept0), lambda gate: beside
     )
-    step_ff0 = sum_ff0.step(terms[1])
     sum_att0 = RingSum((1, 0), g)
     sum_att0.step()
     going = sum_att0.step()
     terms = [late(terms[0]), *terms[1:-1], late(terms[-1])]
     dx0, edge0 = back_first(late(dres0), late(x0), terms, vecs[0])
-    came_dx0 = lax.ppermute(dx0, "section", [(1, 0)])
+    came_dx0 = came_y1 = swap_section(jnp.where(first, y1, dx0))
     second_hop = sum_att0.step(dx0)
-    came_y1 = lax.ppermute(tie(y1, sum_att0.sent), "section", [(0, 1)])
     step_att1 = sum_att1.step(dx0)
     third_hop = sum_att0.step()
     sent = sum_att0.sent
-    last_ff0 = sum_ff0.step()
-    sum_att0.step()
-    came_dx1 = lax.ppermute(tie(dx1, sent), "section", [(0, 1)])
+    third_hop += sum_ff0.step(sent)
+    sum_ff0.step()
+    sum_att0.own = sum_att0.total()
+    low = sum_att0.own.astype(BF)
+    if low.shape == dx1.shape:
+        sum_att0.came = came_dx1 = swap_section(jnp.where(first, dx1, low))
+    else:
+        sum_att0.came = lax.ppermute(low, "section", [(1, 0)])
+        came_dx1 = lax.ppermute(dx1, "section", [(0, 1)])
 
     def both(low, high, came_low, came_high):
         mine = jnp.where(first, low, high)
@@ -1117,7 +1121,7 @@
 
     block_out = both(y0, y1, came_y0, came_y1)
     input_grads = both(dx0, dx1, came_dx0, came_dx1)
-    sum_att0.came = tie(sum_att0.came, block_out, input_grads)
+    sum_att0.came = tie(sum_att0.came, block_out)
 
     def by_unit(qkv_sums, unit_sums):
         q = qkv_sums[:, :width].reshape(heads, 1, size)
@@ -1130,15 +1134,15 @@
     vec = jnp.concatenate(
         [edge0[:2], sums0[:4], edge1[2:4], edge1[:2], sums1[:4], sums_sc_1[:1], sums_fc2_1[:1]]
     )
-    vec = tie(vec, *going, *step_ff0)
+    vec = tie(vec, *going)
     vec = vec + core_swap(vec)
-    vec = tie(sum([from_chip(vec, step) for step in range(1, chips)], vec), *second_hop, came_y1)
-    vec = tie(vec, sent, *last_ff0)
+    vec = tie(sum([from_chip(vec, step) for step in range(1, chips)], vec), *second_hop)
+    vec = tie(vec, sent)
     vec = vec.reshape(2, 8, dp, part).swapaxes(1, 2).reshape(2, dp, 8 * part)
     vec0 = jnp.concatenate([vec[0], unit0], axis=1)
     vec1 = jnp.concatenate([vec[1], unit1], axis=1)
     own = jnp.where(first, vec0, vec1) + swap_section(jnp.where(first, vec1, vec0))
-    own = tie(own, *step_att1, came_dx1, sum_att0.own)
+    own = tie(own, *step_att1, came_y1, *third_hop)
     vec = lax.dynamic_slice_in_dim(own, here, 1, 0)
     for step in range(1, dp):
         pairs = [(i, (i + step) % dp) for i in range(dp)]

time: 535 us -> 527 us (0.985)
  starting transfers between devices: 97.7 us -> 89.2 us
  Pallas kernels: 152 us -> 158 us
  waiting for transfers between devices: 192 us -> 186 us
    ppermute x3 -> x0, starting transfers between devices: 11.7 us -> none  [the longest x1 5.61 us: shards(): came_dx1 = lax.ppermute(tie(dx1, sent), 'section', [(0, 1)])]
    ppermute x17, waiting for transfers between devices: 59.9 us -> 48.8 us  [from_chip(): return lax.ppermute(v, 'tensor', pairs)]
    ppermute x26 -> x28, starting transfers between devices: 26.2 us -> 36.1 us  [swap_section(): return lax.ppermute(v, 'section', [(0, 1), (1, 0)])]
    ppermute x12, waiting for transfers between devices: 39 us -> 45.4 us  [one(): new.append(lax.ppermute(self.sent, 'dp', pairs))]
    unnamed x310 -> x260, local copies, waits for them, and re-layouts: 32.1 us -> 27 us
    ppermute x26 -> x28, waiting for transfers between devices: 30.4 us -> 30.7 us  [swap_section(): return lax.ppermute(v, 'section', [(0, 1), (1, 0)])]
  transfers between devices with their start and end apart: 107 -> 105, of which waited for: 55 -> 53; matrix products, arithmetic and copies ran while one was open for 9% -> 9% of each run, Pallas kernels for 25% -> 27%
where the time goes in v1:
time: 527 us; the launch traced here: 517 us
  waiting for transfers between devices  186 us (35%)
  Pallas kernels  158 us (30%)
  starting transfers between devices  89.2 us (17%)
  other arithmetic  42.4 us (8%)
  local copies, waits for them, and re-layouts  39.1 us (7%)
    ppermute x17, waiting for transfers between devices, from_chip(): return lax.ppermute(v, 'tensor', pairs)  48.8 us
    ppermute x12, waiting for transfers between devices, one(): new.append(lax.ppermute(self.sent, 'dp', pairs))  45.4 us
    pallas_call x6, Pallas kernels, mlp_call(): pl.pallas_call(body, grid=(blocks,), in_specs=in_specs, out_specs=out_spe...  42.3 us
    ppermute x28, starting transfers between devices, swap_section(): return lax.ppermute(v, 'section', [(0, 1), (1, 0)])  36.1 us
    pallas_call x2, Pallas kernels, attention_back(): pl.pallas_call(body, grid=(1,), in_specs=[whole(a.shape) for a in operand...  34.8 us
    pallas_call x4, Pallas kernels, weight_grads(): pl.pallas_call(body, grid=(dp,), in_specs=specs, out_specs=[pl.BlockSpec(...  31 us
    ppermute x28, waiting for transfers between devices, swap_section(): return lax.ppermute(v, 'section', [(0, 1), (1, 0)])  30.7 us
    unnamed x260, local copies, waits for them, and re-layouts  27 us
  transfers between devices with their start and end apart: 105, of which 53 were waited for; matrix products, arithmetic and copies ran while one was open for 9% of the time, Pallas kernels for 27%

profile of v1, /device:TPU:0, one launch (start us, length us, event | category | flops | bytes accessed | tf_op | source)
XLA Modules:
  0.0 516.9 jit_solution(13429855413725137632)
XLA Ops:
  29.6 9.8 %collective-permute-done.6.refs_2_ = bf16[144,1024]{1,0:T(8,128)(2,1)} collective-permute-done((bf16[144,1024]{1,0:T(8,128)(2,1)}, bf16[144,1024]{1,0:T(8,128)(2,1)}, u32[]{:S(2)}, u32[]{:S(2)}) %collective-permute-start.6) | collective-permute-done | bytes 294944 | tf_op jit(solution)/shard_map/ppermute | solution.py:165
  61.9 4.5 collective-permute-done.11.a_ref.refs_2_
  76.0 9.5 %attention.2 = (bf16[512,256]{1,0:T(8,128)(2,1)}, bf16[512,256]{1,0:T(8,128)(2,1)}, f32[4,1024]{1,0:T(4,128)S(1)}, bf16[256,1024]{1,0:T(8,128)(2,1)S(1)}, bf16[2...) custom-call(bf16[512,768]{1,0:T(8,128)(2,1)S(1)} %project_qkv.4.refs_0_, bf16[512,768]{1,0:T(8,128)(2,1)S(1)} %project_qkv.5.refs_1_, ...), custom_call_target="tpu_custom_call" | custom-call | flops 10350000128 | tf_op jit(solution)/shard_map/attention/pallas_call | solution.py:522
  94.1 9.4 %collective-permute-done.18.refs_2_ = bf16[256,1024]{1,0:T(8,128)(2,1)S(1)} collective-permute-done((bf16[256,1024]{1,0:T(8,128)(2,1)S(1)}, bf16[256,1024]{1,0:T(8,128)(2,1)S(1)}, u32[]{:S(2)}, u32[]{:S(2)}) %collective-permute-start.18) | collective-permute-done | bytes 524320 | tf_op jit(solution)/shard_map/ppermute | solution.py:66
  110.8 9.1 %collective-permute-done.24.refs_2_ = bf16[128,1024]{1,0:T(8,128)(2,1)S(1)} collective-permute-done((bf16[128,1024]{1,0:T(8,128)(2,1)S(1)}, bf16[128,1024]{1,0:T(8,128)(2,1)S(1)}, u32[]{:S(2)}, u32[]{:S(2)}) %collective-permute-start.24) | collective-permute-done | bytes 262176 | tf_op jit(solution)/shard_map/ppermute | solution.py:184
  123.6 6.6 %mlp_forward.2 = (bf16[512,1024]{1,0:T(8,128)(2,1)}, bf16[512,1024]{1,0:T(8,128)(2,1)}, f32[1,1024]{1,0:T(1,128)}, bf16[256,1024]{1,0:T(8,128)(2,1)S(1)}, bf16[256,1024]{1,0:T(8,128)(2,1)S(1)}) custom-call(bf16[256,1024]{1,0:T(8,128)(2,1)S(1)} %get-tuple-element.192.a.refs_0_, bf16[256,1024]{1,0:T(8,128)(2,1)S(1)} %collective-permute-done.21.b.refs_1_, ...), custom_call_target="tpu_custom_call" | custom-call | flops 575000000 | tf_op jit(solution)/shard_map/mlp_forward/pallas_call | solution.py:726
  132.2 6.5 %mlp_forward.3 = (bf16[512,1024]{1,0:T(8,128)(2,1)}, bf16[512,1024]{1,0:T(8,128)(2,1)}, f32[1,1024]{1,0:T(1,128)}, bf16[256,1024]{1,0:T(8,128)(2,1)S(1)}, bf16[256,1024]{1,0:T(8,128)(2,1)S(1)}) custom-call(bf16[256,1024]{1,0:T(8,128)(2,1)S(1)} %collective-permute-done.23.a.refs_2_, bf16[256,1024]{1,0:T(8,128)(2,1)S(1)} %collective-permute-done.26.b.refs_3_, ...), custom_call_target="tpu_custom_call" | custom-call | flops 575000000 | tf_op jit(solution)/shard_map/mlp_forward/pallas_call | solution.py:726
  146.3 7.1 %collective-permute-done.33.refs_5_ = bf16[128,1024]{1,0:T(8,128)(2,1)S(1)} collective-permute-done((bf16[128,1024]{1,0:T(8,128)(2,1)S(1)}, bf16[128,1024]{1,0:T(8,128)(2,1)S(1)}, u32[]{:S(2)}, u32[]{:S(2)}) %collective-permute-start.33) | collective-permute-done | bytes 262176 | tf_op jit(solution)/shard_map/ppermute | solution.py:118
  153.4 5.2 %collective-permute-done.34.refs_7_ = bf16[128,1024]{1,0:T(8,128)(2,1)S(1)} collective-permute-done((bf16[128,1024]{1,0:T(8,128)(2,1)S(1)}, bf16[128,1024]{1,0:T(8,128)(2,1)S(1)}, u32[]{:S(2)}, u32[]{:S(2)}) %collective-permute-start.34) | collective-permute-done | bytes 262176 | tf_op jit(solution)/shard_map/ppermute | solution.py:118
  170.5 6.3 %collective-permute-done.36.a_ref.refs_2_ = bf16[256,1024]{1,0:T(8,128)(2,1)} collective-permute-done((bf16[256,1024]{1,0:T(8,128)(2,1)}, bf16[256,1024]{1,0:T(8,128)(2,1)}, u32[]{:S(2)}, u32[]{:S(2)}) %collective-permute-start.36) | collective-permute-done | bytes 524320 | tf_op jit(solution)/shard_map/ppermute | solution.py:66
  184.3 9.9 %attention.3 = (bf16[512,256]{1,0:T(8,128)(2,1)}, bf16[512,256]{1,0:T(8,128)(2,1)}, f32[4,1024]{1,0:T(4,128)S(1)}, bf16[256,1024]{1,0:T(8,128)(2,1)S(1)}, bf16[2...) custom-call(bf16[512,768]{1,0:T(8,128)(2,1)S(1)} %project_qkv.6.refs_0_, bf16[512,768]{1,0:T(8,128)(2,1)S(1)} %project_qkv.7.refs_1_, ...), custom_call_target="tpu_custom_call" | custom-call | flops 10350000128 | tf_op jit(solution)/shard_map/attention/pallas_call | solution.py:522
  200.6 12.4 %collective-permute-done.44.refs_2_ = bf16[256,1024]{1,0:T(8,128)(2,1)S(1)} collective-permute-done((bf16[256,1024]{1,0:T(8,128)(2,1)S(1)}, bf16[256,1024]{1,0:T(8,128)(2,1)S(1)}, u32[]{:S(2)}, u32[]{:S(2)}) %collective-permute-start.44) | collective-permute-done | bytes 524320 | tf_op jit(solution)/shard_map/ppermute | solution.py:66
  218.5 8.9 %mlp_both.2 = (bf16[512,1024]{1,0:T(8,128)(2,1)}, bf16[512,1024]{1,0:T(8,128)(2,1)}, f32[1,1024]{1,0:T(1,128)S(1)}, bf16[256,1024]{1,0:T(8,128)(2,1)S(1)}, bf16[...) custom-call(bf16[256,1024]{1,0:T(8,128)(2,1)S(1)} %get-tuple-element.225.a.refs_0_, ...), custom_call_target="tpu_custom_call" | custom-call | flops 575000000 | tf_op jit(solution)/shard_map/mlp_both/pallas_call | solution.py:726
  231.7 9.0 %mlp_both.3 = (bf16[512,1024]{1,0:T(8,128)(2,1)}, bf16[512,1024]{1,0:T(8,128)(2,1)}, f32[1,1024]{1,0:T(1,128)S(1)}, bf16[256,1024]{1,0:T(8,128)(2,1)S(1)}, bf16[...) custom-call(bf16[256,1024]{1,0:T(8,128)(2,1)S(1)} %collective-permute-done.49.a.refs_2_, ...), custom_call_target="tpu_custom_call" | custom-call | flops 575000000 | tf_op jit(solution)/shard_map/mlp_both/pallas_call | solution.py:726
  248.1 9.3 %grad_ff.2 = (bf16[512,2048]{1,0:T(8,128)(2,1)}, bf16[512,2048]{1,0:T(8,128)(2,1)}) custom-call(s32[1]{0:T(128)} %bitcast.15.side_ref, bf16[256,1024]{1,0:T(8,128)(2,1)S(1)} %get-tuple-element.225.a.refs_0_, bf16[256,1024]{1,0:T(8,128)(2,1)S(1)} %collective-permute-done.48.b.refs_1_, bf16[256,1024]{1,0:T(8,128)(2,1)S(1)} %collective-permute-done.49.a.refs_2_, ...), custom_call_target="tpu_custom_call" | custom-call | flops 5750000128 | tf_op jit(solution)/shard_map/grad_ff/pallas_call | solution.py:884
  264.3 9.7 %collective-permute-done.56 = bf16[128,2048]{1,0:T(8,128)(2,1)S(1)} collective-permute-done((bf16[128,2048]{1,0:T(8,128)(2,1)S(1)}, bf16[128,2048]{1,0:T(8,128)(2,1)S(1)}, u32[]{:S(2)}, u32[]{:S(2)}) %collective-permute-start.56) | collective-permute-done | bytes 524320 | tf_op jit(solution)/shard_map/ppermute | solution.py:118
  278.6 17.3 %attention_back.2 = (bf16[512,768]{1,0:T(8,128)(2,1)}, bf16[512,768]{1,0:T(8,128)(2,1)}, bf16[256,1024]{1,0:T(8,128)(2,1)}, bf16[256,1024]{1,0:T(8,128)(2,1)}, b...) custom-call(bf16[512,768]{1,0:T(8,128)(2,1)} %copy-done.8, bf16[512,768]{1,0:T(8,128)(2,1)} %copy-done.9, ...), custom_call_target="tpu_custom_call" | custom-call | flops 17250000896 | tf_op jit(solution)/shard_map/attention_back/pallas_call | solution.py:664
  304.3 6.3 %grad_att.2 = bf16[1024,1024]{1,0:T(8,128)(2,1)} custom-call(s32[1]{0:T(128)} %bitcast.15.side_ref, bf16[256,1024]{1,0:T(8,128)(2,1)} %get-tuple-element.210.a_ref.refs_0_, bf16[256,1024]{1,0:T(8,128)(2,1)} %copy-done.20, bf16[256,1024]{1,0:T(8,128)(2,1)} %collective-permute-done.36.a_ref.refs_2_, bf16[256,1024]{1,0:T(8,128)(2,1)} %copy-done.22, ...), custom_call_target="tpu_custom_call" | custom-call | flops 5750000128 | tf_op jit(solution)/shard_map/grad_att/pallas_call | solution.py:884
  310.6 4.1 collective-permute-done.64.refs_3_
  325.9 5.6 %mlp_backward.2 = (bf16[512,1024]{1,0:T(8,128)(2,1)}, f32[1,1024]{1,0:T(1,128)S(1)}, bf16[256,1024]{1,0:T(8,128)(2,1)S(1)}, bf16[256,1024]{1,0:T(8,128)(2,1)S(1)}) custom-call(bf16[256,1024]{1,0:T(8,128)(2,1)S(1)} %get-tuple-element.267.a.refs_6_, bf16[256,1024]{1,0:T(8,128)(2,1)S(1)} %collective-permute-done.68.b.refs_7_, ...), custom_call_target="tpu_custom_call" | custom-call | flops 575000000 | tf_op jit(solution)/shard_map/mlp_backward/pallas_call | solution.py:726
  339.4 5.7 %mlp_backward.3 = (bf16[512,1024]{1,0:T(8,128)(2,1)}, f32[1,1024]{1,0:T(1,128)S(1)}, bf16[256,1024]{1,0:T(8,128)(2,1)S(1)}, bf16[256,1024]{1,0:T(8,128)(2,1)}) custom-call(bf16[256,1024]{1,0:T(8,128)(2,1)S(1)} %collective-permute-done.69.a.refs_8_, bf16[256,1024]{1,0:T(8,128)(2,1)S(1)} %collective-permute-done.72.b.refs_9_, ...), custom_call_target="tpu_custom_call" | custom-call | flops 575000000 | tf_op jit(solution)/shard_map/mlp_backward/pallas_call | solution.py:726
  354.4 9.2 %grad_ff.3 = (bf16[512,2048]{1,0:T(8,128)(2,1)}, bf16[512,2048]{1,0:T(8,128)(2,1)}) custom-call(s32[1]{0:T(128)} %bitcast.15.side_ref, bf16[256,1024]{1,0:T(8,128)(2,1)} %copy-done.16, bf16[256,1024]{1,0:T(8,128)(2,1)} %copy-done.17, bf16[256,1024]{1,0:T(8,128)(2,1)} %copy-done.18, bf16[256,1024]{1,0:T(8,128)(2,1)} %copy-done.19, ...), custom_call_target="tpu_custom_call" | custom-call | flops 5750000128 | tf_op jit(solution)/shard_map/grad_ff/pallas_call | solution.py:884
  375.9 8.4 %collective-permute-done.79.refs_7_.refs_8_ = bf16[256,1024]{1,0:T(8,128)(2,1)S(1)} collective-permute-done((bf16[256,1024]{1,0:T(8,128)(2,1)S(1)}, bf16[256,1024]{1,0:T(8,128)(2,1)S(1)}, u32[]{:S(2)}, u32[]{:S(2)}) %collective-permute-start.79) | collective-permute-done | bytes 524320 | tf_op jit(solution)/shard_map/ppermute | solution.py:66
  384.3 4.9 collective-permute-done.80
  395.3 17.6 %attention_back.3 = (bf16[512,768]{1,0:T(8,128)(2,1)}, bf16[512,768]{1,0:T(8,128)(2,1)}, bf16[256,1024]{1,0:T(8,128)(2,1)}, bf16[256,1024]{1,0:T(8,128)(2,1)}, b...) custom-call(bf16[512,768]{1,0:T(8,128)(2,1)} %copy-done.6, bf16[512,768]{1,0:T(8,128)(2,1)} %copy-done.7, ...), custom_call_target="tpu_custom_call" | custom-call | flops 17250000896 | tf_op jit(solution)/shard_map/attention_back/pallas_call | solution.py:664
  412.9 4.9 collective-permute-done.84
  425.2 6.3 %grad_att.3 = bf16[1024,1024]{1,0:T(8,128)(2,1)} custom-call(s32[1]{0:T(128)} %bitcast.15.side_ref, bf16[256,1024]{1,0:T(8,128)(2,1)} %copy-done.12, bf16[256,1024]{1,0:T(8,128)(2,1)} %copy-done.13, bf16[256,1024]{1,0:T(8,128)(2,1)} %collective-permute-done.11.a_ref.refs_2_, bf16[256,1024]{1,0:T(8,128)(2,1)} %copy-done.15, ...), custom_call_target="tpu_custom_call" | custom-call | flops 5750000128 | tf_op jit(solution)/shard_map/grad_att/pallas_call | solution.py:884
  443.1 5.8 %collective-permute-done.91 = bf16[256,1024]{1,0:T(8,128)(2,1)} collective-permute-done((bf16[256,1024]{1,0:T(8,128)(2,1)S(1)}, bf16[256,1024]{1,0:T(8,128)(2,1)}, u32[]{:S(2)}, u32[]{:S(2)}) %collective-permute-start.91) | collective-permute-done | bytes 524320 | tf_op jit(solution)/shard_map/ppermute | solution.py:229
  454.3 3.9 collective-permute-start.98
  458.2 7.2 %collective-permute-done.92 = bf16[256,1024]{1,0:T(8,128)(2,1)} collective-permute-done((bf16[256,1024]{1,0:T(8,128)(2,1)S(1)}, bf16[256,1024]{1,0:T(8,128)(2,1)}, u32[]{:S(2)}, u32[]{:S(2)}) %collective-permute-start.92) | collective-permute-done | bytes 524320 | tf_op jit(solution)/shard_map/ppermute | solution.py:229
  473.3 10.2 %collective-permute-done.93 = bf16[256,1024]{1,0:T(8,128)(2,1)S(1)} collective-permute-done((bf16[256,1024]{1,0:T(8,128)(2,1)S(1)}, bf16[256,1024]{1,0:T(8,128)(2,1)S(1)}, u32[]{:S(2)}, u32[]{:S(2)}) %collective-permute-start.93) | collective-permute-done | bytes 524320 | tf_op jit(solution)/shard_map/ppermute | solution.py:229
  504.2 5.2 %collective-permute-done.104 = bf16[128,2048]{1,0:T(8,128)(2,1)} collective-permute-done((bf16[128,2048]{1,0:T(8,128)(2,1)}, bf16[128,2048]{1,0:T(8,128)(2,1)}, u32[]{:S(2)}, u32[]{:S(2)}) %collective-permute-start.104) | collective-permute-done | bytes 524320 | tf_op jit(solution)/shard_map/ppermute | solution.py:239
  (583 shorter events, 258.4 us)
Async XLA Ops:
  20.2 24.3 %collective-permute-start.4 = (bf16[144,1024]{1,0:T(8,128)(2,1)}, bf16[144,1024]{1,0:T(8,128)(2,1)}, u32[]{:S(2)}, u32[]{:S(2)}) collective-permute-start(bf16[144,1024]{1,0:T(8,128)(2,1)} %pad_maximum_fusion.1.refs_0_), channel_id=1, source_target_pairs={{0,8},{4,12},{8,0},{12,4},{1,9},{5,13},{9,1},{13,5},{2,10},{6,14},... | collective-permute-start | bytes 884744 | tf_op jit(solution)/shard_map/ppermute | solution.py:165
  20.3 19.1 %collective-permute-start.6 = (bf16[144,1024]{1,0:T(8,128)(2,1)}, bf16[144,1024]{1,0:T(8,128)(2,1)}, u32[]{:S(2)}, u32[]{:S(2)}) collective-permute-start(bf16[144,1024]{1,0:T(8,128)(2,1)} %pad_maximum_fusion.1.refs_0_), channel_id=1, source_target_pairs={{0,4},{4,8},{8,12},{12,0},{1,5},{5,9},{9,13},{13,1},{2,6},{6,10},{... | collective-permute-start | bytes 884744 | tf_op jit(solution)/shard_map/ppermute | solution.py:165
  21.3 24.8 %collective-permute-start.2 = (bf16[128,2048]{1,0:T(8,128)(2,1)S(1)}, bf16[128,2048]{1,0:T(8,128)(2,1)S(1)}, u32[]{:S(2)}, u32[]{:S(2)}) collective-permute-start(bf16[128,2048]{1,0:T(8,128)(2,1)S(1)} %fusion.9), channel_id=1, source_target_pairs={{0,16},{16,0},{1,17},{17,1},{2,18},{18,2},{3,19},{19,3},{4,20},{20... | collective-permute-start | bytes 1572872 | tf_op jit(solution)/shard_map/ppermute | solution.py:118
  28.1 19.8 %collective-permute-start.5 = (bf16[144,1024]{1,0:T(8,128)(2,1)S(1)}, bf16[144,1024]{1,0:T(8,128)(2,1)S(1)}, u32[]{:S(2)}, u32[]{:S(2)}) collective-permute-start(bf16[144,1024]{1,0:T(8,128)(2,1)S(1)} %collective-permute-done.3.refs_6_), channel_id=1, source_target_pairs={{0,16},{16,0},{1,17},{17,1},{2,18},{18,2},{3,19},{19,3},{4,20},{20... | collective-permute-start | bytes 884744 | tf_op jit(solution)/shard_map/ppermute | solution.py:118
  54.3 15.9 %collective-permute-start.13 = (bf16[128,2048]{1,0:T(8,128)(2,1)}, bf16[128,2048]{1,0:T(8,128)(2,1)}, u32[]{:S(2)}, u32[]{:S(2)}) collective-permute-start(bf16[128,2048]{1,0:T(8,128)(2,1)} %broadcast_select_fusion.3.refs_0_), channel_id=1, source_target_pairs={{0,4},{4,8},{8,12},{12,0},{1,5},{5,9},{9,13},{13,1},{2,6},{6,10},{... | collective-permute-start | bytes 1572872 | tf_op jit(solution)/shard_map/ppermute | solution.py:184
  70.2 16.3 %collective-permute-start.15 = (bf16[128,2048]{1,0:T(8,128)(2,1)}, bf16[128,2048]{1,0:T(8,128)(2,1)S(1)}, u32[]{:S(2)}, u32[]{:S(2)}) collective-permute-start(bf16[128,2048]{1,0:T(8,128)(2,1)} %collective-permute-done.13.refs_2_), channel_id=1, source_target_pairs={{0,4},{4,8},{8,12},{12,0},{1,5},{5,9},{9,13},{13,1},{2,6},{6,10},{... | collective-permute-start | bytes 1572872 | tf_op jit(solution)/shard_map/ppermute | solution.py:184
  108.4 21.8 %collective-permute-start.23 = (bf16[256,1024]{1,0:T(8,128)(2,1)S(1)}, bf16[256,1024]{1,0:T(8,128)(2,1)S(1)}, u32[]{:S(2)}, u32[]{:S(2)}) collective-permute-start(bf16[256,1024]{1,0:T(8,128)(2,1)S(1)} %get-tuple-element.192.a.refs_0_), channel_id=1, source_target_pairs={{2,0},{3,1},{0,2},{1,3},{6,4},{7,5},{4,6},{5,7},{10,8},{11,9},{8,1... | collective-permute-start | bytes 1572872 | tf_op jit(solution)/shard_map/ppermute | solution.py:66
  144.2 16.2 %collective-permute-start.32 = (bf16[128,2048]{1,0:T(8,128)(2,1)S(1)}, bf16[128,2048]{1,0:T(8,128)(2,1)}, u32[]{:S(2)}, u32[]{:S(2)}) collective-permute-start(bf16[128,2048]{1,0:T(8,128)(2,1)S(1)} %copy-done.74), channel_id=1, source_target_pairs={{0,4},{4,8},{8,12},{12,0},{1,5},{5,9},{9,13},{13,1},{2,6},{6,10},{... | collective-permute-start | bytes 1572872 | tf_op jit(solution)/shard_map/ppermute | solution.py:184
  163.3 16.1 %collective-permute-start.37 = (bf16[128,2048]{1,0:T(8,128)(2,1)}, bf16[128,2048]{1,0:T(8,128)(2,1)}, u32[]{:S(2)}, u32[]{:S(2)}) collective-permute-start(bf16[128,2048]{1,0:T(8,128)(2,1)} %collective-permute-done.32.refs_2_), channel_id=1, source_target_pairs={{0,4},{4,8},{8,12},{12,0},{1,5},{5,9},{9,13},{13,1},{2,6},{6,10},{... | collective-permute-start | bytes 1572872 | tf_op jit(solution)/shard_map/ppermute | solution.py:184
  179.7 16.4 %collective-permute-start.41 = (bf16[128,2048]{1,0:T(8,128)(2,1)}, bf16[128,2048]{1,0:T(8,128)(2,1)S(1)}, u32[]{:S(2)}, u32[]{:S(2)}) collective-permute-start(bf16[128,2048]{1,0:T(8,128)(2,1)} %collective-permute-done.37.refs_4_), channel_id=1, source_target_pairs={{0,4},{4,8},{8,12},{12,0},{1,5},{5,9},{9,13},{13,1},{2,6},{6,10},{... | collective-permute-start | bytes 1572872 | tf_op jit(solution)/shard_map/ppermute | solution.py:184
  179.7 16.3 %collective-permute-start.42 = (bf16[128,2048]{1,0:T(8,128)(2,1)}, bf16[128,2048]{1,0:T(8,128)(2,1)S(1)}, u32[]{:S(2)}, u32[]{:S(2)}) collective-permute-start(bf16[128,2048]{1,0:T(8,128)(2,1)} %collective-permute-done.37.refs_4_), channel_id=1, source_target_pairs={{0,16},{16,0},{1,17},{17,1},{2,18},{18,2},{3,19},{19,3},{4,20},{20... | collective-permute-start | bytes 1572872 | tf_op jit(solution)/shard_map/ppermute | solution.py:118
  263.0 32.9 %collective-permute-start.58 = (bf16[256,1024]{1,0:T(8,128)(2,1)S(1)}, bf16[256,1024]{1,0:T(8,128)(2,1)S(1)}, u32[]{:S(2)}, u32[]{:S(2)}) collective-permute-start(bf16[256,1024]{1,0:T(8,128)(2,1)S(1)} %get-tuple-element.252.refs_0_.refs_1_), channel_id=1, source_target_pairs={{16,0},{17,1},{18,2},{19,3},{20,4},{21,5},{22,6},{23,7},{24,8},{25... | collective-permute-start | bytes 1572872 | tf_op jit(solution)/shard_map/ppermute | solution.py:1050
  275.5 20.4 %collective-permute-start.61 = (bf16[128,2048]{1,0:T(8,128)(2,1)S(1)}, bf16[128,2048]{1,0:T(8,128)(2,1)S(1)}, u32[]{:S(2)}, u32[]{:S(2)}) collective-permute-start(bf16[128,2048]{1,0:T(8,128)(2,1)S(1)} %add_convert_fusion.12), channel_id=1, source_target_pairs={{0,4},{4,8},{8,12},{12,0},{1,5},{5,9},{9,13},{13,1},{2,6},{6,10},{... | collective-permute-start | bytes 1572872 | tf_op jit(solution)/shard_map/ppermute | solution.py:229
  275.7 20.3 %collective-permute-start.62 = (bf16[128,2048]{1,0:T(8,128)(2,1)S(1)}, bf16[128,2048]{1,0:T(8,128)(2,1)S(1)}, u32[]{:S(2)}, u32[]{:S(2)}) collective-permute-start(bf16[128,2048]{1,0:T(8,128)(2,1)S(1)} %get-tuple-element.258), channel_id=1, source_target_pairs={{0,16},{16,0},{1,17},{17,1},{2,18},{18,2},{3,19},{19,3},{4,20},{20... | collective-permute-start | bytes 1572872 | tf_op jit(solution)/shard_map/ppermute | solution.py:118
  277.5 18.6 %collective-permute-start.60 = (bf16[256,1024]{1,0:T(8,128)(2,1)S(1)}, bf16[256,1024]{1,0:T(8,128)(2,1)S(1)}, u32[]{:S(2)}, u32[]{:S(2)}) collective-permute-start(bf16[256,1024]{1,0:T(8,128)(2,1)S(1)} %add_convert_fusion.13), channel_id=1, source_target_pairs={{2,0},{3,1},{0,2},{1,3},{6,4},{7,5},{4,6},{5,7},{10,8},{11,9},{8,1... | collective-permute-start | bytes 1572872 | tf_op jit(solution)/shard_map/ppermute | solution.py:66
  296.7 27.0 %collective-permute-start.67 = (bf16[256,1024]{1,0:T(8,128)(2,1)S(1)}, bf16[256,1024]{1,0:T(8,128)(2,1)S(1)}, u32[]{:S(2)}, u32[]{:S(2)}) collective-permute-start(bf16[256,1024]{1,0:T(8,128)(2,1)S(1)} %copy-done.35), channel_id=1, source_target_pairs={{0,1},{1,0},{2,3},{3,2},{4,5},{5,4},{6,7},{7,6},{8,9},{9,8},{10,11... | collective-permute-start | bytes 1572872 | tf_op jit(solution)/shard_map/ppermute | solution.py:59
  321.6 15.8 %collective-permute-start.70 = (bf16[128,2048]{1,0:T(8,128)(2,1)S(1)}, bf16[128,2048]{1,0:T(8,128)(2,1)S(1)}, u32[]{:S(2)}, u32[]{:S(2)}) collective-permute-start(bf16[128,2048]{1,0:T(8,128)(2,1)S(1)} %add_convert_fusion.9), channel_id=1, source_target_pairs={{0,4},{4,8},{8,12},{12,0},{1,5},{5,9},{9,13},{13,1},{2,6},{6,10},{... | collective-permute-start | bytes 1572872 | tf_op jit(solution)/shard_map/ppermute | solution.py:229
  347.3 19.3 %collective-permute-start.77 = (bf16[256,1024]{1,0:T(8,128)(2,1)S(1)}, bf16[256,1024]{1,0:T(8,128)(2,1)S(1)}, u32[]{:S(2)}, u32[]{:S(2)}) collective-permute-start(bf16[256,1024]{1,0:T(8,128)(2,1)S(1)} %constant_dynamic-slice_fusion.9), channel_id=1, source_target_pairs={{0,4},{4,8},{8,12},{12,0},{1,5},{5,9},{9,13},{13,1},{2,6},{6,10},{... | collective-permute-start | bytes 1572872 | tf_op jit(solution)/shard_map/ppermute | solution.py:229
  349.6 17.0 %collective-permute-start.74 = (bf16[256,1024]{1,0:T(8,128)(2,1)S(1)}, bf16[256,1024]{1,0:T(8,128)(2,1)S(1)}, u32[]{:S(2)}, u32[]{:S(2)}) collective-permute-start(bf16[256,1024]{1,0:T(8,128)(2,1)S(1)} %add_convert_fusion.8), channel_id=1, source_target_pairs={{2,0},{3,1},{0,2},{1,3},{6,4},{7,5},{4,6},{5,7},{10,8},{11,9},{8,1... | collective-permute-start | bytes 1572872 | tf_op jit(solution)/shard_map/ppermute | solution.py:66
  350.6 16.0 %collective-permute-start.75 = (bf16[256,1024]{1,0:T(8,128)(2,1)S(1)}, bf16[256,1024]{1,0:T(8,128)(2,1)S(1)}, u32[]{:S(2)}, u32[]{:S(2)}) collective-permute-start(bf16[256,1024]{1,0:T(8,128)(2,1)S(1)} %copy-done.48), channel_id=1, source_target_pairs={{0,1},{1,0},{2,3},{3,2},{4,5},{5,4},{6,7},{7,6},{8,9},{9,8},{10,11... | collective-permute-start | bytes 1572872 | tf_op jit(solution)/shard_map/ppermute | solution.py:59
  375.9 19.4 %collective-permute-start.78 = (bf16[256,1024]{1,0:T(8,128)(2,1)S(1)}, bf16[256,1024]{1,0:T(8,128)(2,1)S(1)}, u32[]{:S(2)}, u32[]{:S(2)}) collective-permute-start(bf16[256,1024]{1,0:T(8,128)(2,1)S(1)} %get-tuple-element.297.refs_5_.refs_6_), channel_id=1, source_target_pairs={{0,1},{1,0},{2,3},{3,2},{4,5},{5,4},{6,7},{7,6},{8,9},{9,8},{10,11... | collective-permute-start | bytes 1572872 | tf_op jit(solution)/shard_map/ppermute | solution.py:59
  375.9 37.0 %collective-permute-start.85 = (bf16[128,2048]{1,0:T(8,128)(2,1)}, bf16[128,2048]{1,0:T(8,128)(2,1)S(1)}, u32[]{:S(2)}, u32[]{:S(2)}) collective-permute-start(bf16[128,2048]{1,0:T(8,128)(2,1)} %get-tuple-element.306), channel_id=1, source_target_pairs={{0,16},{16,0},{1,17},{17,1},{2,18},{18,2},{3,19},{19,3},{4,20},{20... | collective-permute-start | bytes 1572872 | tf_op jit(solution)/shard_map/ppermute | solution.py:118
  390.4 22.6 %collective-permute-start.83 = (bf16[256,1024]{1,0:T(8,128)(2,1)S(1)}, bf16[256,1024]{1,0:T(8,128)(2,1)S(1)}, u32[]{:S(2)}, u32[]{:S(2)}) collective-permute-start(bf16[256,1024]{1,0:T(8,128)(2,1)S(1)} %add_convert_fusion.6), channel_id=1, source_target_pairs={{0,4},{4,8},{8,12},{12,0},{1,5},{5,9},{9,13},{13,1},{2,6},{6,10},{... | collective-permute-start | bytes 1572872 | tf_op jit(solution)/shard_map/ppermute | solution.py:229
  393.1 24.7 %collective-permute-start.84 = (bf16[128,2048]{1,0:T(8,128)(2,1)S(1)}, bf16[128,2048]{1,0:T(8,128)(2,1)S(1)}, u32[]{:S(2)}, u32[]{:S(2)}) collective-permute-start(bf16[128,2048]{1,0:T(8,128)(2,1)S(1)} %add_convert_fusion.5), channel_id=1, source_target_pairs={{0,4},{4,8},{8,12},{12,0},{1,5},{5,9},{9,13},{13,1},{2,6},{6,10},{... | collective-permute-start | bytes 1572872 | tf_op jit(solution)/shard_map/ppermute | solution.py:229
  421.2 16.7 %collective-permute-start.88 = (bf16[128,2048]{1,0:T(8,128)(2,1)}, bf16[128,2048]{1,0:T(8,128)(2,1)}, u32[]{:S(2)}, u32[]{:S(2)}) collective-permute-start(bf16[128,2048]{1,0:T(8,128)(2,1)} %add_convert_fusion.3), channel_id=1, source_target_pairs={{0,4},{4,8},{8,12},{12,0},{1,5},{5,9},{9,13},{13,1},{2,6},{6,10},{... | collective-permute-start | bytes 1572872 | tf_op jit(solution)/shard_map/ppermute | solution.py:229
  421.2 16.7 %collective-permute-start.89 = (bf16[128,2048]{1,0:T(8,128)(2,1)}, bf16[128,2048]{1,0:T(8,128)(2,1)}, u32[]{:S(2)}, u32[]{:S(2)}) collective-permute-start(bf16[128,2048]{1,0:T(8,128)(2,1)} %get-tuple-element.312), channel_id=1, source_target_pairs={{0,16},{16,0},{1,17},{17,1},{2,18},{18,2},{3,19},{19,3},{4,20},{20... | collective-permute-start | bytes 1572872 | tf_op jit(solution)/shard_map/ppermute | solution.py:118
  432.6 16.3 %collective-permute-start.91 = (bf16[256,1024]{1,0:T(8,128)(2,1)S(1)}, bf16[256,1024]{1,0:T(8,128)(2,1)}, u32[]{:S(2)}, u32[]{:S(2)}) collective-permute-start(bf16[256,1024]{1,0:T(8,128)(2,1)S(1)} %constant_dynamic-slice_fusion.5), channel_id=1, source_target_pairs={{0,4},{4,8},{8,12},{12,0},{1,5},{5,9},{9,13},{13,1},{2,6},{6,10},{... | collective-permute-start | bytes 1572872 | tf_op jit(solution)/shard_map/ppermute | solution.py:229
  441.6 47.0 %collective-permute-start.90 = (bf16[256,1024]{1,0:T(8,128)(2,1)}, bf16[256,1024]{1,0:T(8,128)(2,1)S(1)}, u32[]{:S(2)}, u32[]{:S(2)}) collective-permute-start(bf16[256,1024]{1,0:T(8,128)(2,1)} %broadcast_select_fusion.7), channel_id=1, source_target_pairs={{0,16},{16,0},{1,17},{17,1},{2,18},{18,2},{3,19},{19,3},{4,20},{20... | collective-permute-start | bytes 1572872 | tf_op jit(solution)/shard_map/ppermute | solution.py:118
  454.3 34.3 %collective-permute-start.98 = (bf16[256,1024]{1,0:T(8,128)(2,1)}, bf16[256,1024]{1,0:T(8,128)(2,1)S(1)}, u32[]{:S(2)}, u32[]{:S(2)}) collective-permute-start(bf16[256,1024]{1,0:T(8,128)(2,1)} %fusion.4), channel_id=1, source_target_pairs={{0,16},{1,17},{2,18},{3,19},{4,20},{5,21},{6,22},{7,23},{8,24},{9,... | collective-permute-start | bytes 1572872 | tf_op jit(solution)/shard_map/ppermute | solution.py:239
  466.8 16.7 %collective-permute-start.93 = (bf16[256,1024]{1,0:T(8,128)(2,1)S(1)}, bf16[256,1024]{1,0:T(8,128)(2,1)S(1)}, u32[]{:S(2)}, u32[]{:S(2)}) collective-permute-start(bf16[256,1024]{1,0:T(8,128)(2,1)S(1)} %add_convert_fusion.1), channel_id=1, source_target_pairs={{0,4},{4,8},{8,12},{12,0},{1,5},{5,9},{9,13},{13,1},{2,6},{6,10},{... | collective-permute-start | bytes 1572872 | tf_op jit(solution)/shard_map/ppermute | solution.py:229
  470.7 21.7 %collective-permute-start.99 = (bf16[128,2048]{1,0:T(8,128)(2,1)S(1)}, bf16[128,2048]{1,0:T(8,128)(2,1)S(1)}, u32[]{:S(2)}, u32[]{:S(2)}) collective-permute-start(bf16[128,2048]{1,0:T(8,128)(2,1)S(1)} %add_convert_fusion), channel_id=1, source_target_pairs={{0,4},{4,8},{8,12},{12,0},{1,5},{5,9},{9,13},{13,1},{2,6},{6,10},{... | collective-permute-start | bytes 1572872 | tf_op jit(solution)/shard_map/ppermute | solution.py:229
  471.2 21.1 %collective-permute-start.100 = (bf16[128,2048]{1,0:T(8,128)(2,1)S(1)}, bf16[128,2048]{1,0:T(8,128)(2,1)S(1)}, u32[]{:S(2)}, u32[]{:S(2)}) collective-permute-start(bf16[128,2048]{1,0:T(8,128)(2,1)S(1)} %copy-done.85), channel_id=1, source_target_pairs={{0,16},{16,0},{1,17},{17,1},{2,18},{18,2},{3,19},{19,3},{4,20},{20... | collective-permute-start | bytes 1572872 | tf_op jit(solution)/shard_map/ppermute | solution.py:118
  (188 other events, 1912.8 us)

commit v2 on v1

--- a/solution.py
+++ b/solution.py
@@ -228,7 +228,10 @@
             self.sent = self.total(gate).astype(BF)
             new.append(lax.ppermute(self.sent, "dp", pairs))
         if self.other is not None:
-            new.append(swap_section(tie(dp_rows(self.other, self.done), *gate)))
+            if self.done == 1:
+                new.append(swap_section(dp_rows(tie(self.other, *gate), 1)))
+            else:
+                new.append(swap_section(tie(dp_rows(self.other, self.done), *gate)))
         self.terms = [*new, dp_rows(self.mine, self.done)]
         return new
 
@@ -1121,7 +1124,7 @@
 
     block_out = both(y0, y1, came_y0, came_y1)
     input_grads = both(dx0, dx1, came_dx0, came_dx1)
-    sum_att0.came = tie(sum_att0.came, block_out)
+    sum_ff0.came = tie(sum_ff0.came, block_out, input_grads)
 
     def by_unit(qkv_sums, unit_sums):
         q = qkv_sums[:, :width].reshape(heads, 1, size)

time: 527 us -> 530 us (level)
  transfers between devices with their start and end apart: 105 -> 105, of which waited for: 53 -> 55; matrix products, arithmetic and copies ran while one was open for 9% -> 10% of each run, Pallas kernels for 27% -> 27%
where the time goes in v2:
time: 530 us; the launch traced here: 519 us
  waiting for transfers between devices  184 us (35%)
  Pallas kernels  157 us (30%)
  starting transfers between devices  91.1 us (17%)
  other arithmetic  42.4 us (8%)
  local copies, waits for them, and re-layouts  41.3 us (8%)
    ppermute x17, waiting for transfers between devices, from_chip(): return lax.ppermute(v, 'tensor', pairs)  44 us
    ppermute x12, waiting for transfers between devices, one(): new.append(lax.ppermute(self.sent, 'dp', pairs))  43.1 us
    pallas_call x6, Pallas kernels, mlp_call(): pl.pallas_call(body, grid=(blocks,), in_specs=in_specs, out_specs=out_spe...  42.3 us
    ppermute x28, starting transfers between devices, swap_section(): return lax.ppermute(v, 'section', [(0, 1), (1, 0)])  37.6 us
    pallas_call x2, Pallas kernels, attention_back(): pl.pallas_call(body, grid=(1,), in_specs=[whole(a.shape) for a in operand...  34.8 us
    ppermute x28, waiting for transfers between devices, swap_section(): return lax.ppermute(v, 'section', [(0, 1), (1, 0)])  33.3 us
    pallas_call x4, Pallas kernels, weight_grads(): pl.pallas_call(body, grid=(dp,), in_specs=specs, out_specs=[pl.BlockSpec(...  31.1 us
    unnamed x260, local copies, waits for them, and re-layouts  27.8 us
  transfers between devices with their start and end apart: 105, of which 55 were waited for; matrix products, arithmetic and copies ran while one was open for 10% of the time, Pallas kernels for 27%

profile of v2, /device:TPU:0, one launch (start us, length us, event | category | flops | bytes accessed | tf_op | source)
XLA Modules:
  0.0 519.4 jit_solution(1405018860104358863)
XLA Ops:
  8.2 3.8 collective-permute-done.1
  29.6 9.8 %collective-permute-done.6.refs_2_ = bf16[144,1024]{1,0:T(8,128)(2,1)} collective-permute-done((bf16[144,1024]{1,0:T(8,128)(2,1)}, bf16[144,1024]{1,0:T(8,128)(2,1)}, u32[]{:S(2)}, u32[]{:S(2)}) %collective-permute-start.6) | collective-permute-done | bytes 294944 | tf_op jit(solution)/shard_map/ppermute | solution.py:165
  61.9 4.5 collective-permute-done.11.a_ref.refs_2_
  76.0 9.5 %attention.2 = (bf16[512,256]{1,0:T(8,128)(2,1)}, bf16[512,256]{1,0:T(8,128)(2,1)}, f32[4,1024]{1,0:T(4,128)S(1)}, bf16[256,1024]{1,0:T(8,128)(2,1)S(1)}, bf16[2...) custom-call(bf16[512,768]{1,0:T(8,128)(2,1)S(1)} %project_qkv.4.refs_0_, bf16[512,768]{1,0:T(8,128)(2,1)S(1)} %project_qkv.5.refs_1_, ...), custom_call_target="tpu_custom_call" | custom-call | flops 10350000128 | tf_op jit(solution)/shard_map/attention/pallas_call | solution.py:525
  94.1 9.4 %collective-permute-done.18.refs_2_ = bf16[256,1024]{1,0:T(8,128)(2,1)S(1)} collective-permute-done((bf16[256,1024]{1,0:T(8,128)(2,1)S(1)}, bf16[256,1024]{1,0:T(8,128)(2,1)S(1)}, u32[]{:S(2)}, u32[]{:S(2)}) %collective-permute-start.18) | collective-permute-done | bytes 524320 | tf_op jit(solution)/shard_map/ppermute | solution.py:66
  110.8 9.1 %collective-permute-done.24.refs_2_ = bf16[128,1024]{1,0:T(8,128)(2,1)S(1)} collective-permute-done((bf16[128,1024]{1,0:T(8,128)(2,1)S(1)}, bf16[128,1024]{1,0:T(8,128)(2,1)S(1)}, u32[]{:S(2)}, u32[]{:S(2)}) %collective-permute-start.24) | collective-permute-done | bytes 262176 | tf_op jit(solution)/shard_map/ppermute | solution.py:184
  123.6 6.6 %mlp_forward.2 = (bf16[512,1024]{1,0:T(8,128)(2,1)}, bf16[512,1024]{1,0:T(8,128)(2,1)}, f32[1,1024]{1,0:T(1,128)}, bf16[256,1024]{1,0:T(8,128)(2,1)S(1)}, bf16[256,1024]{1,0:T(8,128)(2,1)S(1)}) custom-call(bf16[256,1024]{1,0:T(8,128)(2,1)S(1)} %get-tuple-element.192.a.refs_0_, bf16[256,1024]{1,0:T(8,128)(2,1)S(1)} %collective-permute-done.21.b.refs_1_, ...), custom_call_target="tpu_custom_call" | custom-call | flops 575000000 | tf_op jit(solution)/shard_map/mlp_forward/pallas_call | solution.py:729
  132.2 6.5 %mlp_forward.3 = (bf16[512,1024]{1,0:T(8,128)(2,1)}, bf16[512,1024]{1,0:T(8,128)(2,1)}, f32[1,1024]{1,0:T(1,128)}, bf16[256,1024]{1,0:T(8,128)(2,1)S(1)}, bf16[256,1024]{1,0:T(8,128)(2,1)S(1)}) custom-call(bf16[256,1024]{1,0:T(8,128)(2,1)S(1)} %collective-permute-done.23.a.refs_2_, bf16[256,1024]{1,0:T(8,128)(2,1)S(1)} %collective-permute-done.26.b.refs_3_, ...), custom_call_target="tpu_custom_call" | custom-call | flops 575000000 | tf_op jit(solution)/shard_map/mlp_forward/pallas_call | solution.py:729
  146.3 7.1 %collective-permute-done.33.refs_5_ = bf16[128,1024]{1,0:T(8,128)(2,1)S(1)} collective-permute-done((bf16[128,1024]{1,0:T(8,128)(2,1)S(1)}, bf16[128,1024]{1,0:T(8,128)(2,1)S(1)}, u32[]{:S(2)}, u32[]{:S(2)}) %collective-permute-start.33) | collective-permute-done | bytes 262176 | tf_op jit(solution)/shard_map/ppermute | solution.py:118
  153.4 5.2 %collective-permute-done.34.refs_7_ = bf16[128,1024]{1,0:T(8,128)(2,1)S(1)} collective-permute-done((bf16[128,1024]{1,0:T(8,128)(2,1)S(1)}, bf16[128,1024]{1,0:T(8,128)(2,1)S(1)}, u32[]{:S(2)}, u32[]{:S(2)}) %collective-permute-start.34) | collective-permute-done | bytes 262176 | tf_op jit(solution)/shard_map/ppermute | solution.py:118
  170.5 6.3 %collective-permute-done.36.a_ref.refs_2_ = bf16[256,1024]{1,0:T(8,128)(2,1)} collective-permute-done((bf16[256,1024]{1,0:T(8,128)(2,1)}, bf16[256,1024]{1,0:T(8,128)(2,1)}, u32[]{:S(2)}, u32[]{:S(2)}) %collective-permute-start.36) | collective-permute-done | bytes 524320 | tf_op jit(solution)/shard_map/ppermute | solution.py:66
  184.3 9.9 %attention.3 = (bf16[512,256]{1,0:T(8,128)(2,1)}, bf16[512,256]{1,0:T(8,128)(2,1)}, f32[4,1024]{1,0:T(4,128)S(1)}, bf16[256,1024]{1,0:T(8,128)(2,1)S(1)}, bf16[2...) custom-call(bf16[512,768]{1,0:T(8,128)(2,1)S(1)} %project_qkv.6.refs_0_, bf16[512,768]{1,0:T(8,128)(2,1)S(1)} %project_qkv.7.refs_1_, ...), custom_call_target="tpu_custom_call" | custom-call | flops 10350000128 | tf_op jit(solution)/shard_map/attention/pallas_call | solution.py:525
  200.6 12.4 %collective-permute-done.44.refs_2_ = bf16[256,1024]{1,0:T(8,128)(2,1)S(1)} collective-permute-done((bf16[256,1024]{1,0:T(8,128)(2,1)S(1)}, bf16[256,1024]{1,0:T(8,128)(2,1)S(1)}, u32[]{:S(2)}, u32[]{:S(2)}) %collective-permute-start.44) | collective-permute-done | bytes 524320 | tf_op jit(solution)/shard_map/ppermute | solution.py:66
  218.5 8.9 %mlp_both.2 = (bf16[512,1024]{1,0:T(8,128)(2,1)}, bf16[512,1024]{1,0:T(8,128)(2,1)}, f32[1,1024]{1,0:T(1,128)S(1)}, bf16[256,1024]{1,0:T(8,128)(2,1)S(1)}, bf16[...) custom-call(bf16[256,1024]{1,0:T(8,128)(2,1)S(1)} %get-tuple-element.225.a.refs_0_, ...), custom_call_target="tpu_custom_call" | custom-call | flops 575000000 | tf_op jit(solution)/shard_map/mlp_both/pallas_call | solution.py:729
  231.7 9.0 %mlp_both.3 = (bf16[512,1024]{1,0:T(8,128)(2,1)}, bf16[512,1024]{1,0:T(8,128)(2,1)}, f32[1,1024]{1,0:T(1,128)S(1)}, bf16[256,1024]{1,0:T(8,128)(2,1)S(1)}, bf16[...) custom-call(bf16[256,1024]{1,0:T(8,128)(2,1)S(1)} %collective-permute-done.49.a.refs_2_, ...), custom_call_target="tpu_custom_call" | custom-call | flops 575000000 | tf_op jit(solution)/shard_map/mlp_both/pallas_call | solution.py:729
  248.1 9.3 %grad_ff.2 = (bf16[512,2048]{1,0:T(8,128)(2,1)}, bf16[512,2048]{1,0:T(8,128)(2,1)}) custom-call(s32[1]{0:T(128)} %bitcast.15.side_ref, bf16[256,1024]{1,0:T(8,128)(2,1)S(1)} %get-tuple-element.225.a.refs_0_, bf16[256,1024]{1,0:T(8,128)(2,1)S(1)} %collective-permute-done.48.b.refs_1_, bf16[256,1024]{1,0:T(8,128)(2,1)S(1)} %collective-permute-done.49.a.refs_2_, ...), custom_call_target="tpu_custom_call" | custom-call | flops 5750000128 | tf_op jit(solution)/shard_map/grad_ff/pallas_call | solution.py:887
  264.3 9.7 %collective-permute-done.56 = bf16[128,2048]{1,0:T(8,128)(2,1)S(1)} collective-permute-done((bf16[128,2048]{1,0:T(8,128)(2,1)S(1)}, bf16[128,2048]{1,0:T(8,128)(2,1)S(1)}, u32[]{:S(2)}, u32[]{:S(2)}) %collective-permute-start.56) | collective-permute-done | bytes 524320 | tf_op jit(solution)/shard_map/ppermute | solution.py:118
  278.6 17.3 %attention_back.2 = (bf16[512,768]{1,0:T(8,128)(2,1)}, bf16[512,768]{1,0:T(8,128)(2,1)}, bf16[256,1024]{1,0:T(8,128)(2,1)}, bf16[256,1024]{1,0:T(8,128)(2,1)}, b...) custom-call(bf16[512,768]{1,0:T(8,128)(2,1)} %copy-done.8, bf16[512,768]{1,0:T(8,128)(2,1)} %copy-done.9, ...), custom_call_target="tpu_custom_call" | custom-call | flops 17250000896 | tf_op jit(solution)/shard_map/attention_back/pallas_call | solution.py:667
  304.3 6.3 %grad_att.2 = bf16[1024,1024]{1,0:T(8,128)(2,1)} custom-call(s32[1]{0:T(128)} %bitcast.15.side_ref, bf16[256,1024]{1,0:T(8,128)(2,1)} %get-tuple-element.210.a_ref.refs_0_, bf16[256,1024]{1,0:T(8,128)(2,1)} %copy-done.20, bf16[256,1024]{1,0:T(8,128)(2,1)} %collective-permute-done.36.a_ref.refs_2_, bf16[256,1024]{1,0:T(8,128)(2,1)} %copy-done.22, ...), custom_call_target="tpu_custom_call" | custom-call | flops 5750000128 | tf_op jit(solution)/shard_map/grad_att/pallas_call | solution.py:887
  310.6 4.1 collective-permute-done.64.refs_3_
  325.9 5.6 %mlp_backward.2 = (bf16[512,1024]{1,0:T(8,128)(2,1)}, f32[1,1024]{1,0:T(1,128)S(1)}, bf16[256,1024]{1,0:T(8,128)(2,1)S(1)}, bf16[256,1024]{1,0:T(8,128)(2,1)S(1)}) custom-call(bf16[256,1024]{1,0:T(8,128)(2,1)S(1)} %get-tuple-element.267.a.refs_6_, bf16[256,1024]{1,0:T(8,128)(2,1)S(1)} %collective-permute-done.68.b.refs_7_, ...), custom_call_target="tpu_custom_call" | custom-call | flops 575000000 | tf_op jit(solution)/shard_map/mlp_backward/pallas_call | solution.py:729
  339.4 5.7 %mlp_backward.3 = (bf16[512,1024]{1,0:T(8,128)(2,1)}, f32[1,1024]{1,0:T(1,128)S(1)}, bf16[256,1024]{1,0:T(8,128)(2,1)S(1)}, bf16[256,1024]{1,0:T(8,128)(2,1)}) custom-call(bf16[256,1024]{1,0:T(8,128)(2,1)S(1)} %collective-permute-done.69.a.refs_8_, bf16[256,1024]{1,0:T(8,128)(2,1)S(1)} %collective-permute-done.72.b.refs_9_, ...), custom_call_target="tpu_custom_call" | custom-call | flops 575000000 | tf_op jit(solution)/shard_map/mlp_backward/pallas_call | solution.py:729
  354.4 9.2 %grad_ff.3 = (bf16[512,2048]{1,0:T(8,128)(2,1)}, bf16[512,2048]{1,0:T(8,128)(2,1)}) custom-call(s32[1]{0:T(128)} %bitcast.15.side_ref, bf16[256,1024]{1,0:T(8,128)(2,1)} %copy-done.16, bf16[256,1024]{1,0:T(8,128)(2,1)} %copy-done.17, bf16[256,1024]{1,0:T(8,128)(2,1)} %copy-done.18, bf16[256,1024]{1,0:T(8,128)(2,1)} %copy-done.19, ...), custom_call_target="tpu_custom_call" | custom-call | flops 5750000128 | tf_op jit(solution)/shard_map/grad_ff/pallas_call | solution.py:887
  384.0 4.8 collective-permute-done.80
  397.8 17.6 %attention_back.3 = (bf16[512,768]{1,0:T(8,128)(2,1)}, bf16[512,768]{1,0:T(8,128)(2,1)}, bf16[256,1024]{1,0:T(8,128)(2,1)}, bf16[256,1024]{1,0:T(8,128)(2,1)}, b...) custom-call(bf16[512,768]{1,0:T(8,128)(2,1)} %copy-done.6, bf16[512,768]{1,0:T(8,128)(2,1)} %copy-done.7, ...), custom_call_target="tpu_custom_call" | custom-call | flops 17250000896 | tf_op jit(solution)/shard_map/attention_back/pallas_call | solution.py:667
  415.4 4.6 collective-permute-done.84
  427.8 6.3 %grad_att.3 = bf16[1024,1024]{1,0:T(8,128)(2,1)} custom-call(s32[1]{0:T(128)} %bitcast.15.side_ref, bf16[256,1024]{1,0:T(8,128)(2,1)} %copy-done.12, bf16[256,1024]{1,0:T(8,128)(2,1)} %copy-done.13, bf16[256,1024]{1,0:T(8,128)(2,1)} %collective-permute-done.11.a_ref.refs_2_, bf16[256,1024]{1,0:T(8,128)(2,1)} %copy-done.15, ...), custom_call_target="tpu_custom_call" | custom-call | flops 5750000128 | tf_op jit(solution)/shard_map/grad_att/pallas_call | solution.py:887
  445.6 5.6 %collective-permute-done.91 = bf16[256,1024]{1,0:T(8,128)(2,1)} collective-permute-done((bf16[256,1024]{1,0:T(8,128)(2,1)S(1)}, bf16[256,1024]{1,0:T(8,128)(2,1)}, u32[]{:S(2)}, u32[]{:S(2)}) %collective-permute-start.91) | collective-permute-done | bytes 524320 | tf_op jit(solution)/shard_map/ppermute | solution.py:229
  456.6 4.0 collective-permute-start.98
  460.7 6.8 %collective-permute-done.92 = bf16[256,1024]{1,0:T(8,128)(2,1)} collective-permute-done((bf16[256,1024]{1,0:T(8,128)(2,1)S(1)}, bf16[256,1024]{1,0:T(8,128)(2,1)}, u32[]{:S(2)}, u32[]{:S(2)}) %collective-permute-start.92) | collective-permute-done | bytes 524320 | tf_op jit(solution)/shard_map/ppermute | solution.py:229
  475.8 9.8 %collective-permute-done.93 = bf16[256,1024]{1,0:T(8,128)(2,1)S(1)} collective-permute-done((bf16[256,1024]{1,0:T(8,128)(2,1)S(1)}, bf16[256,1024]{1,0:T(8,128)(2,1)S(1)}, u32[]{:S(2)}, u32[]{:S(2)}) %collective-permute-start.93) | collective-permute-done | bytes 524320 | tf_op jit(solution)/shard_map/ppermute | solution.py:229
  506.1 5.9 %collective-permute-done.104 = bf16[128,2048]{1,0:T(8,128)(2,1)} collective-permute-done((bf16[128,2048]{1,0:T(8,128)(2,1)}, bf16[128,2048]{1,0:T(8,128)(2,1)}, u32[]{:S(2)}, u32[]{:S(2)}) %collective-permute-start.104) | collective-permute-done | bytes 524320 | tf_op jit(solution)/shard_map/ppermute | solution.py:242
  (584 shorter events, 266.0 us)
Async XLA Ops:
  20.2 24.3 %collective-permute-start.4 = (bf16[144,1024]{1,0:T(8,128)(2,1)}, bf16[144,1024]{1,0:T(8,128)(2,1)}, u32[]{:S(2)}, u32[]{:S(2)}) collective-permute-start(bf16[144,1024]{1,0:T(8,128)(2,1)} %pad_maximum_fusion.1.refs_0_), channel_id=1, source_target_pairs={{0,8},{4,12},{8,0},{12,4},{1,9},{5,13},{9,1},{13,5},{2,10},{6,14},... | collective-permute-start | bytes 884744 | tf_op jit(solution)/shard_map/ppermute | solution.py:165
  20.3 19.1 %collective-permute-start.6 = (bf16[144,1024]{1,0:T(8,128)(2,1)}, bf16[144,1024]{1,0:T(8,128)(2,1)}, u32[]{:S(2)}, u32[]{:S(2)}) collective-permute-start(bf16[144,1024]{1,0:T(8,128)(2,1)} %pad_maximum_fusion.1.refs_0_), channel_id=1, source_target_pairs={{0,4},{4,8},{8,12},{12,0},{1,5},{5,9},{9,13},{13,1},{2,6},{6,10},{... | collective-permute-start | bytes 884744 | tf_op jit(solution)/shard_map/ppermute | solution.py:165
  21.3 24.8 %collective-permute-start.2 = (bf16[128,2048]{1,0:T(8,128)(2,1)S(1)}, bf16[128,2048]{1,0:T(8,128)(2,1)S(1)}, u32[]{:S(2)}, u32[]{:S(2)}) collective-permute-start(bf16[128,2048]{1,0:T(8,128)(2,1)S(1)} %fusion.9), channel_id=1, source_target_pairs={{0,16},{16,0},{1,17},{17,1},{2,18},{18,2},{3,19},{19,3},{4,20},{20... | collective-permute-start | bytes 1572872 | tf_op jit(solution)/shard_map/ppermute | solution.py:118
  28.1 19.8 %collective-permute-start.5 = (bf16[144,1024]{1,0:T(8,128)(2,1)S(1)}, bf16[144,1024]{1,0:T(8,128)(2,1)S(1)}, u32[]{:S(2)}, u32[]{:S(2)}) collective-permute-start(bf16[144,1024]{1,0:T(8,128)(2,1)S(1)} %collective-permute-done.3.refs_6_), channel_id=1, source_target_pairs={{0,16},{16,0},{1,17},{17,1},{2,18},{18,2},{3,19},{19,3},{4,20},{20... | collective-permute-start | bytes 884744 | tf_op jit(solution)/shard_map/ppermute | solution.py:118
  54.3 15.9 %collective-permute-start.13 = (bf16[128,2048]{1,0:T(8,128)(2,1)}, bf16[128,2048]{1,0:T(8,128)(2,1)}, u32[]{:S(2)}, u32[]{:S(2)}) collective-permute-start(bf16[128,2048]{1,0:T(8,128)(2,1)} %broadcast_select_fusion.3.refs_0_), channel_id=1, source_target_pairs={{0,4},{4,8},{8,12},{12,0},{1,5},{5,9},{9,13},{13,1},{2,6},{6,10},{... | collective-permute-start | bytes 1572872 | tf_op jit(solution)/shard_map/ppermute | solution.py:184
  70.2 16.3 %collective-permute-start.15 = (bf16[128,2048]{1,0:T(8,128)(2,1)}, bf16[128,2048]{1,0:T(8,128)(2,1)S(1)}, u32[]{:S(2)}, u32[]{:S(2)}) collective-permute-start(bf16[128,2048]{1,0:T(8,128)(2,1)} %collective-permute-done.13.refs_2_), channel_id=1, source_target_pairs={{0,4},{4,8},{8,12},{12,0},{1,5},{5,9},{9,13},{13,1},{2,6},{6,10},{... | collective-permute-start | bytes 1572872 | tf_op jit(solution)/shard_map/ppermute | solution.py:184
  108.4 21.8 %collective-permute-start.23 = (bf16[256,1024]{1,0:T(8,128)(2,1)S(1)}, bf16[256,1024]{1,0:T(8,128)(2,1)S(1)}, u32[]{:S(2)}, u32[]{:S(2)}) collective-permute-start(bf16[256,1024]{1,0:T(8,128)(2,1)S(1)} %get-tuple-element.192.a.refs_0_), channel_id=1, source_target_pairs={{2,0},{3,1},{0,2},{1,3},{6,4},{7,5},{4,6},{5,7},{10,8},{11,9},{8,1... | collective-permute-start | bytes 1572872 | tf_op jit(solution)/shard_map/ppermute | solution.py:66
  144.2 16.2 %collective-permute-start.32 = (bf16[128,2048]{1,0:T(8,128)(2,1)S(1)}, bf16[128,2048]{1,0:T(8,128)(2,1)}, u32[]{:S(2)}, u32[]{:S(2)}) collective-permute-start(bf16[128,2048]{1,0:T(8,128)(2,1)S(1)} %copy-done.74), channel_id=1, source_target_pairs={{0,4},{4,8},{8,12},{12,0},{1,5},{5,9},{9,13},{13,1},{2,6},{6,10},{... | collective-permute-start | bytes 1572872 | tf_op jit(solution)/shard_map/ppermute | solution.py:184
  163.3 16.1 %collective-permute-start.37 = (bf16[128,2048]{1,0:T(8,128)(2,1)}, bf16[128,2048]{1,0:T(8,128)(2,1)}, u32[]{:S(2)}, u32[]{:S(2)}) collective-permute-start(bf16[128,2048]{1,0:T(8,128)(2,1)} %collective-permute-done.32.refs_2_), channel_id=1, source_target_pairs={{0,4},{4,8},{8,12},{12,0},{1,5},{5,9},{9,13},{13,1},{2,6},{6,10},{... | collective-permute-start | bytes 1572872 | tf_op jit(solution)/shard_map/ppermute | solution.py:184
  163.7 15.7 %collective-permute-start.38 = (bf16[128,2048]{1,0:T(8,128)(2,1)}, bf16[128,2048]{1,0:T(8,128)(2,1)}, u32[]{:S(2)}, u32[]{:S(2)}) collective-permute-start(bf16[128,2048]{1,0:T(8,128)(2,1)} %collective-permute-done.32.refs_2_), channel_id=1, source_target_pairs={{0,16},{16,0},{1,17},{17,1},{2,18},{18,2},{3,19},{19,3},{4,20},{20... | collective-permute-start | bytes 1572872 | tf_op jit(solution)/shard_map/ppermute | solution.py:118
  179.7 16.4 %collective-permute-start.41 = (bf16[128,2048]{1,0:T(8,128)(2,1)}, bf16[128,2048]{1,0:T(8,128)(2,1)S(1)}, u32[]{:S(2)}, u32[]{:S(2)}) collective-permute-start(bf16[128,2048]{1,0:T(8,128)(2,1)} %collective-permute-done.37.refs_4_), channel_id=1, source_target_pairs={{0,4},{4,8},{8,12},{12,0},{1,5},{5,9},{9,13},{13,1},{2,6},{6,10},{... | collective-permute-start | bytes 1572872 | tf_op jit(solution)/shard_map/ppermute | solution.py:184
  179.7 16.3 %collective-permute-start.42 = (bf16[128,2048]{1,0:T(8,128)(2,1)}, bf16[128,2048]{1,0:T(8,128)(2,1)S(1)}, u32[]{:S(2)}, u32[]{:S(2)}) collective-permute-start(bf16[128,2048]{1,0:T(8,128)(2,1)} %collective-permute-done.37.refs_4_), channel_id=1, source_target_pairs={{0,16},{16,0},{1,17},{17,1},{2,18},{18,2},{3,19},{19,3},{4,20},{20... | collective-permute-start | bytes 1572872 | tf_op jit(solution)/shard_map/ppermute | solution.py:118
  263.0 32.9 %collective-permute-start.58 = (bf16[256,1024]{1,0:T(8,128)(2,1)S(1)}, bf16[256,1024]{1,0:T(8,128)(2,1)S(1)}, u32[]{:S(2)}, u32[]{:S(2)}) collective-permute-start(bf16[256,1024]{1,0:T(8,128)(2,1)S(1)} %get-tuple-element.252.refs_0_.refs_1_), channel_id=1, source_target_pairs={{16,0},{17,1},{18,2},{19,3},{20,4},{21,5},{22,6},{23,7},{24,8},{25... | collective-permute-start | bytes 1572872 | tf_op jit(solution)/shard_map/ppermute | solution.py:1053
  275.5 20.4 %collective-permute-start.61 = (bf16[128,2048]{1,0:T(8,128)(2,1)S(1)}, bf16[128,2048]{1,0:T(8,128)(2,1)S(1)}, u32[]{:S(2)}, u32[]{:S(2)}) collective-permute-start(bf16[128,2048]{1,0:T(8,128)(2,1)S(1)} %add_convert_fusion.12), channel_id=1, source_target_pairs={{0,4},{4,8},{8,12},{12,0},{1,5},{5,9},{9,13},{13,1},{2,6},{6,10},{... | collective-permute-start | bytes 1572872 | tf_op jit(solution)/shard_map/ppermute | solution.py:229
  275.7 20.3 %collective-permute-start.62 = (bf16[128,2048]{1,0:T(8,128)(2,1)S(1)}, bf16[128,2048]{1,0:T(8,128)(2,1)S(1)}, u32[]{:S(2)}, u32[]{:S(2)}) collective-permute-start(bf16[128,2048]{1,0:T(8,128)(2,1)S(1)} %get-tuple-element.258), channel_id=1, source_target_pairs={{0,16},{16,0},{1,17},{17,1},{2,18},{18,2},{3,19},{19,3},{4,20},{20... | collective-permute-start | bytes 1572872 | tf_op jit(solution)/shard_map/ppermute | solution.py:118
  277.5 18.6 %collective-permute-start.60 = (bf16[256,1024]{1,0:T(8,128)(2,1)S(1)}, bf16[256,1024]{1,0:T(8,128)(2,1)S(1)}, u32[]{:S(2)}, u32[]{:S(2)}) collective-permute-start(bf16[256,1024]{1,0:T(8,128)(2,1)S(1)} %add_convert_fusion.13), channel_id=1, source_target_pairs={{2,0},{3,1},{0,2},{1,3},{6,4},{7,5},{4,6},{5,7},{10,8},{11,9},{8,1... | collective-permute-start | bytes 1572872 | tf_op jit(solution)/shard_map/ppermute | solution.py:66
  296.7 27.0 %collective-permute-start.67 = (bf16[256,1024]{1,0:T(8,128)(2,1)S(1)}, bf16[256,1024]{1,0:T(8,128)(2,1)S(1)}, u32[]{:S(2)}, u32[]{:S(2)}) collective-permute-start(bf16[256,1024]{1,0:T(8,128)(2,1)S(1)} %copy-done.35), channel_id=1, source_target_pairs={{0,1},{1,0},{2,3},{3,2},{4,5},{5,4},{6,7},{7,6},{8,9},{9,8},{10,11... | collective-permute-start | bytes 1572872 | tf_op jit(solution)/shard_map/ppermute | solution.py:59
  301.8 15.7 %collective-permute-start.65 = (bf16[128,2048]{1,0:T(8,128)(2,1)S(1)}, bf16[128,2048]{1,0:T(8,128)(2,1)S(1)}, u32[]{:S(2)}, u32[]{:S(2)}) collective-permute-start(bf16[128,2048]{1,0:T(8,128)(2,1)S(1)} %add_convert_fusion.10), channel_id=1, source_target_pairs={{0,4},{4,8},{8,12},{12,0},{1,5},{5,9},{9,13},{13,1},{2,6},{6,10},{... | collective-permute-start | bytes 1572872 | tf_op jit(solution)/shard_map/ppermute | solution.py:229
  321.6 15.8 %collective-permute-start.70 = (bf16[128,2048]{1,0:T(8,128)(2,1)S(1)}, bf16[128,2048]{1,0:T(8,128)(2,1)S(1)}, u32[]{:S(2)}, u32[]{:S(2)}) collective-permute-start(bf16[128,2048]{1,0:T(8,128)(2,1)S(1)} %add_convert_fusion.9), channel_id=1, source_target_pairs={{0,4},{4,8},{8,12},{12,0},{1,5},{5,9},{9,13},{13,1},{2,6},{6,10},{... | collective-permute-start | bytes 1572872 | tf_op jit(solution)/shard_map/ppermute | solution.py:229
  347.3 16.4 %collective-permute-start.77 = (bf16[256,1024]{1,0:T(8,128)(2,1)S(1)}, bf16[256,1024]{1,0:T(8,128)(2,1)S(1)}, u32[]{:S(2)}, u32[]{:S(2)}) collective-permute-start(bf16[256,1024]{1,0:T(8,128)(2,1)S(1)} %constant_dynamic-slice_fusion.9), channel_id=1, source_target_pairs={{0,4},{4,8},{8,12},{12,0},{1,5},{5,9},{9,13},{13,1},{2,6},{6,10},{... | collective-permute-start | bytes 1572872 | tf_op jit(solution)/shard_map/ppermute | solution.py:229
  380.8 17.0 %collective-permute-start.78 = (bf16[256,1024]{1,0:T(8,128)(2,1)S(1)}, bf16[256,1024]{1,0:T(8,128)(2,1)S(1)}, u32[]{:S(2)}, u32[]{:S(2)}) collective-permute-start(bf16[256,1024]{1,0:T(8,128)(2,1)S(1)} %get-tuple-element.297.refs_5_.refs_6_), channel_id=1, source_target_pairs={{0,1},{1,0},{2,3},{3,2},{4,5},{5,4},{6,7},{7,6},{8,9},{9,8},{10,11... | collective-permute-start | bytes 1572872 | tf_op jit(solution)/shard_map/ppermute | solution.py:59
  380.8 34.5 %collective-permute-start.85 = (bf16[128,2048]{1,0:T(8,128)(2,1)S(1)}, bf16[128,2048]{1,0:T(8,128)(2,1)S(1)}, u32[]{:S(2)}, u32[]{:S(2)}) collective-permute-start(bf16[128,2048]{1,0:T(8,128)(2,1)S(1)} %get-tuple-element.306), channel_id=1, source_target_pairs={{0,16},{16,0},{1,17},{17,1},{2,18},{18,2},{3,19},{19,3},{4,20},{20... | collective-permute-start | bytes 1572872 | tf_op jit(solution)/shard_map/ppermute | solution.py:118
  392.6 22.8 %collective-permute-start.83 = (bf16[256,1024]{1,0:T(8,128)(2,1)S(1)}, bf16[256,1024]{1,0:T(8,128)(2,1)S(1)}, u32[]{:S(2)}, u32[]{:S(2)}) collective-permute-start(bf16[256,1024]{1,0:T(8,128)(2,1)S(1)} %add_convert_fusion.6), channel_id=1, source_target_pairs={{0,4},{4,8},{8,12},{12,0},{1,5},{5,9},{9,13},{13,1},{2,6},{6,10},{... | collective-permute-start | bytes 1572872 | tf_op jit(solution)/shard_map/ppermute | solution.py:229
  395.6 24.5 %collective-permute-start.84 = (bf16[128,2048]{1,0:T(8,128)(2,1)S(1)}, bf16[128,2048]{1,0:T(8,128)(2,1)S(1)}, u32[]{:S(2)}, u32[]{:S(2)}) collective-permute-start(bf16[128,2048]{1,0:T(8,128)(2,1)S(1)} %add_convert_fusion.5), channel_id=1, source_target_pairs={{0,4},{4,8},{8,12},{12,0},{1,5},{5,9},{9,13},{13,1},{2,6},{6,10},{... | collective-permute-start | bytes 1572872 | tf_op jit(solution)/shard_map/ppermute | solution.py:229
  423.5 16.4 %collective-permute-start.88 = (bf16[128,2048]{1,0:T(8,128)(2,1)}, bf16[128,2048]{1,0:T(8,128)(2,1)}, u32[]{:S(2)}, u32[]{:S(2)}) collective-permute-start(bf16[128,2048]{1,0:T(8,128)(2,1)} %add_convert_fusion.3), channel_id=1, source_target_pairs={{0,4},{4,8},{8,12},{12,0},{1,5},{5,9},{9,13},{13,1},{2,6},{6,10},{... | collective-permute-start | bytes 1572872 | tf_op jit(solution)/shard_map/ppermute | solution.py:229
  423.5 16.4 %collective-permute-start.89 = (bf16[128,2048]{1,0:T(8,128)(2,1)}, bf16[128,2048]{1,0:T(8,128)(2,1)}, u32[]{:S(2)}, u32[]{:S(2)}) collective-permute-start(bf16[128,2048]{1,0:T(8,128)(2,1)} %get-tuple-element.312), channel_id=1, source_target_pairs={{0,16},{16,0},{1,17},{17,1},{2,18},{18,2},{3,19},{19,3},{4,20},{20... | collective-permute-start | bytes 1572872 | tf_op jit(solution)/shard_map/ppermute | solution.py:118
  435.1 16.1 %collective-permute-start.91 = (bf16[256,1024]{1,0:T(8,128)(2,1)S(1)}, bf16[256,1024]{1,0:T(8,128)(2,1)}, u32[]{:S(2)}, u32[]{:S(2)}) collective-permute-start(bf16[256,1024]{1,0:T(8,128)(2,1)S(1)} %constant_dynamic-slice_fusion.5), channel_id=1, source_target_pairs={{0,4},{4,8},{8,12},{12,0},{1,5},{5,9},{9,13},{13,1},{2,6},{6,10},{... | collective-permute-start | bytes 1572872 | tf_op jit(solution)/shard_map/ppermute | solution.py:229
  444.1 47.0 %collective-permute-start.90 = (bf16[256,1024]{1,0:T(8,128)(2,1)}, bf16[256,1024]{1,0:T(8,128)(2,1)S(1)}, u32[]{:S(2)}, u32[]{:S(2)}) collective-permute-start(bf16[256,1024]{1,0:T(8,128)(2,1)} %broadcast_select_fusion.7), channel_id=1, source_target_pairs={{0,16},{16,0},{1,17},{17,1},{2,18},{18,2},{3,19},{19,3},{4,20},{20... | collective-permute-start | bytes 1572872 | tf_op jit(solution)/shard_map/ppermute | solution.py:118
  456.6 34.5 %collective-permute-start.98 = (bf16[256,1024]{1,0:T(8,128)(2,1)}, bf16[256,1024]{1,0:T(8,128)(2,1)S(1)}, u32[]{:S(2)}, u32[]{:S(2)}) collective-permute-start(bf16[256,1024]{1,0:T(8,128)(2,1)} %fusion.4), channel_id=1, source_target_pairs={{0,16},{1,17},{2,18},{3,19},{4,20},{5,21},{6,22},{7,23},{8,24},{9,... | collective-permute-start | bytes 1572872 | tf_op jit(solution)/shard_map/ppermute | solution.py:242
  468.9 16.7 %collective-permute-start.93 = (bf16[256,1024]{1,0:T(8,128)(2,1)S(1)}, bf16[256,1024]{1,0:T(8,128)(2,1)S(1)}, u32[]{:S(2)}, u32[]{:S(2)}) collective-permute-start(bf16[256,1024]{1,0:T(8,128)(2,1)S(1)} %add_convert_fusion.1), channel_id=1, source_target_pairs={{0,4},{4,8},{8,12},{12,0},{1,5},{5,9},{9,13},{13,1},{2,6},{6,10},{... | collective-permute-start | bytes 1572872 | tf_op jit(solution)/shard_map/ppermute | solution.py:229
  473.2 21.0 %collective-permute-start.99 = (bf16[128,2048]{1,0:T(8,128)(2,1)S(1)}, bf16[128,2048]{1,0:T(8,128)(2,1)S(1)}, u32[]{:S(2)}, u32[]{:S(2)}) collective-permute-start(bf16[128,2048]{1,0:T(8,128)(2,1)S(1)} %add_convert_fusion), channel_id=1, source_target_pairs={{0,4},{4,8},{8,12},{12,0},{1,5},{5,9},{9,13},{13,1},{2,6},{6,10},{... | collective-permute-start | bytes 1572872 | tf_op jit(solution)/shard_map/ppermute | solution.py:229
  473.7 20.5 %collective-permute-start.100 = (bf16[128,2048]{1,0:T(8,128)(2,1)S(1)}, bf16[128,2048]{1,0:T(8,128)(2,1)S(1)}, u32[]{:S(2)}, u32[]{:S(2)}) collective-permute-start(bf16[128,2048]{1,0:T(8,128)(2,1)S(1)} %copy-done.75), channel_id=1, source_target_pairs={{0,16},{16,0},{1,17},{17,1},{2,18},{18,2},{3,19},{19,3},{4,20},{20... | collective-permute-start | bytes 1572872 | tf_op jit(solution)/shard_map/ppermute | solution.py:118
  (188 other events, 1908.7 us)

commit v3 on v1

--- a/solution.py
+++ b/solution.py
@@ -511,7 +511,7 @@
                 lse_ref[h : h + 1, at] = top + jnp.log(norm)
             return carry
 
-        lax.fori_loop(0, seq // step, one, 0)
+        lax.fori_loop(0, seq // step, one, 0, unroll=True)
         for c in range(chips):
             at = slice(c * span, (c + 1) * span)
             o = ot_ref[:, at].T.astype(BF)
@@ -638,7 +638,7 @@
 
             return carry
 
-        lax.fori_loop(0, seq // step, one, 0)
+        lax.fori_loop(0, seq // step, one, 0, unroll=True)
         for c in range(chips):
             rows = slice(c * span, (c + 1) * span)
             out = dqkv_refs[c]

time: 527 us -> 524 us (level)
  Pallas kernels: 158 us -> 152 us
  waiting for transfers between devices: 186 us -> 192 us
  transfers between devices with their start and end apart: 105 -> 105, of which waited for: 53 -> 53; matrix products, arithmetic and copies ran while one was open for 9% -> 9% of each run, Pallas kernels for 27% -> 26%
where the time goes in v3:
time: 524 us; the launch traced here: 517 us
  waiting for transfers between devices  192 us (37%)
  Pallas kernels  152 us (29%)
  starting transfers between devices  89 us (17%)
  other arithmetic  42.4 us (8%)
  local copies, waits for them, and re-layouts  38.4 us (7%)
    ppermute x17, waiting for transfers between devices, from_chip(): return lax.ppermute(v, 'tensor', pairs)  51.1 us
    ppermute x12, waiting for transfers between devices, one(): new.append(lax.ppermute(self.sent, 'dp', pairs))  47.6 us
    pallas_call x6, Pallas kernels, mlp_call(): pl.pallas_call(body, grid=(blocks,), in_specs=in_specs, out_specs=out_spe...  42.3 us
    ppermute x28, starting transfers between devices, swap_section(): return lax.ppermute(v, 'section', [(0, 1), (1, 0)])  36 us
    pallas_call x2, Pallas kernels, attention_back(): pl.pallas_call(body, grid=(1,), in_specs=[whole(a.shape) for a in operand...  32.7 us
    ppermute x28, waiting for transfers between devices, swap_section(): return lax.ppermute(v, 'section', [(0, 1), (1, 0)])  31.5 us
    pallas_call x4, Pallas kernels, weight_grads(): pl.pallas_call(body, grid=(dp,), in_specs=specs, out_specs=[pl.BlockSpec(...  31 us
    unnamed x260, local copies, waits for them, and re-layouts  26.3 us
  transfers between devices with their start and end apart: 105, of which 53 were waited for; matrix products, arithmetic and copies ran while one was open for 9% of the time, Pallas kernels for 26%

profile of v3, /device:TPU:0, one launch (start us, length us, event | category | flops | bytes accessed | tf_op | source)
XLA Modules:
  0.0 516.7 jit_solution(4521749685144684877)
XLA Ops:
  29.6 9.8 %collective-permute-done.6.refs_2_ = bf16[144,1024]{1,0:T(8,128)(2,1)} collective-permute-done((bf16[144,1024]{1,0:T(8,128)(2,1)}, bf16[144,1024]{1,0:T(8,128)(2,1)}, u32[]{:S(2)}, u32[]{:S(2)}) %collective-permute-start.6) | collective-permute-done | bytes 294944 | tf_op jit(solution)/shard_map/ppermute | solution.py:165
  61.9 4.5 collective-permute-done.11.a_ref.refs_2_
  76.5 7.7 %attention.2 = (bf16[512,256]{1,0:T(8,128)(2,1)}, bf16[512,256]{1,0:T(8,128)(2,1)}, f32[4,1024]{1,0:T(4,128)S(1)}, bf16[256,1024]{1,0:T(8,128)(2,1)S(1)}, bf16[2...) custom-call(bf16[512,768]{1,0:T(8,128)(2,1)S(1)} %project_qkv.4.refs_0_, bf16[512,768]{1,0:T(8,128)(2,1)S(1)} %project_qkv.5.refs_1_, ...), custom_call_target="tpu_custom_call" | custom-call | flops 10350000128 | tf_op jit(solution)/shard_map/attention/pallas_call | solution.py:522
  94.5 9.4 %collective-permute-done.18.refs_2_ = bf16[256,1024]{1,0:T(8,128)(2,1)S(1)} collective-permute-done((bf16[256,1024]{1,0:T(8,128)(2,1)S(1)}, bf16[256,1024]{1,0:T(8,128)(2,1)S(1)}, u32[]{:S(2)}, u32[]{:S(2)}) %collective-permute-start.18) | collective-permute-done | bytes 524320 | tf_op jit(solution)/shard_map/ppermute | solution.py:66
  111.0 9.1 %collective-permute-done.24.refs_2_ = bf16[128,1024]{1,0:T(8,128)(2,1)S(1)} collective-permute-done((bf16[128,1024]{1,0:T(8,128)(2,1)S(1)}, bf16[128,1024]{1,0:T(8,128)(2,1)S(1)}, u32[]{:S(2)}, u32[]{:S(2)}) %collective-permute-start.24) | collective-permute-done | bytes 262176 | tf_op jit(solution)/shard_map/ppermute | solution.py:184
  123.8 6.6 %mlp_forward.2 = (bf16[512,1024]{1,0:T(8,128)(2,1)}, bf16[512,1024]{1,0:T(8,128)(2,1)}, f32[1,1024]{1,0:T(1,128)}, bf16[256,1024]{1,0:T(8,128)(2,1)S(1)}, bf16[256,1024]{1,0:T(8,128)(2,1)S(1)}) custom-call(bf16[256,1024]{1,0:T(8,128)(2,1)S(1)} %get-tuple-element.192.a.refs_0_, bf16[256,1024]{1,0:T(8,128)(2,1)S(1)} %collective-permute-done.21.b.refs_1_, ...), custom_call_target="tpu_custom_call" | custom-call | flops 575000000 | tf_op jit(solution)/shard_map/mlp_forward/pallas_call | solution.py:726
  132.4 6.6 %mlp_forward.3 = (bf16[512,1024]{1,0:T(8,128)(2,1)}, bf16[512,1024]{1,0:T(8,128)(2,1)}, f32[1,1024]{1,0:T(1,128)}, bf16[256,1024]{1,0:T(8,128)(2,1)S(1)}, bf16[256,1024]{1,0:T(8,128)(2,1)S(1)}) custom-call(bf16[256,1024]{1,0:T(8,128)(2,1)S(1)} %collective-permute-done.23.a.refs_2_, bf16[256,1024]{1,0:T(8,128)(2,1)S(1)} %collective-permute-done.26.b.refs_3_, ...), custom_call_target="tpu_custom_call" | custom-call | flops 575000000 | tf_op jit(solution)/shard_map/mlp_forward/pallas_call | solution.py:726
  146.7 7.1 %collective-permute-done.33.refs_5_ = bf16[128,1024]{1,0:T(8,128)(2,1)S(1)} collective-permute-done((bf16[128,1024]{1,0:T(8,128)(2,1)S(1)}, bf16[128,1024]{1,0:T(8,128)(2,1)S(1)}, u32[]{:S(2)}, u32[]{:S(2)}) %collective-permute-start.33) | collective-permute-done | bytes 262176 | tf_op jit(solution)/shard_map/ppermute | solution.py:118
  153.8 5.2 %collective-permute-done.34.refs_7_ = bf16[128,1024]{1,0:T(8,128)(2,1)S(1)} collective-permute-done((bf16[128,1024]{1,0:T(8,128)(2,1)S(1)}, bf16[128,1024]{1,0:T(8,128)(2,1)S(1)}, u32[]{:S(2)}, u32[]{:S(2)}) %collective-permute-start.34) | collective-permute-done | bytes 262176 | tf_op jit(solution)/shard_map/ppermute | solution.py:118
  170.9 6.3 %collective-permute-done.36.a_ref.refs_2_ = bf16[256,1024]{1,0:T(8,128)(2,1)} collective-permute-done((bf16[256,1024]{1,0:T(8,128)(2,1)}, bf16[256,1024]{1,0:T(8,128)(2,1)}, u32[]{:S(2)}, u32[]{:S(2)}) %collective-permute-start.36) | collective-permute-done | bytes 524320 | tf_op jit(solution)/shard_map/ppermute | solution.py:66
  184.7 7.7 %attention.3 = (bf16[512,256]{1,0:T(8,128)(2,1)}, bf16[512,256]{1,0:T(8,128)(2,1)}, f32[4,1024]{1,0:T(4,128)S(1)}, bf16[256,1024]{1,0:T(8,128)(2,1)S(1)}, bf16[2...) custom-call(bf16[512,768]{1,0:T(8,128)(2,1)S(1)} %project_qkv.6.refs_0_, bf16[512,768]{1,0:T(8,128)(2,1)S(1)} %project_qkv.7.refs_1_, ...), custom_call_target="tpu_custom_call" | custom-call | flops 10350000128 | tf_op jit(solution)/shard_map/attention/pallas_call | solution.py:522
  201.0 12.4 %collective-permute-done.44.refs_2_ = bf16[256,1024]{1,0:T(8,128)(2,1)S(1)} collective-permute-done((bf16[256,1024]{1,0:T(8,128)(2,1)S(1)}, bf16[256,1024]{1,0:T(8,128)(2,1)S(1)}, u32[]{:S(2)}, u32[]{:S(2)}) %collective-permute-start.44) | collective-permute-done | bytes 524320 | tf_op jit(solution)/shard_map/ppermute | solution.py:66
  219.1 8.9 %mlp_both.2 = (bf16[512,1024]{1,0:T(8,128)(2,1)}, bf16[512,1024]{1,0:T(8,128)(2,1)}, f32[1,1024]{1,0:T(1,128)S(1)}, bf16[256,1024]{1,0:T(8,128)(2,1)S(1)}, bf16[...) custom-call(bf16[256,1024]{1,0:T(8,128)(2,1)S(1)} %get-tuple-element.225.a.refs_0_, ...), custom_call_target="tpu_custom_call" | custom-call | flops 575000000 | tf_op jit(solution)/shard_map/mlp_both/pallas_call | solution.py:726
  232.3 9.0 %mlp_both.3 = (bf16[512,1024]{1,0:T(8,128)(2,1)}, bf16[512,1024]{1,0:T(8,128)(2,1)}, f32[1,1024]{1,0:T(1,128)S(1)}, bf16[256,1024]{1,0:T(8,128)(2,1)S(1)}, bf16[...) custom-call(bf16[256,1024]{1,0:T(8,128)(2,1)S(1)} %collective-permute-done.49.a.refs_2_, ...), custom_call_target="tpu_custom_call" | custom-call | flops 575000000 | tf_op jit(solution)/shard_map/mlp_both/pallas_call | solution.py:726
  248.7 9.3 %grad_ff.2 = (bf16[512,2048]{1,0:T(8,128)(2,1)}, bf16[512,2048]{1,0:T(8,128)(2,1)}) custom-call(s32[1]{0:T(128)} %bitcast.15.side_ref, bf16[256,1024]{1,0:T(8,128)(2,1)S(1)} %get-tuple-element.225.a.refs_0_, bf16[256,1024]{1,0:T(8,128)(2,1)S(1)} %collective-permute-done.48.b.refs_1_, bf16[256,1024]{1,0:T(8,128)(2,1)S(1)} %collective-permute-done.49.a.refs_2_, ...), custom_call_target="tpu_custom_call" | custom-call | flops 5750000128 | tf_op jit(solution)/shard_map/grad_ff/pallas_call | solution.py:884
  264.9 9.6 %collective-permute-done.56 = bf16[128,2048]{1,0:T(8,128)(2,1)S(1)} collective-permute-done((bf16[128,2048]{1,0:T(8,128)(2,1)S(1)}, bf16[128,2048]{1,0:T(8,128)(2,1)S(1)}, u32[]{:S(2)}, u32[]{:S(2)}) %collective-permute-start.56) | collective-permute-done | bytes 524320 | tf_op jit(solution)/shard_map/ppermute | solution.py:118
  279.4 16.3 %attention_back.2 = (bf16[512,768]{1,0:T(8,128)(2,1)}, bf16[512,768]{1,0:T(8,128)(2,1)}, bf16[256,1024]{1,0:T(8,128)(2,1)}, bf16[256,1024]{1,0:T(8,128)(2,1)}, b...) custom-call(bf16[512,768]{1,0:T(8,128)(2,1)} %copy-done.8, bf16[512,768]{1,0:T(8,128)(2,1)} %copy-done.9, ...), custom_call_target="tpu_custom_call" | custom-call | flops 17250000896 | tf_op jit(solution)/shard_map/attention_back/pallas_call | solution.py:664
  304.1 6.3 %grad_att.2 = bf16[1024,1024]{1,0:T(8,128)(2,1)} custom-call(s32[1]{0:T(128)} %bitcast.15.side_ref, bf16[256,1024]{1,0:T(8,128)(2,1)} %get-tuple-element.210.a_ref.refs_0_, bf16[256,1024]{1,0:T(8,128)(2,1)} %copy-done.20, bf16[256,1024]{1,0:T(8,128)(2,1)} %collective-permute-done.36.a_ref.refs_2_, bf16[256,1024]{1,0:T(8,128)(2,1)} %copy-done.22, ...), custom_call_target="tpu_custom_call" | custom-call | flops 5750000128 | tf_op jit(solution)/shard_map/grad_att/pallas_call | solution.py:884
  310.4 4.2 collective-permute-done.64.refs_3_
  325.7 5.6 %mlp_backward.2 = (bf16[512,1024]{1,0:T(8,128)(2,1)}, f32[1,1024]{1,0:T(1,128)S(1)}, bf16[256,1024]{1,0:T(8,128)(2,1)S(1)}, bf16[256,1024]{1,0:T(8,128)(2,1)S(1)}) custom-call(bf16[256,1024]{1,0:T(8,128)(2,1)S(1)} %get-tuple-element.267.a.refs_6_, bf16[256,1024]{1,0:T(8,128)(2,1)S(1)} %collective-permute-done.68.b.refs_7_, ...), custom_call_target="tpu_custom_call" | custom-call | flops 575000000 | tf_op jit(solution)/shard_map/mlp_backward/pallas_call | solution.py:726
  339.2 5.7 %mlp_backward.3 = (bf16[512,1024]{1,0:T(8,128)(2,1)}, f32[1,1024]{1,0:T(1,128)S(1)}, bf16[256,1024]{1,0:T(8,128)(2,1)S(1)}, bf16[256,1024]{1,0:T(8,128)(2,1)}) custom-call(bf16[256,1024]{1,0:T(8,128)(2,1)S(1)} %collective-permute-done.69.a.refs_8_, bf16[256,1024]{1,0:T(8,128)(2,1)S(1)} %collective-permute-done.72.b.refs_9_, ...), custom_call_target="tpu_custom_call" | custom-call | flops 575000000 | tf_op jit(solution)/shard_map/mlp_backward/pallas_call | solution.py:726
  354.3 9.2 %grad_ff.3 = (bf16[512,2048]{1,0:T(8,128)(2,1)}, bf16[512,2048]{1,0:T(8,128)(2,1)}) custom-call(s32[1]{0:T(128)} %bitcast.15.side_ref, bf16[256,1024]{1,0:T(8,128)(2,1)} %copy-done.16, bf16[256,1024]{1,0:T(8,128)(2,1)} %copy-done.17, bf16[256,1024]{1,0:T(8,128)(2,1)} %copy-done.18, bf16[256,1024]{1,0:T(8,128)(2,1)} %copy-done.19, ...), custom_call_target="tpu_custom_call" | custom-call | flops 5750000128 | tf_op jit(solution)/shard_map/grad_ff/pallas_call | solution.py:884
  375.7 8.4 %collective-permute-done.79.refs_7_.refs_8_ = bf16[256,1024]{1,0:T(8,128)(2,1)S(1)} collective-permute-done((bf16[256,1024]{1,0:T(8,128)(2,1)S(1)}, bf16[256,1024]{1,0:T(8,128)(2,1)S(1)}, u32[]{:S(2)}, u32[]{:S(2)}) %collective-permute-start.79) | collective-permute-done | bytes 524320 | tf_op jit(solution)/shard_map/ppermute | solution.py:66
  384.2 4.8 collective-permute-done.80
  395.2 16.4 %attention_back.3 = (bf16[512,768]{1,0:T(8,128)(2,1)}, bf16[512,768]{1,0:T(8,128)(2,1)}, bf16[256,1024]{1,0:T(8,128)(2,1)}, bf16[256,1024]{1,0:T(8,128)(2,1)}, b...) custom-call(bf16[512,768]{1,0:T(8,128)(2,1)} %copy-done.6, bf16[512,768]{1,0:T(8,128)(2,1)} %copy-done.7, ...), custom_call_target="tpu_custom_call" | custom-call | flops 17250000896 | tf_op jit(solution)/shard_map/attention_back/pallas_call | solution.py:664
  411.6 6.0 %collective-permute-done.84 = bf16[128,2048]{1,0:T(8,128)(2,1)S(1)} collective-permute-done((bf16[128,2048]{1,0:T(8,128)(2,1)S(1)}, bf16[128,2048]{1,0:T(8,128)(2,1)S(1)}, u32[]{:S(2)}, u32[]{:S(2)}) %collective-permute-start.84) | collective-permute-done | bytes 524320 | tf_op jit(solution)/shard_map/ppermute | solution.py:229
  425.1 6.3 %grad_att.3 = bf16[1024,1024]{1,0:T(8,128)(2,1)} custom-call(s32[1]{0:T(128)} %bitcast.15.side_ref, bf16[256,1024]{1,0:T(8,128)(2,1)} %copy-done.12, bf16[256,1024]{1,0:T(8,128)(2,1)} %copy-done.13, bf16[256,1024]{1,0:T(8,128)(2,1)} %collective-permute-done.11.a_ref.refs_2_, bf16[256,1024]{1,0:T(8,128)(2,1)} %copy-done.15, ...), custom_call_target="tpu_custom_call" | custom-call | flops 5750000128 | tf_op jit(solution)/shard_map/grad_att/pallas_call | solution.py:884
  442.9 5.8 %collective-permute-done.91 = bf16[256,1024]{1,0:T(8,128)(2,1)} collective-permute-done((bf16[256,1024]{1,0:T(8,128)(2,1)S(1)}, bf16[256,1024]{1,0:T(8,128)(2,1)}, u32[]{:S(2)}, u32[]{:S(2)}) %collective-permute-start.91) | collective-permute-done | bytes 524320 | tf_op jit(solution)/shard_map/ppermute | solution.py:229
  458.1 7.3 %collective-permute-done.92 = bf16[256,1024]{1,0:T(8,128)(2,1)} collective-permute-done((bf16[256,1024]{1,0:T(8,128)(2,1)S(1)}, bf16[256,1024]{1,0:T(8,128)(2,1)}, u32[]{:S(2)}, u32[]{:S(2)}) %collective-permute-start.92) | collective-permute-done | bytes 524320 | tf_op jit(solution)/shard_map/ppermute | solution.py:229
  473.1 10.4 %collective-permute-done.93 = bf16[256,1024]{1,0:T(8,128)(2,1)S(1)} collective-permute-done((bf16[256,1024]{1,0:T(8,128)(2,1)S(1)}, bf16[256,1024]{1,0:T(8,128)(2,1)S(1)}, u32[]{:S(2)}, u32[]{:S(2)}) %collective-permute-start.93) | collective-permute-done | bytes 524320 | tf_op jit(solution)/shard_map/ppermute | solution.py:229
  488.5 4.1 collective-permute-done.99
  504.4 4.9 collective-permute-done.104
  (583 shorter events, 262.9 us)
Async XLA Ops:
  20.2 24.3 %collective-permute-start.4 = (bf16[144,1024]{1,0:T(8,128)(2,1)}, bf16[144,1024]{1,0:T(8,128)(2,1)}, u32[]{:S(2)}, u32[]{:S(2)}) collective-permute-start(bf16[144,1024]{1,0:T(8,128)(2,1)} %pad_maximum_fusion.1.refs_0_), channel_id=1, source_target_pairs={{0,8},{4,12},{8,0},{12,4},{1,9},{5,13},{9,1},{13,5},{2,10},{6,14},... | collective-permute-start | bytes 884744 | tf_op jit(solution)/shard_map/ppermute | solution.py:165
  20.3 19.1 %collective-permute-start.6 = (bf16[144,1024]{1,0:T(8,128)(2,1)}, bf16[144,1024]{1,0:T(8,128)(2,1)}, u32[]{:S(2)}, u32[]{:S(2)}) collective-permute-start(bf16[144,1024]{1,0:T(8,128)(2,1)} %pad_maximum_fusion.1.refs_0_), channel_id=1, source_target_pairs={{0,4},{4,8},{8,12},{12,0},{1,5},{5,9},{9,13},{13,1},{2,6},{6,10},{... | collective-permute-start | bytes 884744 | tf_op jit(solution)/shard_map/ppermute | solution.py:165
  21.3 24.8 %collective-permute-start.2 = (bf16[128,2048]{1,0:T(8,128)(2,1)S(1)}, bf16[128,2048]{1,0:T(8,128)(2,1)S(1)}, u32[]{:S(2)}, u32[]{:S(2)}) collective-permute-start(bf16[128,2048]{1,0:T(8,128)(2,1)S(1)} %fusion.9), channel_id=1, source_target_pairs={{0,16},{16,0},{1,17},{17,1},{2,18},{18,2},{3,19},{19,3},{4,20},{20... | collective-permute-start | bytes 1572872 | tf_op jit(solution)/shard_map/ppermute | solution.py:118
  28.1 19.8 %collective-permute-start.5 = (bf16[144,1024]{1,0:T(8,128)(2,1)S(1)}, bf16[144,1024]{1,0:T(8,128)(2,1)S(1)}, u32[]{:S(2)}, u32[]{:S(2)}) collective-permute-start(bf16[144,1024]{1,0:T(8,128)(2,1)S(1)} %collective-permute-done.3.refs_6_), channel_id=1, source_target_pairs={{0,16},{16,0},{1,17},{17,1},{2,18},{18,2},{3,19},{19,3},{4,20},{20... | collective-permute-start | bytes 884744 | tf_op jit(solution)/shard_map/ppermute | solution.py:118
  54.3 15.9 %collective-permute-start.13 = (bf16[128,2048]{1,0:T(8,128)(2,1)}, bf16[128,2048]{1,0:T(8,128)(2,1)}, u32[]{:S(2)}, u32[]{:S(2)}) collective-permute-start(bf16[128,2048]{1,0:T(8,128)(2,1)} %broadcast_select_fusion.3.refs_0_), channel_id=1, source_target_pairs={{0,4},{4,8},{8,12},{12,0},{1,5},{5,9},{9,13},{13,1},{2,6},{6,10},{... | collective-permute-start | bytes 1572872 | tf_op jit(solution)/shard_map/ppermute | solution.py:184
  70.2 16.8 %collective-permute-start.15 = (bf16[128,2048]{1,0:T(8,128)(2,1)}, bf16[128,2048]{1,0:T(8,128)(2,1)S(1)}, u32[]{:S(2)}, u32[]{:S(2)}) collective-permute-start(bf16[128,2048]{1,0:T(8,128)(2,1)} %collective-permute-done.13.refs_2_), channel_id=1, source_target_pairs={{0,4},{4,8},{8,12},{12,0},{1,5},{5,9},{9,13},{13,1},{2,6},{6,10},{... | collective-permute-start | bytes 1572872 | tf_op jit(solution)/shard_map/ppermute | solution.py:184
  108.9 21.5 %collective-permute-start.23 = (bf16[256,1024]{1,0:T(8,128)(2,1)S(1)}, bf16[256,1024]{1,0:T(8,128)(2,1)S(1)}, u32[]{:S(2)}, u32[]{:S(2)}) collective-permute-start(bf16[256,1024]{1,0:T(8,128)(2,1)S(1)} %get-tuple-element.192.a.refs_0_), channel_id=1, source_target_pairs={{2,0},{3,1},{0,2},{1,3},{6,4},{7,5},{4,6},{5,7},{10,8},{11,9},{8,1... | collective-permute-start | bytes 1572872 | tf_op jit(solution)/shard_map/ppermute | solution.py:66
  144.6 16.2 %collective-permute-start.32 = (bf16[128,2048]{1,0:T(8,128)(2,1)S(1)}, bf16[128,2048]{1,0:T(8,128)(2,1)}, u32[]{:S(2)}, u32[]{:S(2)}) collective-permute-start(bf16[128,2048]{1,0:T(8,128)(2,1)S(1)} %copy-done.74), channel_id=1, source_target_pairs={{0,4},{4,8},{8,12},{12,0},{1,5},{5,9},{9,13},{13,1},{2,6},{6,10},{... | collective-permute-start | bytes 1572872 | tf_op jit(solution)/shard_map/ppermute | solution.py:184
  163.6 16.1 %collective-permute-start.37 = (bf16[128,2048]{1,0:T(8,128)(2,1)}, bf16[128,2048]{1,0:T(8,128)(2,1)}, u32[]{:S(2)}, u32[]{:S(2)}) collective-permute-start(bf16[128,2048]{1,0:T(8,128)(2,1)} %collective-permute-done.32.refs_2_), channel_id=1, source_target_pairs={{0,4},{4,8},{8,12},{12,0},{1,5},{5,9},{9,13},{13,1},{2,6},{6,10},{... | collective-permute-start | bytes 1572872 | tf_op jit(solution)/shard_map/ppermute | solution.py:184
  180.0 16.4 %collective-permute-start.41 = (bf16[128,2048]{1,0:T(8,128)(2,1)}, bf16[128,2048]{1,0:T(8,128)(2,1)S(1)}, u32[]{:S(2)}, u32[]{:S(2)}) collective-permute-start(bf16[128,2048]{1,0:T(8,128)(2,1)} %collective-permute-done.37.refs_4_), channel_id=1, source_target_pairs={{0,4},{4,8},{8,12},{12,0},{1,5},{5,9},{9,13},{13,1},{2,6},{6,10},{... | collective-permute-start | bytes 1572872 | tf_op jit(solution)/shard_map/ppermute | solution.py:184
  180.1 16.3 %collective-permute-start.42 = (bf16[128,2048]{1,0:T(8,128)(2,1)}, bf16[128,2048]{1,0:T(8,128)(2,1)S(1)}, u32[]{:S(2)}, u32[]{:S(2)}) collective-permute-start(bf16[128,2048]{1,0:T(8,128)(2,1)} %collective-permute-done.37.refs_4_), channel_id=1, source_target_pairs={{0,16},{16,0},{1,17},{17,1},{2,18},{18,2},{3,19},{19,3},{4,20},{20... | collective-permute-start | bytes 1572872 | tf_op jit(solution)/shard_map/ppermute | solution.py:118
  263.6 32.1 %collective-permute-start.58 = (bf16[256,1024]{1,0:T(8,128)(2,1)S(1)}, bf16[256,1024]{1,0:T(8,128)(2,1)S(1)}, u32[]{:S(2)}, u32[]{:S(2)}) collective-permute-start(bf16[256,1024]{1,0:T(8,128)(2,1)S(1)} %get-tuple-element.252.refs_0_.refs_1_), channel_id=1, source_target_pairs={{16,0},{17,1},{18,2},{19,3},{20,4},{21,5},{22,6},{23,7},{24,8},{25... | collective-permute-start | bytes 1572872 | tf_op jit(solution)/shard_map/ppermute | solution.py:1050
  276.1 19.7 %collective-permute-start.61 = (bf16[128,2048]{1,0:T(8,128)(2,1)S(1)}, bf16[128,2048]{1,0:T(8,128)(2,1)S(1)}, u32[]{:S(2)}, u32[]{:S(2)}) collective-permute-start(bf16[128,2048]{1,0:T(8,128)(2,1)S(1)} %add_convert_fusion.12), channel_id=1, source_target_pairs={{0,4},{4,8},{8,12},{12,0},{1,5},{5,9},{9,13},{13,1},{2,6},{6,10},{... | collective-permute-start | bytes 1572872 | tf_op jit(solution)/shard_map/ppermute | solution.py:229
  276.5 20.1 %collective-permute-start.62 = (bf16[128,2048]{1,0:T(8,128)(2,1)S(1)}, bf16[128,2048]{1,0:T(8,128)(2,1)S(1)}, u32[]{:S(2)}, u32[]{:S(2)}) collective-permute-start(bf16[128,2048]{1,0:T(8,128)(2,1)S(1)} %get-tuple-element.258), channel_id=1, source_target_pairs={{0,16},{16,0},{1,17},{17,1},{2,18},{18,2},{3,19},{19,3},{4,20},{20... | collective-permute-start | bytes 1572872 | tf_op jit(solution)/shard_map/ppermute | solution.py:118
  278.3 18.3 %collective-permute-start.60 = (bf16[256,1024]{1,0:T(8,128)(2,1)S(1)}, bf16[256,1024]{1,0:T(8,128)(2,1)S(1)}, u32[]{:S(2)}, u32[]{:S(2)}) collective-permute-start(bf16[256,1024]{1,0:T(8,128)(2,1)S(1)} %add_convert_fusion.13), channel_id=1, source_target_pairs={{2,0},{3,1},{0,2},{1,3},{6,4},{7,5},{4,6},{5,7},{10,8},{11,9},{8,1... | collective-permute-start | bytes 1572872 | tf_op jit(solution)/shard_map/ppermute | solution.py:66
  296.7 26.9 %collective-permute-start.67 = (bf16[256,1024]{1,0:T(8,128)(2,1)S(1)}, bf16[256,1024]{1,0:T(8,128)(2,1)S(1)}, u32[]{:S(2)}, u32[]{:S(2)}) collective-permute-start(bf16[256,1024]{1,0:T(8,128)(2,1)S(1)} %copy-done.35), channel_id=1, source_target_pairs={{0,1},{1,0},{2,3},{3,2},{4,5},{5,4},{6,7},{7,6},{8,9},{9,8},{10,11... | collective-permute-start | bytes 1572872 | tf_op jit(solution)/shard_map/ppermute | solution.py:59
  321.4 15.8 %collective-permute-start.70 = (bf16[128,2048]{1,0:T(8,128)(2,1)S(1)}, bf16[128,2048]{1,0:T(8,128)(2,1)S(1)}, u32[]{:S(2)}, u32[]{:S(2)}) collective-permute-start(bf16[128,2048]{1,0:T(8,128)(2,1)S(1)} %add_convert_fusion.9), channel_id=1, source_target_pairs={{0,4},{4,8},{8,12},{12,0},{1,5},{5,9},{9,13},{13,1},{2,6},{6,10},{... | collective-permute-start | bytes 1572872 | tf_op jit(solution)/shard_map/ppermute | solution.py:229
  347.1 19.3 %collective-permute-start.77 = (bf16[256,1024]{1,0:T(8,128)(2,1)S(1)}, bf16[256,1024]{1,0:T(8,128)(2,1)S(1)}, u32[]{:S(2)}, u32[]{:S(2)}) collective-permute-start(bf16[256,1024]{1,0:T(8,128)(2,1)S(1)} %constant_dynamic-slice_fusion.9), channel_id=1, source_target_pairs={{0,4},{4,8},{8,12},{12,0},{1,5},{5,9},{9,13},{13,1},{2,6},{6,10},{... | collective-permute-start | bytes 1572872 | tf_op jit(solution)/shard_map/ppermute | solution.py:229
  349.4 17.0 %collective-permute-start.74 = (bf16[256,1024]{1,0:T(8,128)(2,1)S(1)}, bf16[256,1024]{1,0:T(8,128)(2,1)S(1)}, u32[]{:S(2)}, u32[]{:S(2)}) collective-permute-start(bf16[256,1024]{1,0:T(8,128)(2,1)S(1)} %add_convert_fusion.8), channel_id=1, source_target_pairs={{2,0},{3,1},{0,2},{1,3},{6,4},{7,5},{4,6},{5,7},{10,8},{11,9},{8,1... | collective-permute-start | bytes 1572872 | tf_op jit(solution)/shard_map/ppermute | solution.py:66
  350.5 16.0 %collective-permute-start.75 = (bf16[256,1024]{1,0:T(8,128)(2,1)S(1)}, bf16[256,1024]{1,0:T(8,128)(2,1)S(1)}, u32[]{:S(2)}, u32[]{:S(2)}) collective-permute-start(bf16[256,1024]{1,0:T(8,128)(2,1)S(1)} %copy-done.48), channel_id=1, source_target_pairs={{0,1},{1,0},{2,3},{3,2},{4,5},{5,4},{6,7},{7,6},{8,9},{9,8},{10,11... | collective-permute-start | bytes 1572872 | tf_op jit(solution)/shard_map/ppermute | solution.py:59
  375.7 19.4 %collective-permute-start.78 = (bf16[256,1024]{1,0:T(8,128)(2,1)S(1)}, bf16[256,1024]{1,0:T(8,128)(2,1)S(1)}, u32[]{:S(2)}, u32[]{:S(2)}) collective-permute-start(bf16[256,1024]{1,0:T(8,128)(2,1)S(1)} %get-tuple-element.297.refs_5_.refs_6_), channel_id=1, source_target_pairs={{0,1},{1,0},{2,3},{3,2},{4,5},{5,4},{6,7},{7,6},{8,9},{9,8},{10,11... | collective-permute-start | bytes 1572872 | tf_op jit(solution)/shard_map/ppermute | solution.py:59
  375.7 35.9 %collective-permute-start.85 = (bf16[128,2048]{1,0:T(8,128)(2,1)}, bf16[128,2048]{1,0:T(8,128)(2,1)S(1)}, u32[]{:S(2)}, u32[]{:S(2)}) collective-permute-start(bf16[128,2048]{1,0:T(8,128)(2,1)} %get-tuple-element.306), channel_id=1, source_target_pairs={{0,16},{16,0},{1,17},{17,1},{2,18},{18,2},{3,19},{19,3},{4,20},{20... | collective-permute-start | bytes 1572872 | tf_op jit(solution)/shard_map/ppermute | solution.py:118
  390.2 21.4 %collective-permute-start.83 = (bf16[256,1024]{1,0:T(8,128)(2,1)S(1)}, bf16[256,1024]{1,0:T(8,128)(2,1)S(1)}, u32[]{:S(2)}, u32[]{:S(2)}) collective-permute-start(bf16[256,1024]{1,0:T(8,128)(2,1)S(1)} %add_convert_fusion.6), channel_id=1, source_target_pairs={{0,4},{4,8},{8,12},{12,0},{1,5},{5,9},{9,13},{13,1},{2,6},{6,10},{... | collective-permute-start | bytes 1572872 | tf_op jit(solution)/shard_map/ppermute | solution.py:229
  392.7 24.9 %collective-permute-start.84 = (bf16[128,2048]{1,0:T(8,128)(2,1)S(1)}, bf16[128,2048]{1,0:T(8,128)(2,1)S(1)}, u32[]{:S(2)}, u32[]{:S(2)}) collective-permute-start(bf16[128,2048]{1,0:T(8,128)(2,1)S(1)} %add_convert_fusion.5), channel_id=1, source_target_pairs={{0,4},{4,8},{8,12},{12,0},{1,5},{5,9},{9,13},{13,1},{2,6},{6,10},{... | collective-permute-start | bytes 1572872 | tf_op jit(solution)/shard_map/ppermute | solution.py:229
  421.0 16.8 %collective-permute-start.88 = (bf16[128,2048]{1,0:T(8,128)(2,1)}, bf16[128,2048]{1,0:T(8,128)(2,1)}, u32[]{:S(2)}, u32[]{:S(2)}) collective-permute-start(bf16[128,2048]{1,0:T(8,128)(2,1)} %add_convert_fusion.3), channel_id=1, source_target_pairs={{0,4},{4,8},{8,12},{12,0},{1,5},{5,9},{9,13},{13,1},{2,6},{6,10},{... | collective-permute-start | bytes 1572872 | tf_op jit(solution)/shard_map/ppermute | solution.py:229
  421.0 16.8 %collective-permute-start.89 = (bf16[128,2048]{1,0:T(8,128)(2,1)}, bf16[128,2048]{1,0:T(8,128)(2,1)}, u32[]{:S(2)}, u32[]{:S(2)}) collective-permute-start(bf16[128,2048]{1,0:T(8,128)(2,1)} %get-tuple-element.312), channel_id=1, source_target_pairs={{0,16},{16,0},{1,17},{17,1},{2,18},{18,2},{3,19},{19,3},{4,20},{20... | collective-permute-start | bytes 1572872 | tf_op jit(solution)/shard_map/ppermute | solution.py:118
  432.5 16.2 %collective-permute-start.91 = (bf16[256,1024]{1,0:T(8,128)(2,1)S(1)}, bf16[256,1024]{1,0:T(8,128)(2,1)}, u32[]{:S(2)}, u32[]{:S(2)}) collective-permute-start(bf16[256,1024]{1,0:T(8,128)(2,1)S(1)} %constant_dynamic-slice_fusion.5), channel_id=1, source_target_pairs={{0,4},{4,8},{8,12},{12,0},{1,5},{5,9},{9,13},{13,1},{2,6},{6,10},{... | collective-permute-start | bytes 1572872 | tf_op jit(solution)/shard_map/ppermute | solution.py:229
  441.4 47.0 %collective-permute-start.90 = (bf16[256,1024]{1,0:T(8,128)(2,1)}, bf16[256,1024]{1,0:T(8,128)(2,1)S(1)}, u32[]{:S(2)}, u32[]{:S(2)}) collective-permute-start(bf16[256,1024]{1,0:T(8,128)(2,1)} %broadcast_select_fusion.7), channel_id=1, source_target_pairs={{0,16},{16,0},{1,17},{17,1},{2,18},{18,2},{3,19},{19,3},{4,20},{20... | collective-permute-start | bytes 1572872 | tf_op jit(solution)/shard_map/ppermute | solution.py:118
  454.1 34.3 %collective-permute-start.98 = (bf16[256,1024]{1,0:T(8,128)(2,1)}, bf16[256,1024]{1,0:T(8,128)(2,1)S(1)}, u32[]{:S(2)}, u32[]{:S(2)}) collective-permute-start(bf16[256,1024]{1,0:T(8,128)(2,1)} %fusion.4), channel_id=1, source_target_pairs={{0,16},{1,17},{2,18},{3,19},{4,20},{5,21},{6,22},{7,23},{8,24},{9,... | collective-permute-start | bytes 1572872 | tf_op jit(solution)/shard_map/ppermute | solution.py:239
  466.8 16.7 %collective-permute-start.93 = (bf16[256,1024]{1,0:T(8,128)(2,1)S(1)}, bf16[256,1024]{1,0:T(8,128)(2,1)S(1)}, u32[]{:S(2)}, u32[]{:S(2)}) collective-permute-start(bf16[256,1024]{1,0:T(8,128)(2,1)S(1)} %add_convert_fusion.1), channel_id=1, source_target_pairs={{0,4},{4,8},{8,12},{12,0},{1,5},{5,9},{9,13},{13,1},{2,6},{6,10},{... | collective-permute-start | bytes 1572872 | tf_op jit(solution)/shard_map/ppermute | solution.py:229
  470.6 22.0 %collective-permute-start.99 = (bf16[128,2048]{1,0:T(8,128)(2,1)S(1)}, bf16[128,2048]{1,0:T(8,128)(2,1)S(1)}, u32[]{:S(2)}, u32[]{:S(2)}) collective-permute-start(bf16[128,2048]{1,0:T(8,128)(2,1)S(1)} %add_convert_fusion), channel_id=1, source_target_pairs={{0,4},{4,8},{8,12},{12,0},{1,5},{5,9},{9,13},{13,1},{2,6},{6,10},{... | collective-permute-start | bytes 1572872 | tf_op jit(solution)/shard_map/ppermute | solution.py:229
  471.1 21.5 %collective-permute-start.100 = (bf16[128,2048]{1,0:T(8,128)(2,1)S(1)}, bf16[128,2048]{1,0:T(8,128)(2,1)S(1)}, u32[]{:S(2)}, u32[]{:S(2)}) collective-permute-start(bf16[128,2048]{1,0:T(8,128)(2,1)S(1)} %copy-done.85), channel_id=1, source_target_pairs={{0,16},{16,0},{1,17},{17,1},{2,18},{18,2},{3,19},{19,3},{4,20},{20... | collective-permute-start | bytes 1572872 | tf_op jit(solution)/shard_map/ppermute | solution.py:118
  (188 other events, 1907.7 us)
